TPU v7x, 32 devices: a whole 2x2x4 slice. The times are simulated.
32 devices in a mesh: dom: 8 (over y, x, core), sub: 4 (over z).
Axes of the slice: x: 2, y: 2, z: 4, core: 2. Of those that a mesh axis runs over, the one named last changes fastest.
Arguments:
- solution: float32 [8, 8, 8, 16384], P(None, None, None, ('dom', 'sub')), may hold values from -6 to 6
- forcing: float32 [8, 8, 8, 16384], P(None, None, None, ('dom', 'sub')), may hold values from -600 to 600
- metric: float32 [7, 8, 8, 8, 16384], P(None, None, None, None, ('dom', 'sub')), may hold values from -2.5 to 100, as said below
- entity_ids: int32 [26, 16384], P(None, ('dom', 'sub')), may hold values from 0 to 49151, as said below
- new_owner: int32 [16384], P(('dom', 'sub')), may hold values from 0 to 31, as said below
Outputs:
- smoothed: float32 [8, 8, 8, 16384], P(None, None, None, ('dom', 'sub'))
- moved_metric: float32 [7, 8, 8, 8, 16384], P(None, None, None, None, ('dom', 'sub'))
Inputs may be any that keep to these rules, and one draw needn't show every extreme that they name: `new_owner`: an element stays on its device or goes to one of the device's four neighbours: the previous or next device along dom with the same sub index, or the previous or next along sub with the same dom index, indices wrapping around. Two neighbouring devices hand each other equally many elements, at most 64; in every draw some pair of neighbours along dom and some pair along sub hand each other exactly 64. `entity_ids`: face and edge ids come in blocks of 1536 consecutive ids, corner ids in blocks of 512; block b is summed by device b. Every face id is carried by exactly 2 element faces, every edge id by exactly 4 element edges, every corner id by exactly 8 element corners, their shared nodes lining up in the listed order. An id carried by a device's elements lies in the device's own block or in that of the next device along dom, along sub, or along both (indices wrapping around); every device's elements carry exactly 128 faces, 480 edges and 448 corners of the next block along dom, exactly 128 faces, 480 edges and 448 corners of the next block along sub, and exactly 32 edges, 64 corners and no face of the next block along both. metric[0], metric[1], metric[2] and metric[6] are positive; at every node |metric[3]| <= 0.5 sqrt(metric[0] metric[1]), |metric[4]| <= 0.5 sqrt(metric[0] metric[2]), |metric[5]| <= 0.5 sqrt(metric[1] metric[2]).
All inputs are finite; a program needn't handle non-finite values.
Results may differ from a plain program's by a relative error of at most 0.00005.
Values sent between devices are 32-bit elements; how exact they have to be, the bound alone decides.
No kernel may reach another device: no remote copies, remote signals or barrier semaphores. Data moves between devices by JAX's collectives and lax.ppermute only.
A program may use at most 128 MiB of HBM per device.

v0:
```python
import jax
import jax.numpy as jnp
import numpy as np
from jax import lax
from jax.sharding import PartitionSpec as P

EX = 4
EY = 4
EZ = 32
MOVE = 64


RELAX = 0.6


def padded(shard, sides, width):
    for axis, dim in sides:
        size, length = (lax.axis_size(axis), shard.shape[dim])
        up = [(i, (i + 1) % size) for i in range(size)]
        down = [(j, i) for i, j in up]
        last = lax.slice_in_dim(shard, length - width, length, axis=dim)
        leading = lax.slice_in_dim(shard, 0, width, axis=dim)
        before = lax.ppermute(last, axis, up)
        after = lax.ppermute(leading, axis, down)
        shard = jnp.concatenate([before, shard, after], axis=dim)
    return shard


def from_behind(value, axis, steps):
    count = lax.axis_size(axis)
    pairs = [(source, (source + steps) % count) for source in range(count)]
    return lax.ppermute(value, axis, pairs)


def derivative_table(order):
    count = order + 1
    points = -np.cos(np.pi * np.arange(count) / order)
    legendre = np.zeros((count, count))
    for sweep in range(80):
        legendre[:, 0] = 1.0
        legendre[:, 1] = points
        for degree in range(2, count):
            legendre[:, degree] = (
                (2 * degree - 1) * points * legendre[:, degree - 1]
                - (degree - 1) * legendre[:, degree - 2]
            ) / degree
        points = points - (points * legendre[:, order] - legendre[:, order - 1]) / (
            count * legendre[:, order]
        )
    legendre[:, 0] = 1.0
    legendre[:, 1] = points
    for degree in range(2, count):
        legendre[:, degree] = (
            (2 * degree - 1) * points * legendre[:, degree - 1]
            - (degree - 1) * legendre[:, degree - 2]
        ) / degree
    values = legendre[:, order]
    identity = np.eye(count)
    spread = points[:, None] - points[None, :] + identity
    table = values[:, None] / values[None, :] / spread
    table = table * (1.0 - identity)
    table[0, 0] = -order * count / 4.0
    table[order, order] = order * count / 4.0
    return jnp.asarray(table, dtype=jnp.float32)


def element_apply(solution, metric, derivative):
    highest = lax.Precision.HIGHEST
    grad_r = jnp.einsum("ai,ijke->ajke", derivative, solution, precision=highest)
    grad_s = jnp.einsum("bj,ijke->ibke", derivative, solution, precision=highest)
    grad_t = jnp.einsum("ck,ijke->ijce", derivative, solution, precision=highest)
    flux_r = metric[0] * grad_r + metric[3] * grad_s + metric[4] * grad_t
    flux_s = metric[3] * grad_r + metric[1] * grad_s + metric[5] * grad_t
    flux_t = metric[4] * grad_r + metric[5] * grad_s + metric[2] * grad_t
    image = jnp.einsum("ai,ajke->ijke", derivative, flux_r, precision=highest)
    image = image + jnp.einsum("bj,ibke->ijke", derivative, flux_s, precision=highest)
    image = image + jnp.einsum("ck,ijce->ijke", derivative, flux_t, precision=highest)
    image = image + metric[6] * solution
    squared = derivative * derivative
    diagonal = jnp.einsum("ai,ajke->ijke", squared, metric[0], precision=highest)
    diagonal = diagonal + jnp.einsum("bj,ibke->ijke", squared, metric[1], precision=highest)
    diagonal = diagonal + jnp.einsum("ck,ijce->ijke", squared, metric[2], precision=highest)
    along = jnp.diagonal(derivative)
    along_i = along[:, None, None, None]
    along_j = along[None, :, None, None]
    along_k = along[None, None, :, None]
    diagonal = (
        diagonal
        + 2.0 * along_i * along_j * metric[3]
        + 2.0 * along_i * along_k * metric[4]
        + 2.0 * along_j * along_k * metric[5]
    )
    diagonal = diagonal + metric[6]
    return (image, diagonal)


def shared_slots(final_index):
    inside = slice(1, final_index)
    end_points = (0, final_index)
    face_slots = [
        (0, inside, inside),
        (final_index, inside, inside),
        (inside, 0, inside),
        (inside, final_index, inside),
        (inside, inside, 0),
        (inside, inside, final_index),
    ]
    edge_slots = [
        (inside, first_end, second_end) for first_end in end_points for second_end in end_points
    ]
    edge_slots = edge_slots + [
        (first_end, inside, second_end) for first_end in end_points for second_end in end_points
    ]
    edge_slots = edge_slots + [
        (first_end, second_end, inside) for first_end in end_points for second_end in end_points
    ]
    corner_slots = [
        (first_end, second_end, third_end)
        for first_end in end_points
        for second_end in end_points
        for third_end in end_points
    ]
    return (face_slots, edge_slots, corner_slots)


def shared_parts(element_cube):
    face_slots, edge_slots, corner_slots = shared_slots(element_cube.shape[0] - 1)
    face_part = jnp.stack([element_cube[slot_index] for slot_index in face_slots])
    edge_part = jnp.stack([element_cube[slot_index] for slot_index in edge_slots])
    corners = jnp.stack([element_cube[slot_index] for slot_index in corner_slots])
    return (face_part, edge_part, corners)


def place_shared(element_cube, face_part, edge_part, corners):
    face_slots, edge_slots, corner_slots = shared_slots(element_cube.shape[0] - 1)
    for number, slot_index in enumerate(face_slots):
        element_cube = element_cube.at[slot_index].set(face_part[number])
    for number, slot_index in enumerate(edge_slots):
        element_cube = element_cube.at[slot_index].set(edge_part[number])
    for number, slot_index in enumerate(corner_slots):
        element_cube = element_cube.at[slot_index].set(corners[number])
    return element_cube


def pack_values(part):
    kind_count = part.shape[0]
    elem_count = part.shape[-1]
    return jnp.moveaxis(part, 0, -2).reshape(-1, kind_count * elem_count)


def unpack_values(values, part_shape):
    kind_count = part_shape[0]
    return jnp.moveaxis(values.reshape(part_shape[1:-1] + (kind_count, part_shape[-1])), -2, 0)


def select_slots(chosen, capacity):
    ranked = jnp.cumsum(chosen.astype(jnp.int32)) - 1
    return jnp.where(chosen, ranked, capacity)


def pack_columns(values, slots, capacity):
    return jnp.zeros((values.shape[0], capacity), jnp.float32).at[:, slots].set(values, mode="drop")


def pack_index(row_index, slots, capacity, hosted):
    return jnp.full((capacity,), hosted, jnp.int32).at[slots].set(row_index, mode="drop")


def add_rows(totals, values, row_index):
    return totals.at[:, row_index].add(values, mode="drop")


def read_rows(totals, row_index):
    return jnp.take(totals, jnp.clip(row_index, 0, totals.shape[1] - 1), axis=1)


def outgoing_rows(state, source):
    return jnp.take(state, source, axis=1).T


def arrival_rows(dom_got, sub_got, move_cap):
    return jnp.concatenate(
        [dom_got[:move_cap], dom_got[3 * move_cap :], sub_got[:move_cap], sub_got[3 * move_cap :]],
        axis=0,
    )


def land_rows(state, arrived, landing):
    return state.at[:, landing].set(arrived.T, mode="drop")


def on_device(solution, forcing, metric, entity_ids, new_owner):
    dom_count = lax.axis_size("dom")
    sub_count = lax.axis_size("sub")
    dom_index = lax.axis_index("dom")
    sub_index = lax.axis_index("sub")
    own_index = dom_index * sub_count + sub_index
    dom_ahead = (dom_index + 1) % dom_count
    dom_behind = (dom_index + dom_count - 1) % dom_count
    sub_ahead = (sub_index + 1) % sub_count
    sub_behind = (sub_index + sub_count - 1) % sub_count
    next_dom = dom_ahead * sub_count + sub_index
    prev_dom = dom_behind * sub_count + sub_index
    next_sub = dom_index * sub_count + sub_ahead
    prev_sub = dom_index * sub_count + sub_behind
    next_both = dom_ahead * sub_count + sub_ahead
    elem_count = solution.shape[-1]
    metric_rows = metric.reshape(-1, elem_count)
    departed = new_owner != own_index
    column = jnp.full((elem_count,), 4 * MOVE, jnp.int32)
    count_list = []
    for direction, target in enumerate((prev_dom, next_dom, prev_sub, next_sub)):
        chosen = departed & (new_owner == target)
        ranked = jnp.cumsum(chosen.astype(jnp.int32)) - 1
        column = jnp.where(chosen, direction * MOVE + ranked, column)
        count_list.append(jnp.sum(chosen.astype(jnp.int32)))
    source = (
        jnp.zeros((4 * MOVE,), jnp.int32)
        .at[column]
        .set(jnp.arange(elem_count, dtype=jnp.int32), mode="drop")
    )
    counts = jnp.stack(count_list)
    offsets = jnp.cumsum(counts) - counts
    hole_rank = jnp.cumsum(departed.astype(jnp.int32)) - 1
    hole_slot = (
        jnp.zeros((elem_count,), jnp.int32)
        .at[jnp.where(departed, hole_rank, elem_count)]
        .set(jnp.arange(elem_count, dtype=jnp.int32), mode="drop")
    )
    arrive_index = jnp.arange(4 * MOVE, dtype=jnp.int32)
    arrive_dir = arrive_index // MOVE
    arrive_pos = arrive_index % MOVE
    filled = arrive_pos < counts[arrive_dir]
    landing = jnp.where(
        filled, hole_slot[jnp.clip(offsets[arrive_dir] + arrive_pos, 0, elem_count - 1)], elem_count
    )
    metric_out = outgoing_rows(metric_rows, source)
    metric_dom = padded(metric_out[: 2 * MOVE], (("dom", 0),), MOVE)
    metric_sub = padded(metric_out[2 * MOVE :], (("sub", 0),), MOVE)
    moved_metric = land_rows(
        metric_rows, arrival_rows(metric_dom, metric_sub, MOVE), landing
    ).reshape(metric.shape)
    derivative = derivative_table(solution.shape[0] - 1)
    image, diagonal = element_apply(solution, metric, derivative)
    stacked_pair = jnp.stack([image, diagonal], axis=3)
    parts = shared_parts(stacked_pair)
    blocks = (3 * elem_count, 3 * elem_count, elem_count)
    id_ranges = ((0, 6), (6, 18), (18, 26))
    dom_caps = (EY * EZ, EZ * (4 * EY - 1), EZ * (4 * EY - 2))
    sub_caps = (EX * EZ, EZ * (4 * EX - 1), EZ * (4 * EX - 2))
    both_caps = (0, EZ, 2 * EZ)
    totals_list, owner_list, index_list = ([], [], [])
    dom_slots, dom_out, dom_rows = ([], [], [])
    sub_slots, sub_out, sub_rows = ([], [], [])
    both_slots, both_out, both_rows = ([None], [None], [None])
    for kind_index in range(3):
        start_row, stop_row = id_ranges[kind_index]
        id_list = entity_ids[start_row:stop_row].reshape(-1)
        hosted = blocks[kind_index]
        owner_dev = id_list // hosted
        row_index = id_list % hosted
        values = pack_values(parts[kind_index])
        totals = jnp.zeros((values.shape[0], hosted), jnp.float32)
        totals = add_rows(totals, values, jnp.where(owner_dev == own_index, row_index, hosted))
        totals_list.append(totals)
        owner_list.append(owner_dev)
        index_list.append(row_index)
        slot_dom = select_slots(owner_dev == next_dom, dom_caps[kind_index])
        dom_slots.append(slot_dom)
        dom_out.append(pack_columns(values, slot_dom, dom_caps[kind_index]))
        dom_rows.append(pack_index(row_index, slot_dom, dom_caps[kind_index], hosted))
        slot_sub = select_slots(owner_dev == next_sub, sub_caps[kind_index])
        sub_slots.append(slot_sub)
        sub_out.append(pack_columns(values, slot_sub, sub_caps[kind_index]))
        sub_rows.append(pack_index(row_index, slot_sub, sub_caps[kind_index], hosted))
        if kind_index > 0:
            slot_both = select_slots(owner_dev == next_both, both_caps[kind_index])
            both_slots.append(slot_both)
            both_out.append(pack_columns(values, slot_both, both_caps[kind_index]))
            both_rows.append(pack_index(row_index, slot_both, both_caps[kind_index], hosted))
    got_dom = from_behind(
        (
            dom_out[0],
            dom_out[1],
            dom_out[2],
            both_out[1],
            both_out[2],
            dom_rows[0],
            dom_rows[1],
            dom_rows[2],
            both_rows[1],
            both_rows[2],
        ),
        "dom",
        1,
    )
    for kind_index in range(3):
        totals_list[kind_index] = add_rows(
            totals_list[kind_index], got_dom[kind_index], got_dom[5 + kind_index]
        )
    got_sub = from_behind(
        (
            sub_out[0],
            sub_out[1],
            sub_out[2],
            got_dom[3],
            got_dom[4],
            sub_rows[0],
            sub_rows[1],
            sub_rows[2],
            got_dom[8],
            got_dom[9],
        ),
        "sub",
        1,
    )
    for kind_index in range(3):
        totals_list[kind_index] = add_rows(
            totals_list[kind_index], got_sub[kind_index], got_sub[5 + kind_index]
        )
    totals_list[1] = add_rows(totals_list[1], got_sub[3], got_sub[8])
    totals_list[2] = add_rows(totals_list[2], got_sub[4], got_sub[9])
    back_sub = from_behind(
        (
            read_rows(totals_list[0], got_sub[5]),
            read_rows(totals_list[1], got_sub[6]),
            read_rows(totals_list[2], got_sub[7]),
            read_rows(totals_list[1], got_sub[8]),
            read_rows(totals_list[2], got_sub[9]),
        ),
        "sub",
        -1,
    )
    back_dom = from_behind(
        (
            read_rows(totals_list[0], got_dom[5]),
            read_rows(totals_list[1], got_dom[6]),
            read_rows(totals_list[2], got_dom[7]),
            back_sub[3],
            back_sub[4],
        ),
        "dom",
        -1,
    )
    merged_parts = []
    for kind_index in range(3):
        owner_dev = owner_list[kind_index]
        merged = read_rows(totals_list[kind_index], index_list[kind_index])
        from_dom = jnp.take(
            back_dom[kind_index],
            jnp.clip(dom_slots[kind_index], 0, dom_caps[kind_index] - 1),
            axis=1,
        )
        merged = jnp.where((owner_dev == next_dom)[None, :], from_dom, merged)
        from_sub = jnp.take(
            back_sub[kind_index],
            jnp.clip(sub_slots[kind_index], 0, sub_caps[kind_index] - 1),
            axis=1,
        )
        merged = jnp.where((owner_dev == next_sub)[None, :], from_sub, merged)
        if kind_index > 0:
            from_both = jnp.take(
                back_dom[2 + kind_index],
                jnp.clip(both_slots[kind_index], 0, both_caps[kind_index] - 1),
                axis=1,
            )
            merged = jnp.where((owner_dev == next_both)[None, :], from_both, merged)
        merged_parts.append(unpack_values(merged, parts[kind_index].shape))
    assembled = place_shared(stacked_pair, merged_parts[0], merged_parts[1], merged_parts[2])
    relaxed = solution + RELAX * (forcing - assembled[:, :, :, 0]) / assembled[:, :, :, 1]
    relaxed_rows = relaxed.reshape(-1, elem_count)
    field_rows = relaxed_rows.shape[0]
    leaving_rows = outgoing_rows(relaxed_rows, source)
    moved_dom = padded(leaving_rows[: 2 * MOVE], (("dom", 0),), MOVE)
    moved_sub = padded(leaving_rows[2 * MOVE :], (("sub", 0),), MOVE)
    landed = land_rows(relaxed_rows, arrival_rows(moved_dom, moved_sub, MOVE), landing)
    smoothed = landed[:field_rows].reshape(solution.shape)
    return (smoothed, moved_metric)


def solution(mesh):
    placed = (
        P(None, None, None, ("dom", "sub")),
        P(None, None, None, ("dom", "sub")),
        P(None, None, None, None, ("dom", "sub")),
        P(None, ("dom", "sub")),
        P(("dom", "sub")),
    )
    return jax.shard_map(
        on_device,
        mesh=mesh,
        in_specs=placed,
        out_specs=(P(None, None, None, ("dom", "sub")), P(None, None, None, None, ("dom", "sub"))),
        check_vma=False,
    )
```

profile of v0, /device:TPU:0, one launch (start us, length us, event | category | flops | bytes accessed | tf_op | source)
XLA Modules:
  0.0 833.0 jit_solution(11345318418168389421)
XLA Ops:
  4.9 12.2 %scatter_custom_fusion.1 = s32[128]{0:T(128)} fusion(s32[3072]{0:T(1024)S(1)} %bitcast.625, s32[3072]{0:T(1024)S(1)} %add_select_fusion.6, s32[]{:T(128)} %constant.1239.clone.1), kind=kCustom, calls=%fused_computation.568 | custom fusion | bytes 516 | tf_op jit(solution)/shard_map/scatter | solution.py:166
  79.3 12.3 %scatter_custom_fusion.4 = s32[128]{0:T(128)} fusion(s32[3072]{0:T(1024)S(1)} %bitcast.623, s32[3072]{0:T(1024)S(1)} %add_select_fusion.6, s32[]{:T(128)} %constant.1239.clone.1), kind=kCustom, calls=%fused_computation.566 | custom fusion | bytes 516 | tf_op jit(solution)/shard_map/scatter | solution.py:166
  98.1 23.5 %scatter_custom_fusion.9 = s32[480]{0:T(512)} fusion(s32[6144]{0:T(1024)S(1)} %bitcast.613, s32[6144]{0:T(1024)S(1)} %add_select_fusion, s32[]{:T(128)} %constant.1239.clone.1), kind=kCustom, calls=%fused_computation.555 | custom fusion | bytes 1924 | tf_op jit(solution)/shard_map/scatter | solution.py:166
  121.6 23.4 %scatter_custom_fusion.7 = s32[32]{0:T(128)} fusion(s32[6144]{0:T(1024)S(1)} %bitcast.609, s32[6144]{0:T(1024)S(1)} %add_select_fusion, s32[]{:T(128)} %constant.1239.clone.1), kind=kCustom, calls=%fused_computation.564 | custom fusion | bytes 132 | tf_op jit(solution)/shard_map/scatter | solution.py:166
  160.7 16.5 %scatter_custom_fusion.10 = f32[12,480]{0,1:T(8,128)} fusion(s32[6144]{0:T(1024)} %bitcast.614, f32[6144,12]{1,0:T(8,128)} %copy.832, f32[]{:T(128)} %constant.1247.clone.1), kind=kCustom, calls=%fused_computation.232 | custom fusion | bytes 23552 | tf_op jit(solution)/shard_map/scatter | solution.py:162
  177.2 23.7 %scatter_custom_fusion.12 = s32[480]{0:T(512)} fusion(s32[6144]{0:T(1024)} %bitcast.611, s32[6144]{0:T(1024)} %copy-done.48, s32[]{:T(128)} %constant.1239.clone.1), kind=kCustom, calls=%fused_computation.553 | custom fusion | bytes 2432 | tf_op jit(solution)/shard_map/scatter | solution.py:166
  200.9 16.5 %scatter_custom_fusion.13 = f32[12,480]{0,1:T(8,128)} fusion(s32[6144]{0:T(1024)} %bitcast.612, f32[6144,12]{1,0:T(8,128)} %copy.832, f32[]{:T(128)} %constant.1247.clone.1), kind=kCustom, calls=%fused_computation.230 | custom fusion | bytes 23552 | tf_op jit(solution)/shard_map/scatter | solution.py:162
  217.4 16.4 %scatter_custom_fusion.15 = f32[12,32]{0,1:T(8,128)} fusion(s32[6144]{0:T(1024)} %bitcast.610, f32[6144,12]{1,0:T(8,128)} %copy.832, f32[]{:T(128)} %constant.1247.clone.1), kind=kCustom, calls=%fused_computation.436 | custom fusion | bytes 2048 | tf_op jit(solution)/shard_map/scatter | solution.py:162
  240.0 11.3 %scatter_custom_fusion.20 = f32[2,448]{0,1:T(8,128)} fusion(s32[4096]{0:T(1024)S(1)} %bitcast.620, f32[4096,2]{1,0:T(8,128)S(1)} %bitcast.569, f32[]{:T(128)} %constant.1247.clone.1), kind=kCustom, calls=%fused_computation.236 | custom fusion | bytes 3588 | tf_op jit(solution)/shard_map/scatter | solution.py:162
  251.3 16.4 %scatter_custom_fusion.19 = s32[448]{0:T(512)} fusion(s32[4096]{0:T(1024)S(1)} %bitcast.621, s32[4096]{0:T(1024)S(1)} %get-tuple-element.336, s32[]{:T(128)} %constant.1262.clone.1), kind=kCustom, calls=%fused_computation.551 | custom fusion | bytes 1796 | tf_op jit(solution)/shard_map/scatter | solution.py:166
  267.7 16.1 %scatter_custom_fusion.22 = s32[448]{0:T(512)} fusion(s32[4096]{0:T(1024)S(1)} %bitcast.618, s32[4096]{0:T(1024)S(1)} %get-tuple-element.336, s32[]{:T(128)} %constant.1262.clone.1), kind=kCustom, calls=%fused_computation.549 | custom fusion | bytes 1796 | tf_op jit(solution)/shard_map/scatter | solution.py:166
  283.8 10.7 %scatter_custom_fusion.23 = f32[2,448]{0,1:T(8,128)S(1)} fusion(s32[4096]{0:T(1024)S(1)} %bitcast.619, f32[4096,2]{1,0:T(8,128)S(1)} %bitcast.570, f32[]{:T(128)} %constant.1247.clone.1), kind=kCustom, calls=%fused_computation.234 | custom fusion | bytes 3588 | tf_op jit(solution)/shard_map/scatter | solution.py:162
  294.5 16.0 %scatter_custom_fusion.17 = s32[64]{0:T(128)} fusion(s32[4096]{0:T(1024)S(1)} %bitcast.616, s32[4096]{0:T(1024)S(1)} %get-tuple-element.336, s32[]{:T(128)} %constant.1262.clone.1), kind=kCustom, calls=%fused_computation.562 | custom fusion | bytes 260 | tf_op jit(solution)/shard_map/scatter | solution.py:166
  310.4 11.2 %scatter_custom_fusion.25 = f32[2,64]{0,1:T(8,128)} fusion(s32[4096]{0:T(1024)S(1)} %bitcast.617, f32[4096,2]{1,0:T(8,128)S(1)} %bitcast.571, f32[]{:T(128)} %constant.1247.clone.1), kind=kCustom, calls=%fused_computation.387 | custom fusion | bytes 516 | tf_op jit(solution)/shard_map/scatter | solution.py:162
  328.2 17.6 %scatter_custom_fusion = f32[72,1536]{0,1:T(8,128)S(1)} fusion(s32[3072]{0:T(1024)} %bitcast.622, f32[3072,72]{1,0:T(8,128)} %copy.802, f32[]{:T(128)} %constant.1247.clone.1), kind=kCustom, calls=%fused_computation.187 | custom fusion | flops 221184 | bytes 442880 | tf_op jit(solution)/shard_map/scatter-add | solution.py:170
  368.5 33.7 %scatter_custom_fusion.8 = f32[12,1536]{0,1:T(8,128)S(1)} fusion(s32[6144]{0:T(1024)} %bitcast.608, f32[6144,12]{1,0:T(8,128)} %copy.832, f32[]{:T(128)} %constant.1247.clone.1), kind=kCustom, calls=%fused_computation.185 | custom fusion | flops 73728 | bytes 74240 | tf_op jit(solution)/shard_map/scatter-add | solution.py:170
  403.8 22.7 %scatter_custom_fusion.18 = f32[2,512]{0,1:T(8,128)S(1)} fusion(s32[4096]{0:T(1024)} %bitcast.615, f32[4096,2]{1,0:T(8,128)} %bitcast.572, f32[]{:T(128)} %constant.1247.clone.1), kind=kCustom, calls=%fused_computation.228 | custom fusion | flops 8192 | bytes 4608 | tf_op jit(solution)/shard_map/scatter-add | solution.py:170
  482.3 14.1 %gather_fusion.7 = f32[4096,2]{1,0:T(8,128)} fusion(f32[2,512]{0,1:T(8,128)S(1)} %scatter_custom_fusion.26, s32[4096]{0:T(1024)S(1)} %get-tuple-element.519), kind=kCustom, calls=%fused_computation.19 | custom fusion | bytes 81920 | tf_op jit(solution)/shard_map/jit(_take)/gather | solution.py:174
  496.7 14.1 %gather_fusion.6 = f32[4096,2]{1,0:T(8,128)} fusion(f32[2,64]{0,1:T(8,128)S(1)} %collective-permute-done.27, s32[4096]{0:T(1024)S(1)} %get-tuple-element.520), kind=kCustom, calls=%fused_computation.18 | custom fusion | bytes 81920 | tf_op jit(solution)/shard_map/jit(_take)/gather | solution.py:362
  510.7 14.2 %gather_fusion.22 = f32[4096,2]{1,0:T(8,128)} fusion(f32[2,448]{0,1:T(8,128)S(1)} %collective-permute-done.29, s32[4096]{0:T(1024)S(1)} %get-tuple-element.518), kind=kCustom, calls=%fused_computation.11.clone | custom fusion | bytes 81920 | tf_op jit(solution)/shard_map/jit(_take)/gather | solution.py:349
  528.3 14.1 %gather_fusion.20 = f32[4096,2]{1,0:T(8,128)} fusion(f32[2,448]{0,1:T(8,128)S(1)} %collective-permute-done.28, s32[4096]{0:T(1024)S(1)} %get-tuple-element.517), kind=kCustom, calls=%fused_computation.5.clone | custom fusion | bytes 81920 | tf_op jit(solution)/shard_map/jit(_take)/gather | solution.py:355
  542.4 9.2 %fusion.11 = f32[2,4096]{0,1:T(8,128)} fusion(f32[4096,2]{1,0:T(8,128)} %gather_fusion.22, f32[4096,2]{1,0:T(8,128)} %gather_fusion.20, f32[4096,2]{1,0:T(8,128)} %gather_fusion.7, f32[4096,2]{1,0:T(8,128)} %gather_fusion.6, pred[4096]{0:T(1024)(128)(4,1)} %get-tuple-element.471, pred[4096]{0:T(1024)(128)(4,1)} %get-tuple-element.337, ...), kind=kLoop, calls=%fused_computation.120 | loop fusion | flops 57344 | bytes 192512 | tf_op jit(solution)/shard_map/jit(_where)/select_n | solution.py:367
  572.5 23.9 %collective-permute-done.14 = f32[12,32]{0,1:T(8,128)S(1)} collective-permute-done((f32[12,32]{0,1:T(8,128)S(1)}, f32[12,32]{0,1:T(8,128)S(1)}, u32[]{:S(2)}, u32[]{:S(2)}) %collective-permute-start.14) | collective-permute-done | bytes 1568 | tf_op jit(solution)/shard_map/ppermute | solution.py:32
  598.2 20.9 %gather_fusion.4 = f32[6144,12]{1,0:T(8,128)} fusion(f32[12,1536]{0,1:T(8,128)S(1)} %scatter_custom_fusion.16, s32[6144]{0:T(1024)S(1)} %get-tuple-element.515), kind=kCustom, calls=%fused_computation.16 | custom fusion | bytes 614400 | tf_op jit(solution)/shard_map/jit(_take)/gather | solution.py:174
  619.1 20.9 %gather_fusion.3 = f32[6144,12]{1,0:T(8,128)} fusion(f32[12,32]{0,1:T(8,128)S(1)} %collective-permute-done.15, s32[6144]{0:T(1024)S(1)} %get-tuple-element.516), kind=kCustom, calls=%fused_computation.15 | custom fusion | bytes 614400 | tf_op jit(solution)/shard_map/jit(_take)/gather | solution.py:362
  650.0 10.8 %gather_fusion.1 = f32[3072,72]{1,0:T(8,128)} fusion(f32[72,1536]{0,1:T(8,128)S(1)} %scatter_custom_fusion.6, s32[3072]{0:T(1024)S(1)} %copy-done.33), kind=kCustom, calls=%fused_computation.13 | custom fusion | bytes 1781760 | tf_op jit(solution)/shard_map/jit(_take)/gather | solution.py:174
  661.7 21.1 %gather_fusion.18 = f32[6144,12]{1,0:T(8,128)} fusion(f32[12,480]{0,1:T(8,128)S(1)} %collective-permute-done.17, s32[6144]{0:T(1024)S(1)} %get-tuple-element.514), kind=kCustom, calls=%fused_computation.9.clone | custom fusion | bytes 614400 | tf_op jit(solution)/shard_map/jit(_take)/gather | solution.py:349
  683.2 20.9 %gather_fusion.16 = f32[6144,12]{1,0:T(8,128)} fusion(f32[12,480]{0,1:T(8,128)S(1)} %collective-permute-done.16, s32[6144]{0:T(1024)S(1)} %get-tuple-element.513), kind=kCustom, calls=%fused_computation.3.clone | custom fusion | bytes 614400 | tf_op jit(solution)/shard_map/jit(_take)/gather | solution.py:355
  704.2 10.3 %fusion.9 = f32[12,6144]{0,1:T(8,128)} fusion(f32[6144,12]{1,0:T(8,128)} %gather_fusion.18, f32[6144,12]{1,0:T(8,128)} %gather_fusion.16, f32[6144,12]{1,0:T(8,128)} %gather_fusion.4, f32[6144,12]{1,0:T(8,128)} %gather_fusion.3, pred[6144]{0:T(1024)(128)(4,1)S(1)} %copy-done.47, pred[6144]{0:T(1024)(128)(4,1)S(1)} %copy-done.46, ...), kind=kLoop, calls=%fused_computation.117 | loop fusion | flops 516096 | bytes 1517568 | tf_op jit(solution)/shard_map/jit(_where)/select_n | solution.py:367
  722.9 10.9 %gather_fusion.14 = f32[3072,72]{1,0:T(8,128)} fusion(f32[72,128]{0,1:T(8,128)S(1)} %collective-permute-done.5, s32[3072]{0:T(1024)S(1)} %copy-done.32), kind=kCustom, calls=%fused_computation.7.clone | custom fusion | bytes 1781760 | tf_op jit(solution)/shard_map/jit(_take)/gather | solution.py:349
  733.8 10.8 %gather_fusion.12 = f32[3072,72]{1,0:T(8,128)} fusion(f32[72,128]{0,1:T(8,128)S(1)} %collective-permute-done.4, s32[3072]{0:T(1024)S(1)} %copy-done.31), kind=kCustom, calls=%fused_computation.1.clone | custom fusion | bytes 1781760 | tf_op jit(solution)/shard_map/jit(_take)/gather | solution.py:355
  814.0 10.4 %scatter_custom_fusion.30 = f32[3584,512]{0,1:T(8,128)} fusion(f32[3584,512]{0,1:T(8,128)} %copy.880, s32[256]{0:T(256)S(1)} %bitcast.630, f32[64,3584]{1,0:T(8,128)} %collective-permute-done.37, f32[]{:T(128)} %constant.1307, f32[64,3584]{1,0:T(8,128)} %collective-permute-done.36, f32[64,3584]{1,0:T(8,128)} %collective-permute-done.35, ...), kind=kCustom, calls=%fused_computation.107 | custom fusion | flops 2752512 | bytes 11010560 | tf_op jit(solution)/shard_map/scatter | solution.py:189
  (484 shorter events, 303.4 us)
Async XLA Ops:
  17.2 413.9 %collective-permute-start = (s32[128]{0:T(128)}, s32[128]{0:T(128)}, u32[]{:S(2)}, u32[]{:S(2)}) collective-permute-start(s32[128]{0:T(128)} %scatter_custom_fusion.1), channel_id=1, source_target_pairs={{0,4},{4,8},{8,12},{12,16},{16,20},{20,24},{24,28},{28,0},{1,5},{5... | collective-permute-start | bytes 1544 | tf_op jit(solution)/shard_map/ppermute | solution.py:32
  76.7 563.3 %collective-permute-start.1 = (f32[72,128]{0,1:T(8,128)}, f32[72,128]{0,1:T(8,128)}, u32[]{:S(2)}, u32[]{:S(2)}) collective-permute-start(f32[72,128]{0,1:T(8,128)} %scatter_custom_fusion.2), channel_id=1, source_target_pairs={{0,4},{4,8},{8,12},{12,16},{16,20},{20,24},{24,28},{28,0},{1,5},{5... | collective-permute-start | bytes 110600 | tf_op jit(solution)/shard_map/ppermute | solution.py:32
  91.6 344.0 %collective-permute-start.2 = (s32[128]{0:T(128)}, s32[128]{0:T(128)}, u32[]{:S(2)}, u32[]{:S(2)}) collective-permute-start(s32[128]{0:T(128)} %scatter_custom_fusion.4), channel_id=1, source_target_pairs={{0,1},{1,2},{2,3},{3,0},{4,5},{5,6},{6,7},{7,4},{8,9},{9,10},{10,1... | collective-permute-start | bytes 1544 | tf_op jit(solution)/shard_map/ppermute | solution.py:32
  121.6 330.8 %collective-permute-start.8 = (s32[480]{0:T(512)}, s32[480]{0:T(512)}, u32[]{:S(2)}, u32[]{:S(2)}) collective-permute-start(s32[480]{0:T(512)} %scatter_custom_fusion.9), channel_id=1, source_target_pairs={{0,4},{4,8},{8,12},{12,16},{16,20},{20,24},{24,28},{28,0},{1,5},{5... | collective-permute-start | bytes 5768 | tf_op jit(solution)/shard_map/ppermute | solution.py:32
  145.0 257.1 %collective-permute-start.6 = (s32[32]{0:T(128)}, s32[32]{0:T(128)}, u32[]{:S(2)}, u32[]{:S(2)}) collective-permute-start(s32[32]{0:T(128)} %scatter_custom_fusion.7), channel_id=1, source_target_pairs={{0,4},{4,8},{8,12},{12,16},{16,20},{20,24},{24,28},{28,0},{1,5},{5... | collective-permute-start | bytes 392 | tf_op jit(solution)/shard_map/ppermute | solution.py:32
  402.2 24.4 %collective-permute-start.7 = (s32[32]{0:T(128)}, s32[32]{0:T(128)}, u32[]{:S(2)}, u32[]{:S(2)}) collective-permute-start(s32[32]{0:T(128)} %collective-permute-done.6), channel_id=1, source_target_pairs={{0,1},{1,2},{2,3},{3,0},{4,5},{5,6},{6,7},{7,4},{8,9},{9,10},{10,1... | collective-permute-start | bytes 392 | tf_op jit(solution)/shard_map/ppermute | solution.py:32
  426.5 30.9 %collective-permute-start.10 = (s32[480]{0:T(512)}, s32[480]{0:T(512)S(1)}, u32[]{:S(2)}, u32[]{:S(2)}) collective-permute-start(s32[480]{0:T(512)} %scatter_custom_fusion.12), channel_id=1, source_target_pairs={{0,1},{1,2},{2,3},{3,0},{4,5},{5,6},{6,7},{7,4},{8,9},{9,10},{10,1... | collective-permute-start | bytes 5768 | tf_op jit(solution)/shard_map/ppermute | solution.py:32
  435.0 89.9 %collective-permute-start.12 = (f32[12,32]{0,1:T(8,128)}, f32[12,32]{0,1:T(8,128)}, u32[]{:S(2)}, u32[]{:S(2)}) collective-permute-start(f32[12,32]{0,1:T(8,128)} %scatter_custom_fusion.15), channel_id=1, source_target_pairs={{0,4},{4,8},{8,12},{12,16},{16,20},{20,24},{24,28},{28,0},{1,5},{5... | collective-permute-start | bytes 4616 | tf_op jit(solution)/shard_map/ppermute | solution.py:32
  445.1 5.6 collective-permute-start.22
  450.7 8.0 collective-permute-start.21
  457.5 7.9 collective-permute-start.23
  457.5 11.6 %collective-permute-start.25 = (f32[2,64]{0,1:T(8,128)}, f32[2,64]{0,1:T(8,128)S(1)}, u32[]{:S(2)}, u32[]{:S(2)}) collective-permute-start(f32[2,64]{0,1:T(8,128)} %collective-permute-done.24), channel_id=1, source_target_pairs={{0,1},{1,2},{2,3},{3,0},{4,5},{5,6},{6,7},{7,4},{8,9},{9,10},{10,1... | collective-permute-start | bytes 1544 | tf_op jit(solution)/shard_map/ppermute | solution.py:32
  473.0 37.8 %collective-permute-start.29 = (f32[2,448]{0,1:T(8,128)}, f32[2,448]{0,1:T(8,128)S(1)}, u32[]{:S(2)}, u32[]{:S(2)}) collective-permute-start(f32[2,448]{0,1:T(8,128)} %select_bitcast_fusion.2), channel_id=1, source_target_pairs={{0,28},{4,0},{8,4},{12,8},{16,12},{20,16},{24,20},{28,24},{1,29},{... | collective-permute-start | bytes 10760 | tf_op jit(solution)/shard_map/ppermute | solution.py:32
  478.4 48.2 %collective-permute-start.28 = (f32[2,448]{0,1:T(8,128)}, f32[2,448]{0,1:T(8,128)S(1)}, u32[]{:S(2)}, u32[]{:S(2)}) collective-permute-start(f32[2,448]{0,1:T(8,128)} %select_bitcast_fusion.3), channel_id=1, source_target_pairs={{0,3},{1,0},{2,1},{3,2},{4,7},{5,4},{6,5},{7,6},{8,11},{9,8},{10,9... | collective-permute-start | bytes 10760 | tf_op jit(solution)/shard_map/ppermute | solution.py:32
  480.5 15.9 %collective-permute-start.27 = (f32[2,64]{0,1:T(8,128)}, f32[2,64]{0,1:T(8,128)S(1)}, u32[]{:S(2)}, u32[]{:S(2)}) collective-permute-start(f32[2,64]{0,1:T(8,128)} %collective-permute-done.26), channel_id=1, source_target_pairs={{0,28},{4,0},{8,4},{12,8},{16,12},{20,16},{24,20},{28,24},{1,29},{... | collective-permute-start | bytes 1544 | tf_op jit(solution)/shard_map/ppermute | solution.py:32
  496.4 146.0 %collective-permute-start.3 = (f32[72,128]{0,1:T(8,128)}, f32[72,128]{0,1:T(8,128)}, u32[]{:S(2)}, u32[]{:S(2)}) collective-permute-start(f32[72,128]{0,1:T(8,128)} %scatter_custom_fusion.5), channel_id=1, source_target_pairs={{0,1},{1,2},{2,3},{3,0},{4,5},{5,6},{6,7},{7,4},{8,9},{9,10},{10,1... | collective-permute-start | bytes 110600 | tf_op jit(solution)/shard_map/ppermute | solution.py:32
  510.7 43.8 %collective-permute-start.9 = (f32[12,480]{0,1:T(8,128)}, f32[12,480]{0,1:T(8,128)}, u32[]{:S(2)}, u32[]{:S(2)}) collective-permute-start(f32[12,480]{0,1:T(8,128)} %scatter_custom_fusion.10), channel_id=1, source_target_pairs={{0,4},{4,8},{8,12},{12,16},{16,20},{20,24},{24,28},{28,0},{1,5},{5... | collective-permute-start | bytes 69128 | tf_op jit(solution)/shard_map/ppermute | solution.py:32
  524.9 35.6 %collective-permute-start.11 = (f32[12,480]{0,1:T(8,128)}, f32[12,480]{0,1:T(8,128)S(1)}, u32[]{:S(2)}, u32[]{:S(2)}) collective-permute-start(f32[12,480]{0,1:T(8,128)} %scatter_custom_fusion.13), channel_id=1, source_target_pairs={{0,1},{1,2},{2,3},{3,0},{4,5},{5,6},{6,7},{7,4},{8,9},{9,10},{10,1... | collective-permute-start | bytes 69128 | tf_op jit(solution)/shard_map/ppermute | solution.py:32
  526.7 37.5 %collective-permute-start.13 = (f32[12,32]{0,1:T(8,128)}, f32[12,32]{0,1:T(8,128)S(1)}, u32[]{:S(2)}, u32[]{:S(2)}) collective-permute-start(f32[12,32]{0,1:T(8,128)} %collective-permute-done.12), channel_id=1, source_target_pairs={{0,1},{1,2},{2,3},{3,0},{4,5},{5,6},{6,7},{7,4},{8,9},{9,10},{10,1... | collective-permute-start | bytes 4616 | tf_op jit(solution)/shard_map/ppermute | solution.py:32
  554.5 259.5 %collective-permute-start.37 = (f32[64,3584]{1,0:T(8,128)}, f32[64,3584]{1,0:T(8,128)}, u32[]{:S(2)}, u32[]{:S(2)}) collective-permute-start(f32[64,3584]{1,0:T(8,128)} %get-tuple-element.391), channel_id=1, source_target_pairs={{1,0},{2,1},{3,2},{0,3},{5,4},{6,5},{7,6},{4,7},{9,8},{10,9},{11,1... | collective-permute-start | bytes 2752520 | tf_op jit(solution)/shard_map/ppermute | solution.py:24
  560.5 253.4 %collective-permute-start.36 = (f32[64,3584]{1,0:T(8,128)}, f32[64,3584]{1,0:T(8,128)}, u32[]{:S(2)}, u32[]{:S(2)}) collective-permute-start(f32[64,3584]{1,0:T(8,128)} %get-tuple-element.389), channel_id=1, source_target_pairs={{0,1},{1,2},{2,3},{3,0},{4,5},{5,6},{6,7},{7,4},{8,9},{9,10},{10,1... | collective-permute-start | bytes 2752520 | tf_op jit(solution)/shard_map/ppermute | solution.py:23
  567.3 29.0 %collective-permute-start.14 = (f32[12,32]{0,1:T(8,128)S(1)}, f32[12,32]{0,1:T(8,128)S(1)}, u32[]{:S(2)}, u32[]{:S(2)}) collective-permute-start(f32[12,32]{0,1:T(8,128)S(1)} %select_bitcast_fusion.7), channel_id=1, source_target_pairs={{0,3},{1,0},{2,1},{3,2},{4,7},{5,4},{6,5},{7,6},{8,11},{9,8},{10,9... | collective-permute-start | bytes 4616 | tf_op jit(solution)/shard_map/ppermute | solution.py:32
  596.3 22.8 %collective-permute-start.15 = (f32[12,32]{0,1:T(8,128)S(1)}, f32[12,32]{0,1:T(8,128)S(1)}, u32[]{:S(2)}, u32[]{:S(2)}) collective-permute-start(f32[12,32]{0,1:T(8,128)S(1)} %collective-permute-done.14), channel_id=1, source_target_pairs={{0,28},{4,0},{8,4},{12,8},{16,12},{20,16},{24,20},{28,24},{1,29},{... | collective-permute-start | bytes 4616 | tf_op jit(solution)/shard_map/ppermute | solution.py:32
  619.1 194.8 %collective-permute-start.35 = (f32[64,3584]{1,0:T(8,128)}, f32[64,3584]{1,0:T(8,128)}, u32[]{:S(2)}, u32[]{:S(2)}) collective-permute-start(f32[64,3584]{1,0:T(8,128)} %get-tuple-element.390), channel_id=1, source_target_pairs={{4,0},{8,4},{12,8},{16,12},{20,16},{24,20},{28,24},{0,28},{5,1},{9... | collective-permute-start | bytes 2752520 | tf_op jit(solution)/shard_map/ppermute | solution.py:24
  640.0 20.8 %collective-permute-start.17 = (f32[12,480]{0,1:T(8,128)S(1)}, f32[12,480]{0,1:T(8,128)S(1)}, u32[]{:S(2)}, u32[]{:S(2)}) collective-permute-start(f32[12,480]{0,1:T(8,128)S(1)} %select_bitcast_fusion), channel_id=1, source_target_pairs={{0,28},{4,0},{8,4},{12,8},{16,12},{20,16},{24,20},{28,24},{1,29},{... | collective-permute-start | bytes 69128 | tf_op jit(solution)/shard_map/ppermute | solution.py:32
  642.4 40.5 %collective-permute-start.16 = (f32[12,480]{0,1:T(8,128)S(1)}, f32[12,480]{0,1:T(8,128)S(1)}, u32[]{:S(2)}, u32[]{:S(2)}) collective-permute-start(f32[12,480]{0,1:T(8,128)S(1)} %select_bitcast_fusion.1), channel_id=1, source_target_pairs={{0,3},{1,0},{2,1},{3,2},{4,7},{5,4},{6,5},{7,6},{8,11},{9,8},{10,9... | collective-permute-start | bytes 69128 | tf_op jit(solution)/shard_map/ppermute | solution.py:32
  660.9 62.0 %collective-permute-start.5 = (f32[72,128]{0,1:T(8,128)S(1)}, f32[72,128]{0,1:T(8,128)S(1)}, u32[]{:S(2)}, u32[]{:S(2)}) collective-permute-start(f32[72,128]{0,1:T(8,128)S(1)} %select_bitcast_fusion.4), channel_id=1, source_target_pairs={{0,28},{4,0},{8,4},{12,8},{16,12},{20,16},{24,20},{28,24},{1,29},{... | collective-permute-start | bytes 110600 | tf_op jit(solution)/shard_map/ppermute | solution.py:32
  682.9 50.9 %collective-permute-start.4 = (f32[72,128]{0,1:T(8,128)S(1)}, f32[72,128]{0,1:T(8,128)S(1)}, u32[]{:S(2)}, u32[]{:S(2)}) collective-permute-start(f32[72,128]{0,1:T(8,128)S(1)} %select_bitcast_fusion.5), channel_id=1, source_target_pairs={{0,3},{1,0},{2,1},{3,2},{4,7},{5,4},{6,5},{7,6},{8,11},{9,8},{10,9... | collective-permute-start | bytes 110600 | tf_op jit(solution)/shard_map/ppermute | solution.py:32
  722.9 91.1 %collective-permute-start.34 = (f32[64,3584]{1,0:T(8,128)}, f32[64,3584]{1,0:T(8,128)}, u32[]{:S(2)}, u32[]{:S(2)}) collective-permute-start(f32[64,3584]{1,0:T(8,128)} %get-tuple-element.388), channel_id=1, source_target_pairs={{0,4},{4,8},{8,12},{12,16},{16,20},{20,24},{24,28},{28,0},{1,5},{5... | collective-permute-start | bytes 2752520 | tf_op jit(solution)/shard_map/ppermute | solution.py:23
  784.1 6.1 collective-permute-start.33
  790.2 7.4 collective-permute-start.32
  797.6 7.8 collective-permute-start.31
  (73 other events, 1794.4 us)
where the time goes:
time: 846 us; the launch traced here: 833 us
  local copies, waits for them, and re-layouts  519 us (61%)
  other arithmetic  192 us (23%)
  waiting for transfers between devices  47.2 us (6%)
  matrix products  37.6 us (4%)
  starting transfers between devices  34.2 us (4%)
    scatter x8, local copies, waits for them, and re-layouts, pack_index(): jnp.full((capacity,), hosted, jnp.int32).at[slots]  144 us
    scatter x8, local copies, waits for them, and re-layouts, pack_columns(): jnp.zeros((values.shape[0], capacity), jnp.float32).at[:, slots]  101 us
    scatter-add x11, other arithmetic, add_rows(): return totals.at[:, row_index].add(values, mode='drop')  95 us
    gather x11, local copies, waits for them, and re-layouts, read_rows(): return jnp.take(totals, jnp.clip(row_index, 0, totals.shape[1] - 1), axis=1)  53.7 us
    gather x3, local copies, waits for them, and re-layouts, on_device(): jnp.take(back_dom[kind_index], jnp.clip(dom_slots[kind_index], 0, dom_cap...  46.2 us
    gather x3, local copies, waits for them, and re-layouts, on_device(): jnp.take(back_sub[kind_index], jnp.clip(sub_slots[kind_index], 0, sub_cap...  45.8 us
    ppermute x30, waiting for transfers between devices, from_behind(): return lax.ppermute(value, axis, pairs)  39.2 us
    gather x2, local copies, waits for them, and re-layouts, on_device(): jnp.take(back_dom[2 + kind_index], jnp.clip(both_slots[kind_index], 0, bo...  35 us
  transfers between devices with their start and end apart: 38, of which 10 were waited for; matrix products, arithmetic and copies ran while one was open for 86% of the time, Pallas kernels for 0%

commit v1 on v0

v1 whole, which is shorter than its diff:
```python
import functools

import jax
import jax.numpy as jnp
import numpy as np
from jax import lax
from jax.experimental import pallas as pl
from jax.experimental.pallas import tpu as pltpu
from jax.sharding import PartitionSpec as P

EX = 4
EY = 4
EZ = 32
MOVE = 64
RELAX = 0.6
LANES = 128
INNER = 6
CHUNKS = (4, 3)

NT = (((1,), (1,)), ((), ()))
VMEM = pl.BlockSpec(memory_space=pltpu.VMEM)
F32 = jnp.float32
BF16 = jnp.bfloat16
I32 = jnp.int32


def derivative_table(order):
    count = order + 1
    points = -np.cos(np.pi * np.arange(count) / order)
    legendre = np.zeros((count, count))
    for sweep in range(80):
        legendre[:, 0] = 1.0
        legendre[:, 1] = points
        for degree in range(2, count):
            legendre[:, degree] = (
                (2 * degree - 1) * points * legendre[:, degree - 1]
                - (degree - 1) * legendre[:, degree - 2]
            ) / degree
        points = points - (points * legendre[:, order] - legendre[:, order - 1]) / (
            count * legendre[:, order]
        )
    legendre[:, 0] = 1.0
    legendre[:, 1] = points
    for degree in range(2, count):
        legendre[:, degree] = (
            (2 * degree - 1) * points * legendre[:, degree - 1]
            - (degree - 1) * legendre[:, degree - 2]
        ) / degree
    values = legendre[:, order]
    identity = np.eye(count)
    spread = points[:, None] - points[None, :] + identity
    table = values[:, None] / values[None, :] / spread
    table = table * (1.0 - identity)
    table[0, 0] = -order * count / 4.0
    table[order, order] = order * count / 4.0
    return table.astype(np.float32)


def split_np(matrix):
    high = matrix.astype(jnp.bfloat16).astype(np.float32)
    low = (matrix - high).astype(jnp.bfloat16)
    return np.concatenate([high.astype(jnp.bfloat16), low, high.astype(jnp.bfloat16)], axis=1)


def split(values):
    high = values.astype(BF16)
    low = (values - high.astype(F32)).astype(BF16)
    return high, low


def triple(values):
    high, low = split(values)
    return jnp.concatenate([high, high, low], axis=0)


def dot(left, right):
    return jnp.dot(left, right, preferred_element_type=F32)


def dot_nt(left, right):
    return lax.dot_general(left, right, NT, preferred_element_type=F32)


def iota(shape, dim):
    return lax.broadcasted_iota(I32, shape, dim)


def one_hot_rows(index_row, start, count):
    size = index_row.shape[1]
    out = []
    for base in range(0, count, LANES):
        local = (index_row - (start + base)).astype(BF16)
        rows = iota((LANES, size), 0).astype(BF16)
        out.append(
            jnp.where(rows == local, jnp.ones((LANES, size), BF16), jnp.zeros((LANES, size), BF16))
        )
    return out[0] if len(out) == 1 else jnp.concatenate(out, axis=0)


def exclusive_count(masks):
    size = masks.shape[1]
    upper = jnp.where(iota((size, size), 0) < iota((size, size), 1), 1.0, 0.0).astype(BF16)
    return dot(masks.astype(BF16), upper)


def gather_tiles(tiles, low, high):
    out = None
    for number, tile in enumerate(tiles):
        got = jnp.take_along_axis(tile, low, axis=1)
        out = got if out is None else jnp.where(high == number, got, out)
    return out


def devices():
    dom_count = lax.axis_size("dom")
    sub_count = lax.axis_size("sub")
    dom = lax.axis_index("dom")
    sub = lax.axis_index("sub")
    dom_ahead = lax.rem(dom + 1, dom_count)
    dom_behind = lax.rem(dom + dom_count - 1, dom_count)
    sub_ahead = lax.rem(sub + 1, sub_count)
    sub_behind = lax.rem(sub + sub_count - 1, sub_count)
    return jnp.stack(
        [
            dom_behind * sub_count + sub,
            dom_ahead * sub_count + sub,
            dom * sub_count + sub_behind,
            dom * sub_count + sub_ahead,
            dom * sub_count + sub,
            dom_ahead * sub_count + sub_ahead,
        ]
    ).astype(I32)


def pack_pair(values):
    half = values.shape[0] // 2
    top, bottom = values[:half], values[half:]
    left = iota(top.shape, 1) < MOVE
    first = jnp.where(left, top, pltpu.roll(bottom, MOVE, 1))
    second = jnp.where(left, pltpu.roll(top, MOVE, 1), bottom)
    return first, second


def unpack_pair(first, second):
    left = iota(first.shape, 1) < MOVE
    top = jnp.where(left, first, pltpu.roll(second, MOVE, 1))
    bottom = jnp.where(left, pltpu.roll(first, MOVE, 1), second)
    return jnp.concatenate([top, bottom], axis=0)


def pick_columns(values, source_row):
    rows, size = values.shape
    source = jnp.broadcast_to(source_row, (rows, LANES))
    tiles = [values[:, c : c + LANES] for c in range(0, size, LANES)]
    return gather_tiles(tiles, source & (LANES - 1), source >> 7)


def move_plan(owner, place):
    size = owner.shape[1]
    own = place[4]
    line = iota((8, size), 0)
    target = jnp.where(
        line == 0,
        place[0],
        jnp.where(line == 1, place[1], jnp.where(line == 2, place[2], place[3])),
    )
    nobody = jnp.broadcast_to(owner, (8, size))
    away = nobody != own
    masks = jnp.where(away & (((nobody == target) & (line < 4)) | (line == 4)), 1.0, 0.0)
    ranks = exclusive_count(masks)
    counts = jnp.sum(masks, axis=1, keepdims=True)
    hole = ranks[4:5]
    gone = masks[4:5] > 0.5
    column = jnp.full((1, size), -1.0, F32)
    landing = jnp.full((1, size), -1.0, F32)
    offset = jnp.zeros((1, 1), F32)
    for way in range(4):
        column = jnp.where(masks[way : way + 1] > 0.5, way * MOVE + ranks[way : way + 1], column)
        ahead = hole - offset
        here = gone & (ahead >= 0.0) & (ahead < counts[way : way + 1])
        landing = jnp.where(here, way * MOVE + ahead, landing)
        offset = offset + counts[way : way + 1]
    spots = one_hot_rows(column.astype(I32), 0, 4 * MOVE)
    element = iota((8, size), 1)
    parts = jnp.where(iota((8, size), 0) == 0, element >> 4, element & 15)
    found = dot_nt(parts.astype(BF16), spots)
    source = found[0:1] * 16.0 + found[1:2]
    return source.astype(I32), landing.astype(I32)


def pack_metric_kernel(place, owner, metric, *refs):
    source_ref, landing_ref = refs[0], refs[1]
    outs = refs[2:]
    step = pl.program_id(0)

    @pl.when(step == 0)
    def _():
        source, landing = move_plan(owner[...], place)
        source_ref[...] = source
        landing_ref[...] = landing

    values = metric[...]
    source = source_ref[...]
    start = 0
    packed = []
    for pair in range(2):
        picked = pick_columns(values, source[:, pair * LANES : (pair + 1) * LANES])
        packed.extend(pack_pair(picked))
    for number, count in enumerate(CHUNKS):

        @pl.when((step >= start) & (step < start + count))
        def _(number=number):
            for way in range(4):
                outs[number * 4 + way][...] = packed[way]

        start += count


def pack_metric(place, owner, metric_rows):
    rows, size = metric_rows.shape
    total = sum(CHUNKS)
    block = rows // total
    half = block // 2
    whole = lambda g: (0, 0)
    out_shape = [
        jax.ShapeDtypeStruct((1, 4 * MOVE), I32),
        jax.ShapeDtypeStruct((1, size), I32),
    ]
    out_specs = [pl.BlockSpec((1, 4 * MOVE), whole), pl.BlockSpec((1, size), whole)]
    start = 0
    for count in CHUNKS:
        for way in range(4):
            out_shape.append(jax.ShapeDtypeStruct((count * half, LANES), F32))
            out_specs.append(
                pl.BlockSpec(
                    (half, LANES),
                    lambda g, start=start, count=count: (jnp.clip(g - start, 0, count - 1), 0),
                )
            )
        start += count
    return pl.pallas_call(
        pack_metric_kernel,
        grid=(total,),
        in_specs=[
            pl.BlockSpec(memory_space=pltpu.SMEM),
            pl.BlockSpec((1, size), whole),
            pl.BlockSpec((block, size), lambda g: (g, 0)),
        ],
        out_specs=out_specs,
        out_shape=out_shape,
        name="pack_metric",
        cost_estimate=pl.CostEstimate(flops=10**6, bytes_accessed=11 * 10**6, transcendentals=0),
        compiler_params=pltpu.CompilerParams(vmem_limit_bytes=24 << 20),
    )(place, owner, metric_rows)


def land(values, landing_row, pairs):
    rows, size = values.shape
    out = []
    for c in range(0, size, LANES):
        spot = jnp.broadcast_to(landing_row[:, c : c + LANES], (rows, LANES))
        got = gather_tiles(pairs, spot & (LANES - 1), spot >> 7)
        out.append(jnp.where(spot < 0, values[:, c : c + LANES], got))
    return jnp.concatenate(out, axis=1)


def land_kernel(landing, values, first, second, third, fourth, *rest):
    pairs = [unpack_pair(first[...], second[...]), unpack_pair(third[...], fourth[...])]
    rest[-1][...] = land(values[...], landing[...], pairs)


def land_rows(landing, values, arrived, block, start, count, before, name):
    rows, size = values.shape
    half = block // 2
    arrival = pl.BlockSpec((half, LANES), lambda g: (g, 0))
    in_specs = [
        pl.BlockSpec((1, size), lambda g: (0, 0)),
        pl.BlockSpec((block, size), lambda g: (g + start, 0)),
    ] + [arrival] * 4
    operands = [landing, values, *arrived]
    aliases = {}
    if before is not None:
        in_specs.append(pl.BlockSpec(memory_space=pl.ANY))
        operands.append(before)
        aliases = {6: 0}
    return pl.pallas_call(
        land_kernel,
        grid=(count,),
        in_specs=in_specs,
        out_specs=pl.BlockSpec((block, size), lambda g: (g + start, 0)),
        out_shape=jax.ShapeDtypeStruct((rows, size), F32),
        input_output_aliases=aliases,
        name=name,
        cost_estimate=pl.CostEstimate(
            flops=10**6, bytes_accessed=count * block * size * 10, transcendentals=0
        ),
        compiler_params=pltpu.CompilerParams(vmem_limit_bytes=24 << 20),
    )(*operands)


FACE_DOM = EY * EZ
FACE_SUB = EX * EZ
EDGE_DOM = EZ * (4 * EY - 1)
EDGE_SUB = EZ * (4 * EX - 1)
CORNER_DOM = EZ * (4 * EY - 2)
CORNER_SUB = EZ * (4 * EX - 2)


def up(count):
    return -(-count // LANES) * LANES


def table_starts(hosted):
    faces = (0, hosted[0], hosted[0] + up(FACE_DOM), hosted[0] + up(FACE_DOM) + up(FACE_SUB))
    edges = (0, hosted[1], hosted[1] + up(EDGE_DOM), hosted[1] + up(EDGE_DOM) + up(EDGE_SUB))
    corners = (
        0,
        hosted[2],
        hosted[2] + up(CORNER_DOM),
        hosted[2] + up(CORNER_DOM) + up(CORNER_SUB),
    )
    return (faces, edges, corners)


KINDS = (6, 12, 8)
FACE_ROWS = 2 * INNER * 8
EDGE_ROWS = 16
CORNER_ROWS = 4


def shared_columns(ids, place, hosted):
    lines, size = ids.shape
    line = iota((lines, 1), 0)
    per = jnp.where(line < 6, hosted[0], jnp.where(line < 18, hosted[1], hosted[2]))
    owns, rows, masks = [], jnp.zeros((lines, size), I32), []
    for device in (place[4], place[1], place[3], place[5]):
        local = ids - device * per
        inside = (local >= 0) & (local < per)
        rows = jnp.where(inside, local, rows)
        owns.append(inside)
    starts = table_starts(hosted)
    lower = (iota((lines, lines), 1) < iota((lines, lines), 0)) & (
        (iota((lines, lines), 0) < 6) == (iota((lines, lines), 1) < 6)
    )
    lower = lower & ((iota((lines, lines), 0) < 18) == (iota((lines, lines), 1) < 18))
    lower = jnp.where(lower, 1.0, 0.0).astype(BF16)
    column = rows
    marks = jnp.concatenate([jnp.where(inside, 1.0, 0.0) for inside in owns[1:]], axis=0)
    ranks = exclusive_count(marks)
    for number in range(3):
        inside = owns[1 + number]
        mark = marks[number * lines : (number + 1) * lines]
        above = jnp.sum(dot(lower, mark.astype(BF16)), axis=1, keepdims=True)
        rank = (ranks[number * lines : (number + 1) * lines] + above).astype(I32)
        base = jnp.where(
            line < 6,
            starts[0][1 + number],
            jnp.where(line < 18, starts[1][1 + number], starts[2][1 + number]),
        )
        column = jnp.where(inside, base + rank, column)
    return column, rows


def scatter_two(parts, column_row, tiles):
    high, low = split(parts)
    both = jnp.concatenate([high, low], axis=0)
    size = column_row.shape[1]
    tile = jnp.broadcast_to((column_row >> 7).astype(BF16), both.shape)
    zero = jnp.zeros(both.shape, BF16)
    left = jnp.concatenate([jnp.where(tile == h, both, zero) for h in range(tiles)], axis=0)
    return dot_nt(left, one_hot_rows(column_row & (LANES - 1), 0, LANES))


def face_rows(face, inner):
    end = 7 * (face % 2)
    if face < 2:
        return pl.ds(end * 64 + inner * 8, 8)
    if face < 4:
        return pl.ds(inner * 64 + end * 8, 8)
    return pl.ds(inner * 64 + end, 8, stride=8)


def all_lanes(ref, rows):
    return jnp.concatenate([ref[c, rows, :] for c in range(ref.shape[0])], axis=1)


def face_nodes(ref, face):
    return jnp.concatenate(
        [all_lanes(ref, face_rows(face, inner)) for inner in range(1, INNER + 1)], axis=0
    )


def edge_place(edge):
    ends = (7 * (edge % 4 // 2), 7 * (edge % 2))
    if edge < 4:
        return ends[0] * 8 + ends[1], 64
    if edge < 8:
        return ends[0] * 64 + ends[1], 8
    return ends[0] * 64 + ends[1] * 8, 1


def edge_rows(edge):
    start, stride = edge_place(edge)
    return pl.ds(start, 8) if stride == 1 else pl.ds(start, 8, stride=stride)


def corner_place(corner):
    return (corner // 4) * 448 + (corner // 2 % 2) * 56 + (corner % 2) * 7


def apply_kernel(
    place,
    ids,
    solution,
    metric,
    grad_left,
    image_left,
    square_left,
    after,
    image_ref,
    diagonal_ref,
    column_ref,
    face_table,
    edge_table,
    corner_table,
    dom_out,
    sub_out,
    both_out,
    flux_r,
    *,
    table,
):
    del after
    step = pl.program_id(0)
    width = solution.shape[1]
    size = image_ref.shape[0] * LANES
    tiles_here = width // LANES

    def write(ref, rows, values, add=False):
        for c in range(tiles_here):
            tile = step * tiles_here + c
            part = values[:, c * LANES : (c + 1) * LANES]
            ref[tile, rows, :] = ref[tile, rows, :] + part if add else part

    count = table.shape[0]
    plane = count * count

    field = [solution[i * plane : (i + 1) * plane, :] for i in range(count)]
    node = iota((count, width), 0)
    ends = (0, count - 1)
    end_value = {0: float(table[0, 0]), count - 1: float(table[count - 1, count - 1])}
    ends_k = jnp.where(
        node == 0, end_value[0], jnp.where(node == count - 1, end_value[count - 1], 0.0)
    )
    for i in range(count):
        rows = slice(i * plane, (i + 1) * plane)
        part = [metric[c * count * plane + i * plane : c * count * plane + (i + 1) * plane, :] for c in range(7)]
        grad_r = sum(float(table[i, s]) * field[s] for s in range(count))
        grads = dot(grad_left[...], triple(field[i]))
        grad_s, grad_t = grads[:plane], grads[plane:]
        flux_r[rows, :] = part[0] * grad_r + part[3] * grad_s + part[4] * grad_t
        flux_s = part[3] * grad_r + part[1] * grad_s + part[5] * grad_t
        flux_t = part[4] * grad_r + part[5] * grad_s + part[2] * grad_t
        image = dot(image_left[...], triple(jnp.concatenate([flux_s, flux_t], axis=0)))
        write(image_ref, rows, image + part[6] * field[i])
        diagonal = dot(square_left[...], triple(jnp.concatenate([part[1], part[2]], axis=0)))
        diagonal = diagonal + part[6]
        cross = []
        for j in range(count):
            lines = slice(j * count, (j + 1) * count)
            term = None
            if j in ends:
                term = part[5][lines] * (ends_k * (2.0 * end_value[j]))
            if i in ends:
                extra = part[4][lines] * (ends_k * (2.0 * end_value[i]))
                if j in ends:
                    extra = extra + part[3][lines] * (2.0 * end_value[i] * end_value[j])
                term = extra if term is None else term + extra
            cross.append(diagonal[lines] if term is None else diagonal[lines] + term)
        write(diagonal_ref, rows, jnp.concatenate(cross, axis=0))
    for i in range(count):
        rows = slice(i * plane, (i + 1) * plane)
        more = sum(float(table[a, i]) * flux_r[a * plane : (a + 1) * plane, :] for a in range(count))
        write(image_ref, rows, more, add=True)
        square = sum(
            float(table[a, i] * table[a, i]) * metric[a * plane : (a + 1) * plane, :]
            for a in range(count)
        )
        write(diagonal_ref, rows, square, add=True)

    @pl.when(step == pl.num_programs(0) - 1)
    def _():
        hosted = (3 * size, 3 * size, size)
        starts = table_starts(hosted)
        column, row = shared_columns(ids[...], place, hosted)
        column_ref[...] = column
        row_high = (row >> 4).astype(F32)
        row_low = (row & 15).astype(F32)
        face_parts = []
        spot = iota((48, size), 0)
        for face in range(6):
            values = face_nodes(image_ref, face)
            values = jnp.where(spot == 0, row_high[face : face + 1], values)
            values = jnp.where(spot == 7, row_low[face : face + 1], values)
            values = jnp.concatenate([values, face_nodes(diagonal_ref, face)], axis=0)
            face_parts.append(jnp.concatenate(split(values), axis=0))
        faces_end = starts[0][3]
        for base in range(0, faces_end, 2 * LANES):
            total = None
            for face in range(6):
                more = dot_nt(
                    face_parts[face], one_hot_rows(column[face : face + 1], base, 2 * LANES)
                )
                total = more if total is None else total + more
            total = total[:FACE_ROWS] + total[FACE_ROWS:]
            for side in range(2):
                tile = total[:, side * LANES : (side + 1) * LANES]
                place_column = base + side * LANES
                if place_column < starts[0][1]:
                    face_table[:, place_column : place_column + LANES] = tile
                elif place_column < starts[0][2]:
                    dom_out[0:FACE_ROWS, :] = tile
                else:
                    sub_out[0:FACE_ROWS, :] = tile
        tiles = (starts[1][3] + LANES) // LANES
        total = None
        line = iota((8, size), 0)
        for edge in range(12):
            values = all_lanes(image_ref, edge_rows(edge))
            values = jnp.where(line == 0, row_high[6 + edge : 7 + edge], values)
            values = jnp.where(line == 7, row_low[6 + edge : 7 + edge], values)
            values = jnp.concatenate([values, all_lanes(diagonal_ref, edge_rows(edge))], axis=0)
            more = scatter_two(values, column[6 + edge : 7 + edge], tiles)
            total = more if total is None else total + more
        for number in range(tiles):
            first = number * 2 * EDGE_ROWS
            tile = total[first : first + EDGE_ROWS] + total[first + EDGE_ROWS : first + 2 * EDGE_ROWS]
            place_column = number * LANES
            if place_column < starts[1][1]:
                edge_table[:, place_column : place_column + LANES] = tile
            elif place_column < starts[1][2]:
                base = FACE_ROWS + (place_column - starts[1][1]) // LANES * EDGE_ROWS
                dom_out[base : base + EDGE_ROWS, :] = tile
            elif place_column < starts[1][3]:
                base = FACE_ROWS + (place_column - starts[1][2]) // LANES * EDGE_ROWS
                sub_out[base : base + EDGE_ROWS, :] = tile
            else:
                both_out[0:EDGE_ROWS, :] = tile
        tiles = (starts[2][3] + LANES) // LANES
        total = None
        for corner in range(8):
            at = corner_place(corner)
            values = jnp.concatenate(
                [
                    all_lanes(image_ref, slice(at, at + 1)),
                    all_lanes(diagonal_ref, slice(at, at + 1)),
                    row_high[18 + corner : 19 + corner],
                    row_low[18 + corner : 19 + corner],
                    jnp.zeros((4, size), F32),
                ],
                axis=0,
            )
            more = scatter_two(values, column[18 + corner : 19 + corner], tiles)
            total = more if total is None else total + more
        for number in range(tiles):
            tile = total[number * 16 : number * 16 + 8] + total[number * 16 + 8 : number * 16 + 16]
            place_column = number * LANES
            if place_column < starts[2][1]:
                corner_table[:, place_column : place_column + LANES] = tile
            elif place_column < starts[2][2]:
                base = CORNER_BASE + (place_column - starts[2][1]) // LANES * CORNER_ROWS
                dom_out[base : base + CORNER_ROWS, :] = tile[:CORNER_ROWS]
            elif place_column < starts[2][3]:
                base = CORNER_BASE + (place_column - starts[2][2]) // LANES * CORNER_ROWS
                sub_out[base : base + CORNER_ROWS, :] = tile[:CORNER_ROWS]
            else:
                both_out[EDGE_ROWS : EDGE_ROWS + 8, :] = tile


EDGE_TILES = up(EDGE_DOM) // LANES
CORNER_TILES = up(CORNER_DOM) // LANES
CORNER_BASE = FACE_ROWS + EDGE_TILES * EDGE_ROWS
MESSAGE_ROWS = CORNER_BASE + CORNER_TILES * CORNER_ROWS
BOTH_ROWS = EDGE_ROWS + 8


def apply_and_pack(place, ids, field, metric_rows, after, table):
    nodes, size = field.shape
    width = size // 2
    count = table.shape[0]
    eye = np.eye(count, dtype=np.float32)
    grad = np.concatenate([np.kron(table, eye), np.kron(eye, table)], axis=0)
    square = (table * table).astype(np.float32)
    squares = np.concatenate([np.kron(square, eye), np.kron(eye, square)], axis=0)
    lefts = [split_np(grad), split_np(grad.T), split_np(squares.T)]
    whole = lambda g: (0, 0)

    def out(*shape, dtype=F32):
        return jax.ShapeDtypeStruct(shape, dtype), pl.BlockSpec(shape, lambda g: (0,) * len(shape))

    outs = [
        out(size // LANES, nodes, LANES),
        out(size // LANES, nodes, LANES),
        out(sum(KINDS), size, dtype=I32),
        out(FACE_ROWS, 3 * size),
        out(EDGE_ROWS, 3 * size),
        out(8, size),
        out(MESSAGE_ROWS, LANES),
        out(MESSAGE_ROWS, LANES),
        out(BOTH_ROWS, LANES),
    ]
    return pl.pallas_call(
        functools.partial(apply_kernel, table=table),
        grid=(size // width,),
        in_specs=[
            pl.BlockSpec(memory_space=pltpu.SMEM),
            pl.BlockSpec(ids.shape, whole),
            pl.BlockSpec((nodes, width), lambda g: (0, g)),
            pl.BlockSpec((metric_rows.shape[0], width), lambda g: (0, g)),
        ]
        + [pl.BlockSpec(left.shape, whole) for left in lefts]
        + [pl.BlockSpec(memory_space=pl.ANY)],
        out_specs=[spec for _, spec in outs],
        out_shape=[shape for shape, _ in outs],
        scratch_shapes=[pltpu.VMEM((nodes, width), F32)],
        name="apply_and_pack",
        cost_estimate=pl.CostEstimate(flops=10**9, bytes_accessed=12 * 10**6, transcendentals=0),
        compiler_params=pltpu.CompilerParams(vmem_limit_bytes=48 << 20),
    )(place, ids, field, metric_rows, *[jnp.asarray(left) for left in lefts], after)


def arrived_rows(high, low):
    return (high * 16.0 + low).astype(I32)


def add_kernel(face_in, edge_in, corner_in, dom, sub, both, faces, edges, corners, dom_back, sub_back, both_back):
    values = jnp.concatenate([dom[0:FACE_ROWS, :], sub[0:FACE_ROWS, :]], axis=1)
    row = arrived_rows(values[0:1], values[7:8])
    parts = jnp.concatenate(split(values), axis=0)
    for base in range(0, faces.shape[1], 2 * LANES):
        more = dot_nt(parts, one_hot_rows(row, base, 2 * LANES))
        faces[:, base : base + 2 * LANES] = (
            face_in[:, base : base + 2 * LANES] + more[:FACE_ROWS] + more[FACE_ROWS:]
        )
    tiles = [faces[:, c : c + LANES] for c in range(0, faces.shape[1], LANES)]
    for side, back in enumerate((dom_back, sub_back)):
        spot = jnp.broadcast_to(row[:, side * LANES : (side + 1) * LANES], (FACE_ROWS, LANES))
        back[0:FACE_ROWS, :] = gather_tiles(tiles, spot & (LANES - 1), spot >> 7)
    places = [(ref, FACE_ROWS + q * EDGE_ROWS) for ref in (dom, sub) for q in range(EDGE_TILES)]
    places.append((both, 0))
    values = jnp.concatenate([ref[at : at + EDGE_ROWS, :] for ref, at in places], axis=1)
    row = arrived_rows(values[0:1], values[7:8])
    count = edges.shape[1] // LANES
    total = scatter_two(values, row, count)
    tiles = []
    for number in range(count):
        first = number * 2 * EDGE_ROWS
        tile = total[first : first + EDGE_ROWS] + total[first + EDGE_ROWS : first + 2 * EDGE_ROWS]
        tile = tile + edge_in[:, number * LANES : (number + 1) * LANES]
        edges[:, number * LANES : (number + 1) * LANES] = tile
        tiles.append(tile)
    backs = {id(dom): dom_back, id(sub): sub_back, id(both): both_back}
    for number, (ref, at) in enumerate(places):
        spot = jnp.broadcast_to(
            row[:, number * LANES : (number + 1) * LANES], (EDGE_ROWS, LANES)
        )
        backs[id(ref)][at : at + EDGE_ROWS, :] = gather_tiles(tiles, spot & (LANES - 1), spot >> 7)
    places = [(ref, CORNER_BASE + q * CORNER_ROWS) for ref in (dom, sub) for q in range(CORNER_TILES)]
    places.append((both, EDGE_ROWS))
    values = jnp.concatenate([ref[at : at + CORNER_ROWS, :] for ref, at in places], axis=1)
    values = jnp.concatenate([values, jnp.zeros_like(values)], axis=0)
    row = arrived_rows(values[2:3], values[3:4])
    count = corners.shape[1] // LANES
    total = scatter_two(values, row, count)
    tiles = []
    for number in range(count):
        tile = total[number * 16 : number * 16 + 8] + total[number * 16 + 8 : number * 16 + 16]
        tile = tile + corner_in[:, number * LANES : (number + 1) * LANES]
        corners[:, number * LANES : (number + 1) * LANES] = tile
        tiles.append(tile)
    for number, (ref, at) in enumerate(places):
        spot = jnp.broadcast_to(row[:, number * LANES : (number + 1) * LANES], (8, LANES))
        got = gather_tiles(tiles, spot & (LANES - 1), spot >> 7)
        backs[id(ref)][at : at + CORNER_ROWS, :] = got[:CORNER_ROWS]


def add_and_read(faces, edges, corners, dom, sub, both):
    shapes = [faces, edges, corners, dom, sub, both]
    return pl.pallas_call(
        add_kernel,
        in_specs=[VMEM] * 6,
        out_specs=[VMEM] * 6,
        out_shape=[jax.ShapeDtypeStruct(a.shape, F32) for a in shapes],
        name="add_and_read",
        cost_estimate=pl.CostEstimate(flops=10**8, bytes_accessed=2 * 10**6, transcendentals=0),
        compiler_params=pltpu.CompilerParams(vmem_limit_bytes=24 << 20),
    )(*shapes)


def relax_kernel(
    column_ref, faces, edges, corners, dom, sub, both, image, diagonal, field, forcing, source,
    relaxed, *rest,
):
    size = relaxed.shape[1]
    *outs, full_image, full_diagonal = rest
    full_image[...] = image[...]
    full_diagonal[...] = diagonal[...]

    def spots(line, rows, c):
        spot = jnp.broadcast_to(column_ref[line : line + 1, c : c + LANES], (rows, LANES))
        return spot & (LANES - 1), spot >> 7

    def put(ref, c, rows, values):
        ref[c, rows, :] = jnp.where(inside, values, ref[c, rows, :])

    tiles = [faces[:, c : c + LANES] for c in range(0, faces.shape[1], LANES)]
    tiles += [dom[0:FACE_ROWS, :], sub[0:FACE_ROWS, :]]
    line = iota((8, LANES), 0)
    inside = (line > 0) & (line < 7)
    for c in range(0, size, LANES):
        for face in range(6):
            low, high = spots(face, FACE_ROWS, c)
            got = gather_tiles(tiles, low, high)
            for number in range(INNER):
                rows = face_rows(face, number + 1)
                put(full_image, c // LANES, rows, got[number * 8 : number * 8 + 8])
                put(full_diagonal, c // LANES, rows, got[48 + number * 8 : 56 + number * 8])
    tiles = [edges[:, c : c + LANES] for c in range(0, edges.shape[1], LANES)]
    for ref in (dom, sub):
        tiles += [
            ref[FACE_ROWS + q * EDGE_ROWS : FACE_ROWS + (q + 1) * EDGE_ROWS, :]
            for q in range(EDGE_TILES)
        ]
    tiles.append(both[0:EDGE_ROWS, :])
    for c in range(0, size, LANES):
        for edge in range(12):
            low, high = spots(6 + edge, EDGE_ROWS, c)
            got = gather_tiles(tiles, low, high)
            put(full_image, c // LANES, edge_rows(edge), got[:8])
            put(full_diagonal, c // LANES, edge_rows(edge), got[8:])
    tiles = [corners[0:8, c : c + LANES] for c in range(0, corners.shape[1], LANES)]
    for ref in (dom, sub):
        tiles += [
            ref[CORNER_BASE + q * CORNER_ROWS : CORNER_BASE + (q + 1) * CORNER_ROWS, :]
            for q in range(CORNER_TILES)
        ]
    tiles.append(both[EDGE_ROWS : EDGE_ROWS + 8, :])
    tiles = [jnp.concatenate([t[0:2]] * 4, axis=0) for t in tiles]
    for c in range(0, size, LANES):
        lanes = slice(c, c + LANES)
        for group in range(2):
            spot = jnp.concatenate(
                [
                    jnp.broadcast_to(column_ref[n : n + 1, lanes], (2, LANES))
                    for n in range(18 + group * 4, 22 + group * 4)
                ],
                axis=0,
            )
            got = gather_tiles(tiles, spot & (LANES - 1), spot >> 7)
            for number in range(4):
                at = corner_place(group * 4 + number)
                full_image[c // LANES, at : at + 1, :] = got[2 * number : 2 * number + 1]
                full_diagonal[c // LANES, at : at + 1, :] = got[2 * number + 1 : 2 * number + 2]
    for c in range(0, size, LANES):
        lanes = slice(c, c + LANES)
        step = (forcing[:, lanes] - full_image[c // LANES]) / full_diagonal[c // LANES]
        relaxed[:, lanes] = field[:, lanes] + RELAX * step
    for pair in range(2):
        picked = pick_columns(relaxed[...], source[:, pair * LANES : (pair + 1) * LANES])
        first, second = pack_pair(picked)
        outs[2 * pair][...] = first
        outs[2 * pair + 1][...] = second


def relax_and_pack(column, faces, edges, corners, dom, sub, both, image, diagonal, field, forcing, source):
    nodes, size = field.shape
    message = jax.ShapeDtypeStruct((nodes // 2, LANES), F32)
    return pl.pallas_call(
        relax_kernel,
        in_specs=[VMEM] * 12,
        out_specs=[VMEM] * 5,
        out_shape=[jax.ShapeDtypeStruct((nodes, size), F32)] + [message] * 4,
        scratch_shapes=[pltpu.VMEM((size // LANES, nodes, LANES), F32)] * 2,
        name="relax_and_pack",
        cost_estimate=pl.CostEstimate(flops=10**7, bytes_accessed=10**7, transcendentals=0),
        compiler_params=pltpu.CompilerParams(vmem_limit_bytes=32 << 20),
    )(column, faces, edges, corners, dom, sub, both, image, diagonal, field, forcing, source)


def shifted(value, dom_steps, sub_steps):
    dom_count = lax.axis_size("dom")
    sub_count = lax.axis_size("sub")
    if sub_steps == 0:
        pairs = [(d, (d + dom_steps) % dom_count) for d in range(dom_count)]
        return lax.ppermute(value, "dom", pairs)
    if dom_steps == 0:
        pairs = [(s, (s + sub_steps) % sub_count) for s in range(sub_count)]
        return lax.ppermute(value, "sub", pairs)
    pairs = [
        (
            d * sub_count + s,
            (d + dom_steps) % dom_count * sub_count + (s + sub_steps) % sub_count,
        )
        for d in range(dom_count)
        for s in range(sub_count)
    ]
    return lax.ppermute(value, ("dom", "sub"), pairs)


def exchanged(messages):
    to_prev_dom, to_next_dom, to_prev_sub, to_next_sub = messages
    from_prev_sub = shifted(to_next_sub, 0, 1)
    from_next_sub = shifted(to_prev_sub, 0, -1)
    from_prev_dom = shifted(to_next_dom, 1, 0)
    from_next_dom = shifted(to_prev_dom, -1, 0)
    return (from_prev_dom, from_next_dom, from_prev_sub, from_next_sub)


def on_device(solution, forcing, metric, entity_ids, new_owner):
    size = solution.shape[-1]
    place = devices()
    table = derivative_table(solution.shape[0] - 1)
    field = solution.reshape(-1, size)
    metric_rows = metric.reshape(-1, size)
    components = metric.shape[0]
    block = metric_rows.shape[0] // components
    source, landing, *messages = pack_metric(place, new_owner.reshape(1, size), metric_rows)
    arrived = [exchanged(messages[4 * n : 4 * n + 4]) for n in range(len(CHUNKS))]

    image, diagonal, column, faces, edges, corners, dom, sub, both = apply_and_pack(
        place, entity_ids, field, metric_rows, landing, table
    )
    both = shifted(both, 1, 1)
    sub = shifted(sub, 0, 1)
    dom = shifted(dom, 1, 0)
    faces, edges, corners, dom, sub, both = add_and_read(faces, edges, corners, dom, sub, both)
    both = shifted(both, -1, -1)
    sub = shifted(sub, 0, -1)
    dom = shifted(dom, -1, 0)
    relaxed, *leaving = relax_and_pack(
        column, faces, edges, corners, dom, sub, both, image, diagonal,
        field, forcing.reshape(-1, size), source,
    )
    got = exchanged(leaving)
    moved, start = None, 0
    for count, part in zip(CHUNKS, arrived):
        moved = land_rows(landing, metric_rows, part, block, start, count, moved, "land_metric")
        start += count
    smoothed = land_rows(landing, relaxed, got, block, 0, 1, None, "land_field")
    return smoothed.reshape(solution.shape), moved.reshape(metric.shape)


def solution(mesh):
    placed = (
        P(None, None, None, ("dom", "sub")),
        P(None, None, None, ("dom", "sub")),
        P(None, None, None, None, ("dom", "sub")),
        P(None, ("dom", "sub")),
        P(("dom", "sub")),
    )
    return jax.shard_map(
        on_device,
        mesh=mesh,
        in_specs=placed,
        out_specs=(P(None, None, None, ("dom", "sub")), P(None, None, None, None, ("dom", "sub"))),
        check_vma=False,
    )
```

time: 846 us -> 112 us (0.13)
  the two profiles are of different devices: /device:TPU:0 before, /device:TPU:28 now
where the time goes in v1:
time: 112 us
  waiting for transfers between devices  46.8 us (42%)
  Pallas kernels  40.5 us (36%)
  starting transfers between devices  20 us (18%)
  local copies, waits for them, and re-layouts  3.91 us (3%)
    ppermute x8, waiting for transfers between devices, shifted(): return lax.ppermute(value, 'sub', pairs)  32.6 us
    pallas_call x1, Pallas kernels, apply_and_pack(): pl.pallas_call(functools.partial(apply_kernel, table=table), grid=(size /...  14.6 us
    ppermute x2, waiting for transfers between devices, shifted(): return lax.ppermute(value, ('dom', 'sub'), pairs)  10.9 us
    pallas_call x3, Pallas kernels, land_rows(): pl.pallas_call(land_kernel, grid=(count,), in_specs=in_specs, out_specs=p...  9.46 us
    ppermute x8, starting transfers between devices, shifted(): return lax.ppermute(value, 'sub', pairs)  9.24 us
    ppermute x8, starting transfers between devices, shifted(): return lax.ppermute(value, 'dom', pairs)  8.3 us
    pallas_call x1, Pallas kernels, relax_and_pack(): pl.pallas_call(relax_kernel, in_specs=[VMEM] * 12, out_specs=[VMEM] * 5,...  7.96 us
    pallas_call x1, Pallas kernels, pack_metric(): pl.pallas_call(pack_metric_kernel, grid=(total,), in_specs=[pl.BlockSpec(...  7.04 us
  transfers between devices with their start and end apart: 18, of which 7 were waited for; matrix products, arithmetic and copies ran while one was open for 0% of the time, Pallas kernels for 14%

profile of v1, /device:TPU:28, one launch (start us, length us, event | category | flops | bytes accessed | tf_op | source)
XLA Modules:
  0.0 112.0 jit_solution(16499930820535594181)
XLA Ops:
  0.7 0.1 stack.27.place
  0.7 3.1 %copy-done = f32[7,8,8,8,512]{4,3,2,1,0:T(8,128)S(1)} copy-done((f32[7,8,8,8,512]{4,3,2,1,0:T(8,128)S(1)}, f32[7,8,8,8,512]{4,3,2,1,0:T(8,128)}, u32[]{:S(2)}) %copy-start) | copy-done | bytes 7340056
  3.8 0.7 copy-done.7
  4.6 7.0 %pack_metric.1 = (s32[1,256]{1,0:T(1,128)S(1)}, s32[1,512]{1,0:T(1,128)S(1)}, f32[1024,128]{1,0:T(8,128)S(1)}, f32[1024,128]{1,0:T(8,128)S(1)}, f32[1024,128]{1,...) custom-call(s32[6]{0:T(128)S(1)} %stack.27.place, ...), custom_call_target="tpu_custom_call" | custom-call | flops 1000000 | bytes 11000000 | tf_op jit(solution)/shard_map/pack_metric/pallas_call | solution.py:241
  11.7 14.6 %apply_and_pack.1 = (f32[4,512,128]{2,1,0:T(8,128)S(1)}, f32[4,512,128]{2,1,0:T(8,128)S(1)}, s32[26,512]{1,0:T(8,128)S(1)}, f32[96,1536]{1,0:T(8,128)S(1)}, f32[...) custom-call(s32[6]{0:T(128)S(1)} %stack.27.place, ...), custom_call_target="tpu_custom_call" | custom-call | flops 1000000000 | bytes 12000000 | tf_op jit(solution)/shard_map/apply_and_pack/pallas_call | solution.py:612
  26.3 0.1 collective-permute-start
  26.4 0.3 collective-permute-start.1
  26.6 2.4 %collective-permute-start.2 = (f32[24,128]{1,0:T(8,128)S(1)}, f32[24,128]{1,0:T(8,128)S(1)}, u32[]{:S(2)}, u32[]{:S(2)}) collective-permute-start(f32[24,128]{1,0:T(8,128)S(1)} %get-tuple-element.39), channel_id=1, source_target_pairs={{0,5},{1,6},{2,7},{3,4},{4,9},{5,10},{6,11},{7,8},{8,13},{9,14},{1... | collective-permute-start | bytes 36872 | tf_op jit(solution)/shard_map/ppermute | solution.py:807
  29.1 0.2 collective-permute-start.14
  29.3 2.5 %collective-permute-start.15 = (f32[1024,128]{1,0:T(8,128)S(1)}, f32[1024,128]{1,0:T(8,128)S(1)}, u32[]{:S(2)}, u32[]{:S(2)}) collective-permute-start(f32[1024,128]{1,0:T(8,128)S(1)} %get-tuple-element.59), channel_id=1, source_target_pairs={{0,28},{4,0},{8,4},{12,8},{16,12},{20,16},{24,20},{28,24},{1,29},{... | collective-permute-start | bytes 1572872 | tf_op jit(solution)/shard_map/ppermute | solution.py:795
  31.7 1.3 %collective-permute-done.2.both = f32[24,128]{1,0:T(8,128)S(1)} collective-permute-done((f32[24,128]{1,0:T(8,128)S(1)}, f32[24,128]{1,0:T(8,128)S(1)}, u32[]{:S(2)}, u32[]{:S(2)}) %collective-permute-start.2) | collective-permute-done | bytes 12320 | tf_op jit(solution)/shard_map/ppermute | solution.py:807
  33.0 2.0 %collective-permute-start.16 = (f32[1024,128]{1,0:T(8,128)S(1)}, f32[1024,128]{1,0:T(8,128)S(1)}, u32[]{:S(2)}, u32[]{:S(2)}) collective-permute-start(f32[1024,128]{1,0:T(8,128)S(1)} %get-tuple-element.60), channel_id=1, source_target_pairs={{0,1},{1,2},{2,3},{3,0},{4,5},{5,6},{6,7},{7,4},{8,9},{9,10},{10,1... | collective-permute-start | bytes 1572872 | tf_op jit(solution)/shard_map/ppermute | solution.py:798
  35.0 1.4 %add_and_read.1 = (f32[96,1536]{1,0:T(8,128)S(1)}, f32[16,1536]{1,0:T(8,128)S(1)}, f32[8,512]{1,0:T(8,128)S(1)}, f32[176,128]{1,0:T(8,128)S(1)}, f32[176,128]{1,0:T(8,128)S(1)}, /*index=5*/f32[24,128]{1,0:T(8,128)S(1)}) custom-call(f32[96,1536]{1,0:T(8,128)S(1)} %get-tuple-element.34.face_in, f32[16,1536]{1,0:T(8,128)S(1)} %get-tuple-element.35.edge_in, ...), custom_call_target="tpu_custom_call" | custom-call | flops 100000000 | bytes 2000000 | tf_op jit(solution)/shard_map/add_and_read/pallas_call | solution.py:689
  36.5 0.1 collective-permute-start.5
  36.5 0.3 collective-permute-start.3
  36.8 9.5 %collective-permute-done.5.both = f32[24,128]{1,0:T(8,128)S(1)} collective-permute-done((f32[24,128]{1,0:T(8,128)S(1)}, f32[24,128]{1,0:T(8,128)S(1)}, u32[]{:S(2)}, u32[]{:S(2)}) %collective-permute-start.5) | collective-permute-done | bytes 12320 | tf_op jit(solution)/shard_map/ppermute | solution.py:807
  46.3 1.1 %collective-permute-start.4 = (f32[176,128]{1,0:T(8,128)S(1)}, f32[176,128]{1,0:T(8,128)S(1)}, u32[]{:S(2)}, u32[]{:S(2)}) collective-permute-start(f32[176,128]{1,0:T(8,128)S(1)} %get-tuple-element.44), channel_id=1, source_target_pairs={{0,3},{1,0},{2,1},{3,2},{4,7},{5,4},{6,5},{7,6},{8,11},{9,8},{10,9... | collective-permute-start | bytes 270344 | tf_op jit(solution)/shard_map/ppermute | solution.py:798
  47.5 5.9 %collective-permute-done.4.sub = f32[176,128]{1,0:T(8,128)S(1)} collective-permute-done((f32[176,128]{1,0:T(8,128)S(1)}, f32[176,128]{1,0:T(8,128)S(1)}, u32[]{:S(2)}, u32[]{:S(2)}) %collective-permute-start.4) | collective-permute-done | bytes 90144 | tf_op jit(solution)/shard_map/ppermute | solution.py:798
  53.4 8.0 %relax_and_pack.1 = (f32[512,512]{1,0:T(8,128)S(1)}, f32[256,128]{1,0:T(8,128)S(1)}, f32[256,128]{1,0:T(8,128)S(1)}, f32[256,128]{1,0:T(8,128)S(1)}, f32[256,128]{1,0:T(8,128)S(1)}) custom-call(s32[26,512]{1,0:T(8,128)S(1)} %get-tuple-element.33.column_ref, f32[96,1536]{1,0:T(8,128)S(1)} %get-tuple-element.40.faces, f32[16,1536]{1,0:T(8,128)S(1)} %get-tuple-element.41.edges, ...), custom_call_target="tpu_custom_call" | custom-call | flops 10000000 | bytes 10000000 | tf_op jit(solution)/shard_map/relax_and_pack/pallas_call | solution.py:778
  61.4 0.1 collective-permute-start.6
  61.4 2.6 %collective-permute-start.7 = (f32[256,128]{1,0:T(8,128)S(1)}, f32[256,128]{1,0:T(8,128)S(1)}, u32[]{:S(2)}, u32[]{:S(2)}) collective-permute-start(f32[256,128]{1,0:T(8,128)S(1)} %get-tuple-element.51), channel_id=1, source_target_pairs={{0,28},{4,0},{8,4},{12,8},{16,12},{20,16},{24,20},{28,24},{1,29},{... | collective-permute-start | bytes 393224 | tf_op jit(solution)/shard_map/ppermute | solution.py:795
  64.1 3.3 %collective-permute-done.6.first = f32[256,128]{1,0:T(8,128)S(1)} collective-permute-done((f32[256,128]{1,0:T(8,128)S(1)}, f32[256,128]{1,0:T(8,128)S(1)}, u32[]{:S(2)}, u32[]{:S(2)}) %collective-permute-start.6) | collective-permute-done | bytes 131104 | tf_op jit(solution)/shard_map/ppermute | solution.py:795
  67.4 1.5 %collective-permute-start.8 = (f32[256,128]{1,0:T(8,128)S(1)}, f32[256,128]{1,0:T(8,128)S(1)}, u32[]{:S(2)}, u32[]{:S(2)}) collective-permute-start(f32[256,128]{1,0:T(8,128)S(1)} %get-tuple-element.52), channel_id=1, source_target_pairs={{0,1},{1,2},{2,3},{3,0},{4,5},{5,6},{6,7},{7,4},{8,9},{9,10},{10,1... | collective-permute-start | bytes 393224 | tf_op jit(solution)/shard_map/ppermute | solution.py:798
  68.8 0.6 collective-permute-start.9
  69.4 11.4 %collective-permute-done.8.third = f32[256,128]{1,0:T(8,128)S(1)} collective-permute-done((f32[256,128]{1,0:T(8,128)S(1)}, f32[256,128]{1,0:T(8,128)S(1)}, u32[]{:S(2)}, u32[]{:S(2)}) %collective-permute-start.8) | collective-permute-done | bytes 131104 | tf_op jit(solution)/shard_map/ppermute | solution.py:798
  80.8 2.6 %collective-permute-start.11 = (f32[768,128]{1,0:T(8,128)S(1)}, f32[768,128]{1,0:T(8,128)S(1)}, u32[]{:S(2)}, u32[]{:S(2)}) collective-permute-start(f32[768,128]{1,0:T(8,128)S(1)} %get-tuple-element.55), channel_id=1, source_target_pairs={{0,28},{4,0},{8,4},{12,8},{16,12},{20,16},{24,20},{28,24},{1,29},{... | collective-permute-start | bytes 1179656 | tf_op jit(solution)/shard_map/ppermute | solution.py:795
  83.4 3.8 %collective-permute-start.12 = (f32[768,128]{1,0:T(8,128)S(1)}, f32[768,128]{1,0:T(8,128)S(1)}, u32[]{:S(2)}, u32[]{:S(2)}) collective-permute-start(f32[768,128]{1,0:T(8,128)S(1)} %get-tuple-element.56), channel_id=1, source_target_pairs={{0,1},{1,2},{2,3},{3,0},{4,5},{5,6},{6,7},{7,4},{8,9},{9,10},{10,1... | collective-permute-start | bytes 1179656 | tf_op jit(solution)/shard_map/ppermute | solution.py:798
  87.3 1.7 %land_field.1 = f32[512,512]{1,0:T(8,128)} custom-call(s32[1,512]{1,0:T(1,128)S(1)} %get-tuple-element.32.after.landing, f32[512,512]{1,0:T(8,128)S(1)} %get-tuple-element.49.values, f32[256,128]{1,0:T(8,128)S(1)} %collective-permute-done.6.first, f32[256,128]{1,0:T(8,128)S(1)} %collective-permute-done.7.second, ...), custom_call_target="tpu_custom_call" | custom-call | flops 1000000 | bytes 2621440 | tf_op jit(solution)/shard_map/land_field/pallas_call | solution.py:286
  89.0 8.5 %collective-permute-done.17.fourth = f32[1024,128]{1,0:T(8,128)S(1)} collective-permute-done((f32[1024,128]{1,0:T(8,128)S(1)}, f32[1024,128]{1,0:T(8,128)S(1)}, u32[]{:S(2)}, u32[]{:S(2)}) %collective-permute-start.17) | collective-permute-done | bytes 524320 | tf_op jit(solution)/shard_map/ppermute | solution.py:798
  97.5 4.3 %land_metric.2.rest_0_ = f32[3584,512]{1,0:T(8,128)} custom-call(s32[1,512]{1,0:T(1,128)S(1)} %get-tuple-element.32.after.landing, f32[3584,512]{1,0:T(8,128)S(1)} %bitcast.16, f32[1024,128]{1,0:T(8,128)S(1)} %collective-permute-done.14.first, f32[1024,128]{1,0:T(8,128)S(1)} %collective-permute-done.15.second, ...), custom_call_target="tpu_custom_call" | custom-call | flops 1000000 | bytes 10485760 | tf_op jit(solution)/shard_map/land_metric/pallas_call | solution.py:286
  101.8 6.7 %collective-permute-done.13.fourth = f32[768,128]{1,0:T(8,128)S(1)} collective-permute-done((f32[768,128]{1,0:T(8,128)S(1)}, f32[768,128]{1,0:T(8,128)S(1)}, u32[]{:S(2)}, u32[]{:S(2)}) %collective-permute-start.13) | collective-permute-done | bytes 393248 | tf_op jit(solution)/shard_map/ppermute | solution.py:798
  108.5 3.5 %land_metric.3 = f32[3584,512]{1,0:T(8,128)} custom-call(s32[1,512]{1,0:T(1,128)S(1)} %get-tuple-element.32.after.landing, f32[3584,512]{1,0:T(8,128)S(1)} %bitcast.17, f32[768,128]{1,0:T(8,128)S(1)} %collective-permute-done.10.first, f32[768,128]{1,0:T(8,128)S(1)} %collective-permute-done.11.second, ...), custom_call_target="tpu_custom_call", output_to_operand_aliasing={{}: (6, {})} | custom-call | flops 1000000 | bytes 7864320 | tf_op jit(solution)/shard_map/land_metric/pallas_call | solution.py:286
  (33 shorter events, 0.1 us)
Async XLA Ops:
  0.6 11.0 %copy-start.3 = (s32[26,512]{1,0:T(8,128)S(1)}, s32[26,512]{1,0:T(8,128)}, u32[]{:S(2)}) copy-start(s32[26,512]{1,0:T(8,128)} %ids.1) | copy-start | bytes 159748
  0.7 3.1 %copy-start = (f32[7,8,8,8,512]{4,3,2,1,0:T(8,128)S(1)}, f32[7,8,8,8,512]{4,3,2,1,0:T(8,128)}, u32[]{:S(2)}) copy-start(f32[7,8,8,8,512]{4,3,2,1,0:T(8,128)} %param.10) | copy-start | bytes 22020100
  3.8 0.7 copy-start.7
  4.5 7.1 %copy-start.1 = (f32[8,8,8,512]{3,2,1,0:T(8,128)S(1)}, f32[8,8,8,512]{3,2,1,0:T(8,128)}, u32[]{:S(2)}) copy-start(f32[8,8,8,512]{3,2,1,0:T(8,128)} %param.8) | copy-start | bytes 3145732
  4.5 7.1 %copy-start.4 = (bf16[128,192]{1,0:T(8,128)(2,1)S(1)}, bf16[128,192]{1,0:T(8,128)(2,1)}, u32[]{:S(2)}) copy-start(bf16[128,192]{1,0:T(8,128)(2,1)} %constant.35.clone.grad_left) | copy-start | bytes 147460
  4.5 7.1 %copy-start.5 = (bf16[64,384]{1,0:T(8,128)(2,1)S(1)}, bf16[64,384]{1,0:T(8,128)(2,1)}, u32[]{:S(2)}) copy-start(bf16[64,384]{1,0:T(8,128)(2,1)} %constant.36.clone.image_left) | copy-start | bytes 147460
  4.5 7.1 %copy-start.6 = (bf16[64,384]{1,0:T(8,128)(2,1)S(1)}, bf16[64,384]{1,0:T(8,128)(2,1)}, u32[]{:S(2)}) copy-start(bf16[64,384]{1,0:T(8,128)(2,1)} %constant.37.clone.square_left) | copy-start | bytes 147460
  4.5 48.8 %copy-start.2 = (f32[8,8,8,512]{3,2,1,0:T(8,128)S(1)}, f32[8,8,8,512]{3,2,1,0:T(8,128)}, u32[]{:S(2)}) copy-start(f32[8,8,8,512]{3,2,1,0:T(8,128)} %param.9) | copy-start | bytes 3145732
  11.7 85.9 %slice-start = ((s8[7340032]{0:T(1024)(128)(4,1)}), s8[3145728]{0:T(1024)(128)(4,1)S(1)}, s32[]{:S(2)}) async-start(s8[7340032]{0:T(1024)(128)(4,1)} %bitcast.14), calls=%async_computation | async-start | bytes 6291456
  26.3 8.7 %collective-permute-start = (f32[176,128]{1,0:T(8,128)S(1)}, f32[176,128]{1,0:T(8,128)S(1)}, u32[]{:S(2)}, u32[]{:S(2)}) collective-permute-start(f32[176,128]{1,0:T(8,128)S(1)} %get-tuple-element.37), channel_id=1, source_target_pairs={{0,4},{4,8},{8,12},{12,16},{16,20},{20,24},{24,28},{28,0},{1,5},{5... | collective-permute-start | bytes 270344 | tf_op jit(solution)/shard_map/ppermute | solution.py:795
  26.4 8.7 %collective-permute-start.1 = (f32[176,128]{1,0:T(8,128)S(1)}, f32[176,128]{1,0:T(8,128)S(1)}, u32[]{:S(2)}, u32[]{:S(2)}) collective-permute-start(f32[176,128]{1,0:T(8,128)S(1)} %get-tuple-element.38), channel_id=1, source_target_pairs={{0,1},{1,2},{2,3},{3,0},{4,5},{5,6},{6,7},{7,4},{8,9},{9,10},{10,1... | collective-permute-start | bytes 270344 | tf_op jit(solution)/shard_map/ppermute | solution.py:798
  26.6 6.4 %collective-permute-start.2 = (f32[24,128]{1,0:T(8,128)S(1)}, f32[24,128]{1,0:T(8,128)S(1)}, u32[]{:S(2)}, u32[]{:S(2)}) collective-permute-start(f32[24,128]{1,0:T(8,128)S(1)} %get-tuple-element.39), channel_id=1, source_target_pairs={{0,5},{1,6},{2,7},{3,4},{4,9},{5,10},{6,11},{7,8},{8,13},{9,14},{1... | collective-permute-start | bytes 36872 | tf_op jit(solution)/shard_map/ppermute | solution.py:807
  29.1 51.7 %collective-permute-start.14 = (f32[1024,128]{1,0:T(8,128)S(1)}, f32[1024,128]{1,0:T(8,128)S(1)}, u32[]{:S(2)}, u32[]{:S(2)}) collective-permute-start(f32[1024,128]{1,0:T(8,128)S(1)} %get-tuple-element.58), channel_id=1, source_target_pairs={{0,4},{4,8},{8,12},{12,16},{16,20},{20,24},{24,28},{28,0},{1,5},{5... | collective-permute-start | bytes 1572872 | tf_op jit(solution)/shard_map/ppermute | solution.py:795
  29.3 54.2 %collective-permute-start.15 = (f32[1024,128]{1,0:T(8,128)S(1)}, f32[1024,128]{1,0:T(8,128)S(1)}, u32[]{:S(2)}, u32[]{:S(2)}) collective-permute-start(f32[1024,128]{1,0:T(8,128)S(1)} %get-tuple-element.59), channel_id=1, source_target_pairs={{0,28},{4,0},{8,4},{12,8},{16,12},{20,16},{24,20},{28,24},{1,29},{... | collective-permute-start | bytes 1572872 | tf_op jit(solution)/shard_map/ppermute | solution.py:795
  33.0 54.2 %collective-permute-start.16 = (f32[1024,128]{1,0:T(8,128)S(1)}, f32[1024,128]{1,0:T(8,128)S(1)}, u32[]{:S(2)}, u32[]{:S(2)}) collective-permute-start(f32[1024,128]{1,0:T(8,128)S(1)} %get-tuple-element.60), channel_id=1, source_target_pairs={{0,1},{1,2},{2,3},{3,0},{4,5},{5,6},{6,7},{7,4},{8,9},{9,10},{10,1... | collective-permute-start | bytes 1572872 | tf_op jit(solution)/shard_map/ppermute | solution.py:798
  35.0 62.5 %slice-start.1 = ((s8[7340032]{0:T(1024)(128)(4,1)}), s8[4194304]{0:T(1024)(128)(4,1)S(1)}, s32[]{:S(2)}) async-start(s8[7340032]{0:T(1024)(128)(4,1)} %bitcast.14), calls=%async_computation.1 | async-start | bytes 8388608
  36.5 9.9 %collective-permute-start.5 = (f32[24,128]{1,0:T(8,128)S(1)}, f32[24,128]{1,0:T(8,128)S(1)}, u32[]{:S(2)}, u32[]{:S(2)}) collective-permute-start(f32[24,128]{1,0:T(8,128)S(1)} %get-tuple-element.45), channel_id=1, source_target_pairs={{0,31},{1,28},{2,29},{3,30},{4,3},{5,0},{6,1},{7,2},{8,7},{9,4},{1... | collective-permute-start | bytes 36872 | tf_op jit(solution)/shard_map/ppermute | solution.py:807
  36.5 10.9 %collective-permute-start.3 = (f32[176,128]{1,0:T(8,128)S(1)}, f32[176,128]{1,0:T(8,128)S(1)}, u32[]{:S(2)}, u32[]{:S(2)}) collective-permute-start(f32[176,128]{1,0:T(8,128)S(1)} %get-tuple-element.43), channel_id=1, source_target_pairs={{0,28},{4,0},{8,4},{12,8},{16,12},{20,16},{24,20},{28,24},{1,29},{... | collective-permute-start | bytes 270344 | tf_op jit(solution)/shard_map/ppermute | solution.py:795
  46.3 7.0 %collective-permute-start.4 = (f32[176,128]{1,0:T(8,128)S(1)}, f32[176,128]{1,0:T(8,128)S(1)}, u32[]{:S(2)}, u32[]{:S(2)}) collective-permute-start(f32[176,128]{1,0:T(8,128)S(1)} %get-tuple-element.44), channel_id=1, source_target_pairs={{0,3},{1,0},{2,1},{3,2},{4,7},{5,4},{6,5},{7,6},{8,11},{9,8},{10,9... | collective-permute-start | bytes 270344 | tf_op jit(solution)/shard_map/ppermute | solution.py:798
  61.4 6.0 %collective-permute-start.6 = (f32[256,128]{1,0:T(8,128)S(1)}, f32[256,128]{1,0:T(8,128)S(1)}, u32[]{:S(2)}, u32[]{:S(2)}) collective-permute-start(f32[256,128]{1,0:T(8,128)S(1)} %get-tuple-element.50), channel_id=1, source_target_pairs={{0,4},{4,8},{8,12},{12,16},{16,20},{20,24},{24,28},{28,0},{1,5},{5... | collective-permute-start | bytes 393224 | tf_op jit(solution)/shard_map/ppermute | solution.py:795
  61.4 7.4 %collective-permute-start.7 = (f32[256,128]{1,0:T(8,128)S(1)}, f32[256,128]{1,0:T(8,128)S(1)}, u32[]{:S(2)}, u32[]{:S(2)}) collective-permute-start(f32[256,128]{1,0:T(8,128)S(1)} %get-tuple-element.51), channel_id=1, source_target_pairs={{0,28},{4,0},{8,4},{12,8},{16,12},{20,16},{24,20},{28,24},{1,29},{... | collective-permute-start | bytes 393224 | tf_op jit(solution)/shard_map/ppermute | solution.py:795
  67.4 13.4 %collective-permute-start.8 = (f32[256,128]{1,0:T(8,128)S(1)}, f32[256,128]{1,0:T(8,128)S(1)}, u32[]{:S(2)}, u32[]{:S(2)}) collective-permute-start(f32[256,128]{1,0:T(8,128)S(1)} %get-tuple-element.52), channel_id=1, source_target_pairs={{0,1},{1,2},{2,3},{3,0},{4,5},{5,6},{6,7},{7,4},{8,9},{9,10},{10,1... | collective-permute-start | bytes 393224 | tf_op jit(solution)/shard_map/ppermute | solution.py:798
  68.8 11.9 %collective-permute-start.9 = (f32[256,128]{1,0:T(8,128)S(1)}, f32[256,128]{1,0:T(8,128)S(1)}, u32[]{:S(2)}, u32[]{:S(2)}) collective-permute-start(f32[256,128]{1,0:T(8,128)S(1)} %get-tuple-element.53), channel_id=1, source_target_pairs={{0,3},{1,0},{2,1},{3,2},{4,7},{5,4},{6,5},{7,6},{8,11},{9,8},{10,9... | collective-permute-start | bytes 393224 | tf_op jit(solution)/shard_map/ppermute | solution.py:798
  80.8 16.7 %collective-permute-start.17 = (f32[1024,128]{1,0:T(8,128)S(1)}, f32[1024,128]{1,0:T(8,128)S(1)}, u32[]{:S(2)}, u32[]{:S(2)}) collective-permute-start(f32[1024,128]{1,0:T(8,128)S(1)} %get-tuple-element.61), channel_id=1, source_target_pairs={{0,3},{1,0},{2,1},{3,2},{4,7},{5,4},{6,5},{7,6},{8,11},{9,8},{10,9... | collective-permute-start | bytes 1572872 | tf_op jit(solution)/shard_map/ppermute | solution.py:798
  80.8 21.0 %collective-permute-start.10 = (f32[768,128]{1,0:T(8,128)S(1)}, f32[768,128]{1,0:T(8,128)S(1)}, u32[]{:S(2)}, u32[]{:S(2)}) collective-permute-start(f32[768,128]{1,0:T(8,128)S(1)} %get-tuple-element.54), channel_id=1, source_target_pairs={{0,4},{4,8},{8,12},{12,16},{16,20},{20,24},{24,28},{28,0},{1,5},{5... | collective-permute-start | bytes 1179656 | tf_op jit(solution)/shard_map/ppermute | solution.py:795
  80.8 21.0 %collective-permute-start.11 = (f32[768,128]{1,0:T(8,128)S(1)}, f32[768,128]{1,0:T(8,128)S(1)}, u32[]{:S(2)}, u32[]{:S(2)}) collective-permute-start(f32[768,128]{1,0:T(8,128)S(1)} %get-tuple-element.55), channel_id=1, source_target_pairs={{0,28},{4,0},{8,4},{12,8},{16,12},{20,16},{24,20},{28,24},{1,29},{... | collective-permute-start | bytes 1179656 | tf_op jit(solution)/shard_map/ppermute | solution.py:795
  83.4 18.4 %collective-permute-start.12 = (f32[768,128]{1,0:T(8,128)S(1)}, f32[768,128]{1,0:T(8,128)S(1)}, u32[]{:S(2)}, u32[]{:S(2)}) collective-permute-start(f32[768,128]{1,0:T(8,128)S(1)} %get-tuple-element.56), channel_id=1, source_target_pairs={{0,1},{1,2},{2,3},{3,0},{4,5},{5,6},{6,7},{7,4},{8,9},{9,10},{10,1... | collective-permute-start | bytes 1179656 | tf_op jit(solution)/shard_map/ppermute | solution.py:798
  87.3 21.3 %collective-permute-start.13 = (f32[768,128]{1,0:T(8,128)S(1)}, f32[768,128]{1,0:T(8,128)S(1)}, u32[]{:S(2)}, u32[]{:S(2)}) collective-permute-start(f32[768,128]{1,0:T(8,128)S(1)} %get-tuple-element.57), channel_id=1, source_target_pairs={{0,3},{1,0},{2,1},{3,2},{4,7},{5,4},{6,5},{7,6},{8,11},{9,8},{10,9... | collective-permute-start | bytes 1179656 | tf_op jit(solution)/shard_map/ppermute | solution.py:798

commit v2 on v1

v2 whole, which is shorter than its diff:
```python
import functools

import jax
import jax.numpy as jnp
import numpy as np
from jax import lax
from jax.experimental import pallas as pl
from jax.experimental.pallas import tpu as pltpu
from jax.sharding import PartitionSpec as P

EX = 4
EY = 4
EZ = 32
MOVE = 64
RELAX = 0.6
LANES = 128
INNER = 6
EARLY = 4

NT = (((1,), (1,)), ((), ()))
VMEM = pl.BlockSpec(memory_space=pltpu.VMEM)
ANY = pl.BlockSpec(memory_space=pl.ANY)
SMEM = pl.BlockSpec(memory_space=pltpu.SMEM)
QUICK = pl.CostEstimate(flops=1000, bytes_accessed=1000, transcendentals=0)
HBM = pl.BlockSpec(memory_space=pltpu.HBM)
LARGE = pltpu.CompilerParams(vmem_limit_bytes=24 << 20)
SMALL = pltpu.CompilerParams(vmem_limit_bytes=16 << 20)
STRIP = 64
F32 = jnp.float32
BF16 = jnp.bfloat16
I32 = jnp.int32


def derivative_table(order):
    count = order + 1
    points = -np.cos(np.pi * np.arange(count) / order)
    legendre = np.zeros((count, count))
    for sweep in range(80):
        legendre[:, 0] = 1.0
        legendre[:, 1] = points
        for degree in range(2, count):
            legendre[:, degree] = (
                (2 * degree - 1) * points * legendre[:, degree - 1]
                - (degree - 1) * legendre[:, degree - 2]
            ) / degree
        points = points - (points * legendre[:, order] - legendre[:, order - 1]) / (
            count * legendre[:, order]
        )
    legendre[:, 0] = 1.0
    legendre[:, 1] = points
    for degree in range(2, count):
        legendre[:, degree] = (
            (2 * degree - 1) * points * legendre[:, degree - 1]
            - (degree - 1) * legendre[:, degree - 2]
        ) / degree
    values = legendre[:, order]
    identity = np.eye(count)
    spread = points[:, None] - points[None, :] + identity
    table = values[:, None] / values[None, :] / spread
    table = table * (1.0 - identity)
    table[0, 0] = -order * count / 4.0
    table[order, order] = order * count / 4.0
    return table.astype(np.float32)


def split_np(matrix):
    high = matrix.astype(jnp.bfloat16).astype(np.float32)
    low = (matrix - high).astype(jnp.bfloat16)
    return np.concatenate([high.astype(jnp.bfloat16), low, high.astype(jnp.bfloat16)], axis=1)


def split(values):
    high = values.astype(BF16)
    low = (values - high.astype(F32)).astype(BF16)
    return high, low


def triple(values):
    high, low = split(values)
    return jnp.concatenate([high, high, low], axis=0)


def dot(left, right):
    return jnp.dot(left, right, preferred_element_type=F32)


def dot_nt(left, right):
    return lax.dot_general(left, right, NT, preferred_element_type=F32)


def iota(shape, dim):
    return lax.broadcasted_iota(I32, shape, dim)


def one_hot_rows(index_row, start, count):
    size = index_row.shape[1]
    out = []
    for base in range(0, count, LANES):
        local = (index_row - (start + base)).astype(BF16)
        rows = iota((LANES, size), 0).astype(BF16)
        out.append(
            jnp.where(rows == local, jnp.ones((LANES, size), BF16), jnp.zeros((LANES, size), BF16))
        )
    return out[0] if len(out) == 1 else jnp.concatenate(out, axis=0)


def exclusive_count(masks):
    size = masks.shape[1]
    upper = jnp.where(iota((size, size), 0) < iota((size, size), 1), 1.0, 0.0).astype(BF16)
    return dot(masks.astype(BF16), upper)


def gather_tiles(tiles, low, high):
    out = None
    for number, tile in enumerate(tiles):
        got = jnp.take_along_axis(tile, low, axis=1)
        out = got if out is None else jnp.where(high == number, got, out)
    return out


def devices():
    dom_count = lax.axis_size("dom")
    sub_count = lax.axis_size("sub")
    dom = lax.axis_index("dom")
    sub = lax.axis_index("sub")
    dom_ahead = lax.rem(dom + 1, dom_count)
    dom_behind = lax.rem(dom + dom_count - 1, dom_count)
    sub_ahead = lax.rem(sub + 1, sub_count)
    sub_behind = lax.rem(sub + sub_count - 1, sub_count)
    return jnp.stack(
        [
            dom_behind * sub_count + sub,
            dom_ahead * sub_count + sub,
            dom * sub_count + sub_behind,
            dom * sub_count + sub_ahead,
            dom * sub_count + sub,
            dom_ahead * sub_count + sub_ahead,
        ]
    ).astype(I32)


def pack_pair(top, bottom):
    left = iota(top.shape, 1) < MOVE
    first = jnp.where(left, top, pltpu.roll(bottom, MOVE, 1))
    second = jnp.where(left, pltpu.roll(top, MOVE, 1), bottom)
    return first, second


def pick_columns(ref, rows, low, high):
    tiles = [ref[rows, c : c + LANES] for c in range(0, ref.shape[1], LANES)]
    return gather_tiles(tiles, low, high)


def pack_block(ref, start, block, source_row, outs, to):
    half = block // 2
    source = jnp.broadcast_to(source_row, (STRIP, LANES))
    low, high = source & (LANES - 1), source >> 7
    for row in range(0, half, STRIP):
        top = pick_columns(ref, slice(start + row, start + row + STRIP), low, high)
        bottom = pick_columns(ref, slice(start + half + row, start + half + row + STRIP), low, high)
        for out, message in zip(outs, pack_pair(top, bottom)):
            out[to + row : to + row + STRIP, :] = message


def land_block(ref, start, block, landing_row, messages, at, out, to):
    half = block // 2
    size = ref.shape[1]
    spots = []
    for c in range(0, size, LANES):
        spot = jnp.broadcast_to(landing_row[:, c : c + LANES], (STRIP, LANES))
        spots.append((spot < 0, spot & (LANES - 1), spot >> 7))
    for row in range(0, half, STRIP):
        parts = [message[at + row : at + row + STRIP, :] for message in messages]
        pairs = [pack_pair(parts[0], parts[1]), pack_pair(parts[2], parts[3])]
        for side in range(2):
            tiles = [pair[side] for pair in pairs]
            first = start + side * half + row
            last = to + side * half + row
            for number, (stays, low, high) in enumerate(spots):
                lanes = slice(number * LANES, (number + 1) * LANES)
                got = gather_tiles(tiles, low, high)
                out[last : last + STRIP, lanes] = jnp.where(
                    stays, ref[first : first + STRIP, lanes], got
                )


def move_plan(owner, place):
    size = owner.shape[1]
    own = place[4]
    line = iota((8, size), 0)
    target = jnp.where(
        line == 0,
        place[0],
        jnp.where(line == 1, place[1], jnp.where(line == 2, place[2], place[3])),
    )
    nobody = jnp.broadcast_to(owner, (8, size))
    away = nobody != own
    masks = jnp.where(away & (((nobody == target) & (line < 4)) | (line == 4)), 1.0, 0.0)
    ranks = exclusive_count(masks)
    counts = jnp.sum(masks, axis=1, keepdims=True)
    hole = ranks[4:5]
    gone = masks[4:5] > 0.5
    column = jnp.full((1, size), -1.0, F32)
    landing = jnp.full((1, size), -1.0, F32)
    offset = jnp.zeros((1, 1), F32)
    for way in range(4):
        column = jnp.where(masks[way : way + 1] > 0.5, way * MOVE + ranks[way : way + 1], column)
        ahead = hole - offset
        here = gone & (ahead >= 0.0) & (ahead < counts[way : way + 1])
        landing = jnp.where(here, way * MOVE + ahead, landing)
        offset = offset + counts[way : way + 1]
    spots = one_hot_rows(column.astype(I32), 0, 4 * MOVE)
    element = iota((8, size), 1)
    parts = jnp.where(iota((8, size), 0) == 0, element >> 4, element & 15)
    found = dot_nt(parts.astype(BF16), spots)
    source = found[0:1] * 16.0 + found[1:2]
    return source.astype(I32), landing.astype(I32)


def fetch(source, target, sems, number, start, count, to):
    return pltpu.make_async_copy(
        source.at[pl.ds(start, count), :], target.at[pl.ds(to, count), :], sems.at[number]
    )


def send_parts(metric, first, source, outs, held, sems, block):
    half = block // 2
    for number in range(held.shape[0] // block):
        fetch(metric, held, sems, number, (first + number) * block, block, number * block).wait()
        pack_block(held, number * block, block, source, outs, number * half)


def fetch_parts(metric, first, held, sems, block):
    for number in range(held.shape[0] // block):
        fetch(metric, held, sems, number, (first + number) * block, block, number * block).start()


def plan_and_pack_kernel(place, owner, metric, source_ref, landing_ref, *rest, block):
    *outs, held, sems = rest
    fetch_parts(metric, 0, held, sems, block)
    source, landing = move_plan(owner[...], place)
    source_ref[...] = source
    landing_ref[...] = landing
    send_parts(metric, 0, source[:, LANES:], outs, held, sems, block)


def pack_kernel(source, metric, after, *rest, first, pair, block):
    del after
    *outs, held, sems = rest
    fetch_parts(metric, first, held, sems, block)
    lanes = slice(pair * LANES, (pair + 1) * LANES)
    send_parts(metric, first, source[:, lanes], outs, held, sems, block)


def sent_shapes(count, block, size):
    outs = [jax.ShapeDtypeStruct((count * block // 2, LANES), F32)] * 2
    scratch = [pltpu.VMEM((count * block, size), F32), pltpu.SemaphoreType.DMA((count,))]
    return outs, scratch


def plan_and_pack(place, owner, metric_rows, block):
    size = metric_rows.shape[1]
    outs, scratch = sent_shapes(EARLY, block, size)
    plan = [jax.ShapeDtypeStruct((1, 4 * MOVE), I32), jax.ShapeDtypeStruct((1, size), I32)]
    return pl.pallas_call(
        functools.partial(plan_and_pack_kernel, block=block),
        in_specs=[SMEM, VMEM, HBM],
        out_specs=[VMEM] * 4,
        out_shape=plan + outs,
        scratch_shapes=scratch,
        name="plan_and_pack",
        cost_estimate=QUICK,
        compiler_params=LARGE,
    )(place, owner, metric_rows)


def pack(source, metric_rows, first, count, pair, block, after, name):
    outs, scratch = sent_shapes(count, block, metric_rows.shape[1])
    return pl.pallas_call(
        functools.partial(pack_kernel, first=first, pair=pair, block=block),
        in_specs=[VMEM, HBM, ANY],
        out_specs=[VMEM] * 2,
        out_shape=outs,
        scratch_shapes=scratch,
        name=name,
        cost_estimate=QUICK,
        compiler_params=LARGE,
    )(source, metric_rows, after)


def land_metric_kernel(landing, metric, *rest, first, block):
    messages = rest[:4]
    out, held, ready, sems, out_sems = rest[-5:]
    count = held.shape[0] // block
    fetch_parts(metric, first, held, sems, block)
    for number in range(count):
        start = number * block
        fetch(metric, held, sems, number, (first + number) * block, block, start).wait()
        land_block(held, start, block, landing[...], messages, start // 2, ready, start)
        fetch(ready, out, out_sems, number, start, block, (first + number) * block).start()
    for number in range(count):
        start = number * block
        fetch(ready, out, out_sems, number, start, block, (first + number) * block).wait()


def land_metric(landing, metric_rows, arrived, first, count, block, before, after, name):
    size = metric_rows.shape[1]
    operands = [landing, metric_rows, *arrived, after]
    specs = [VMEM, HBM] + [VMEM] * 4 + [ANY]
    aliases = {}
    if before is not None:
        operands.append(before)
        specs.append(HBM)
        aliases = {7: 0}
    return pl.pallas_call(
        functools.partial(land_metric_kernel, first=first, block=block),
        in_specs=specs,
        out_specs=HBM,
        out_shape=jax.ShapeDtypeStruct(metric_rows.shape, F32),
        scratch_shapes=[
            pltpu.VMEM((count * block, size), F32),
            pltpu.VMEM((count * block, size), F32),
            pltpu.SemaphoreType.DMA((count,)),
            pltpu.SemaphoreType.DMA((count,)),
        ],
        input_output_aliases=aliases,
        name=name,
        cost_estimate=QUICK,
        compiler_params=LARGE,
    )(*operands)


def land_field_kernel(landing, relaxed, first, second, third, fourth, out):
    rows = relaxed.shape[0]
    land_block(relaxed, 0, rows, landing[...], (first, second, third, fourth), 0, out, 0)


def land_field(landing, relaxed, arrived):
    return pl.pallas_call(
        land_field_kernel,
        in_specs=[VMEM] * 6,
        out_specs=VMEM,
        out_shape=jax.ShapeDtypeStruct(relaxed.shape, F32),
        name="land_field",
        cost_estimate=QUICK,
        compiler_params=SMALL,
    )(landing, relaxed, *arrived)


FACE_DOM = EY * EZ
FACE_SUB = EX * EZ
EDGE_DOM = EZ * (4 * EY - 1)
EDGE_SUB = EZ * (4 * EX - 1)
CORNER_DOM = EZ * (4 * EY - 2)
CORNER_SUB = EZ * (4 * EX - 2)


def up(count):
    return -(-count // LANES) * LANES


EDGE_TILES = up(EDGE_DOM) // LANES
CORNER_TILES = up(CORNER_DOM) // LANES


def table_starts(hosted):
    edge_dom, edge_sub = hosted[1], hosted[1] + EDGE_TILES * LANES
    corner_dom, corner_sub = hosted[2], hosted[2] + CORNER_TILES * LANES
    return (
        (0, hosted[0], hosted[0] + up(FACE_DOM), hosted[0]),
        (0, edge_dom, edge_sub, edge_sub + EDGE_SUB),
        (0, corner_dom, corner_sub, corner_sub + CORNER_SUB),
    )


KINDS = (6, 12, 8)
FACE_ROWS = 2 * INNER * 8
EDGE_ROWS = 16
CORNER_ROWS = 4
CORNER_BASE = FACE_ROWS + EDGE_TILES * EDGE_ROWS
MESSAGE_ROWS = CORNER_BASE + CORNER_TILES * CORNER_ROWS


def shared_columns(ids, place, hosted):
    lines, size = ids.shape
    line = iota((lines, 1), 0)
    per = jnp.where(line < 6, hosted[0], jnp.where(line < 18, hosted[1], hosted[2]))
    owns, rows, masks = [], jnp.zeros((lines, size), I32), []
    for device in (place[4], place[1], place[3], place[5]):
        local = ids - device * per
        inside = (local >= 0) & (local < per)
        rows = jnp.where(inside, local, rows)
        owns.append(inside)
    starts = table_starts(hosted)
    lower = (iota((lines, lines), 1) < iota((lines, lines), 0)) & (
        (iota((lines, lines), 0) < 6) == (iota((lines, lines), 1) < 6)
    )
    lower = lower & ((iota((lines, lines), 0) < 18) == (iota((lines, lines), 1) < 18))
    lower = jnp.where(lower, 1.0, 0.0).astype(BF16)
    column = rows
    marks = jnp.concatenate([jnp.where(inside, 1.0, 0.0) for inside in owns[1:]], axis=0)
    ranks = exclusive_count(marks)
    for number in range(3):
        inside = owns[1 + number]
        mark = marks[number * lines : (number + 1) * lines]
        above = jnp.sum(dot(lower, mark.astype(BF16)), axis=1, keepdims=True)
        rank = (ranks[number * lines : (number + 1) * lines] + above).astype(I32)
        base = jnp.where(
            line < 6,
            starts[0][1 + number],
            jnp.where(line < 18, starts[1][1 + number], starts[2][1 + number]),
        )
        column = jnp.where(inside, base + rank, column)
    return column, rows


def scatter_two(parts, column_row, tiles):
    high, low = split(parts)
    both = jnp.concatenate([high, low], axis=0)
    size = column_row.shape[1]
    tile = jnp.broadcast_to((column_row >> 7).astype(BF16), both.shape)
    zero = jnp.zeros(both.shape, BF16)
    left = jnp.concatenate([jnp.where(tile == h, both, zero) for h in range(tiles)], axis=0)
    return dot_nt(left, one_hot_rows(column_row & (LANES - 1), 0, LANES))


def face_rows(face, inner):
    end = 7 * (face % 2)
    if face < 2:
        return pl.ds(end * 64 + inner * 8, 8)
    if face < 4:
        return pl.ds(inner * 64 + end * 8, 8)
    return pl.ds(inner * 64 + end, 8, stride=8)


def all_lanes(ref, rows):
    return jnp.concatenate([ref[c, rows, :] for c in range(ref.shape[0])], axis=1)


def face_nodes(ref, face):
    return jnp.concatenate(
        [all_lanes(ref, face_rows(face, inner)) for inner in range(1, INNER + 1)], axis=0
    )


def edge_place(edge):
    ends = (7 * (edge % 4 // 2), 7 * (edge % 2))
    if edge < 4:
        return ends[0] * 8 + ends[1], 64
    if edge < 8:
        return ends[0] * 64 + ends[1], 8
    return ends[0] * 64 + ends[1] * 8, 1


def edge_rows(edge):
    start, stride = edge_place(edge)
    return pl.ds(start, 8) if stride == 1 else pl.ds(start, 8, stride=stride)


def corner_place(corner):
    return (corner // 4) * 448 + (corner // 2 % 2) * 56 + (corner % 2) * 7


def apply_kernel(
    place,
    ids,
    solution,
    metric_hbm,
    grad_left,
    image_left,
    square_left,
    after,
    image_ref,
    diagonal_ref,
    column_ref,
    face_table,
    edge_table,
    corner_table,
    dom_out,
    sub_out,
    metric,
    flux_r,
    sems,
    *,
    table,
):
    del after
    size = image_ref.shape[0] * LANES
    count = table.shape[0]
    plane = count * count
    nodes = count * plane
    halves = 2
    part_rows = nodes // halves
    copies = [
        [
            fetch(metric_hbm, metric, sems, h * 7 + c, c * nodes + h * part_rows, part_rows,
                  c * nodes + h * part_rows)
            for c in range(7)
        ]
        for h in range(halves)
    ]
    for group in copies:
        for copy in group:
            copy.start()

    width = 2 * LANES
    node = iota((count, width), 0)
    ends = (0, count - 1)
    end_value = {0: float(table[0, 0]), count - 1: float(table[count - 1, count - 1])}
    ends_k = jnp.where(
        node == 0, end_value[0], jnp.where(node == count - 1, end_value[count - 1], 0.0)
    )
    for i in range(count):
        if i % (count // halves) == 0:
            for copy in copies[i // (count // halves)]:
                copy.wait()
        rows = slice(i * plane, (i + 1) * plane)
        for base in range(0, size, width):
            lanes = slice(base, base + width)

            grads = dot(grad_left[...], triple(solution[rows, lanes]))
            fluxes, weights = [[], []], [[], []]
            strip = 2 * count
            for start in range(0, plane, strip):
                at = slice(start, start + strip)
                part = [
                    metric[c * nodes + i * plane + start : c * nodes + i * plane + start + strip, lanes]
                    for c in range(6)
                ]
                grad_r = sum(
                    float(table[i, q])
                    * solution[q * plane + start : q * plane + start + strip, lanes]
                    for q in range(count)
                )
                grad_s, grad_t = grads[start : start + strip], grads[plane + start : plane + start + strip]
                flux_r[i * plane + start : i * plane + start + strip, lanes] = (
                    part[0] * grad_r + part[3] * grad_s + part[4] * grad_t
                )
                fluxes[0].append(split(part[3] * grad_r + part[1] * grad_s + part[5] * grad_t))
                fluxes[1].append(split(part[4] * grad_r + part[5] * grad_s + part[2] * grad_t))
                weights[0].append(split(part[1]))
                weights[1].append(split(part[2]))

            def stacked(pieces):
                pieces = pieces[0] + pieces[1]
                high = [piece[0] for piece in pieces]
                return jnp.concatenate(high + high + [piece[1] for piece in pieces], axis=0)

            image = dot(image_left[...], stacked(fluxes))
            diagonal = dot(square_left[...], stacked(weights))
            for j in range(count):
                lines = slice(j * count, (j + 1) * count)
                first = i * plane + j * count

                def here(c):
                    return metric[c * nodes + first : c * nodes + first + count, lanes]

                mass = here(6)
                total = diagonal[lines] + mass
                if j in ends:
                    total = total + here(5) * (ends_k * (2.0 * end_value[j]))
                if i in ends:
                    total = total + here(4) * (ends_k * (2.0 * end_value[i]))
                    if j in ends:
                        total = total + here(3) * (2.0 * end_value[i] * end_value[j])
                value = image[lines] + mass * solution[first : first + count, lanes]
                for c in range(width // LANES):
                    side = slice(c * LANES, (c + 1) * LANES)
                    image_ref[base // LANES + c, first : first + count, :] = value[:, side]
                    diagonal_ref[base // LANES + c, first : first + count, :] = total[:, side]
    for i in range(count):
        rows = slice(i * plane, (i + 1) * plane)
        for c in range(size // LANES):
            lanes = slice(c * LANES, (c + 1) * LANES)
            image_ref[c, rows, :] += sum(
                float(table[a, i]) * flux_r[a * plane : (a + 1) * plane, lanes]
                for a in range(count)
            )
            diagonal_ref[c, rows, :] += sum(
                float(table[a, i] * table[a, i]) * metric[a * plane : (a + 1) * plane, lanes]
                for a in range(count)
            )

    def _():
        hosted = (3 * size, 3 * size, size)
        starts = table_starts(hosted)
        column, row = shared_columns(ids[...], place, hosted)
        column_ref[...] = column
        row_high = (row >> 4).astype(F32)
        row_low = (row & 15).astype(F32)
        face_parts = []
        spot = iota((48, size), 0)
        for face in range(6):
            values = face_nodes(image_ref, face)
            values = jnp.where(spot == 0, row_high[face : face + 1], values)
            values = jnp.where(spot == 7, row_low[face : face + 1], values)
            values = jnp.concatenate([values, face_nodes(diagonal_ref, face)], axis=0)
            face_parts.append(jnp.concatenate(split(values), axis=0))
        faces_end = starts[0][2] + up(FACE_SUB)
        for base in range(0, faces_end, 2 * LANES):
            total = None
            for face in range(6):
                more = dot_nt(
                    face_parts[face], one_hot_rows(column[face : face + 1], base, 2 * LANES)
                )
                total = more if total is None else total + more
            total = total[:FACE_ROWS] + total[FACE_ROWS:]
            for side in range(2):
                tile = total[:, side * LANES : (side + 1) * LANES]
                place_column = base + side * LANES
                if place_column < starts[0][1]:
                    face_table[:, place_column : place_column + LANES] = tile
                elif place_column < starts[0][2]:
                    dom_out[0:FACE_ROWS, :] = tile
                else:
                    sub_out[0:FACE_ROWS, :] = tile
        tiles = starts[1][2] // LANES + EDGE_TILES
        total = None
        line = iota((8, size), 0)
        for edge in range(12):
            values = all_lanes(image_ref, edge_rows(edge))
            values = jnp.where(line == 0, row_high[6 + edge : 7 + edge], values)
            values = jnp.where(line == 7, row_low[6 + edge : 7 + edge], values)
            values = jnp.concatenate([values, all_lanes(diagonal_ref, edge_rows(edge))], axis=0)
            more = scatter_two(values, column[6 + edge : 7 + edge], tiles)
            total = more if total is None else total + more
        for number in range(tiles):
            first = number * 2 * EDGE_ROWS
            tile = total[first : first + EDGE_ROWS] + total[first + EDGE_ROWS : first + 2 * EDGE_ROWS]
            place_column = number * LANES
            if place_column < starts[1][1]:
                edge_table[:, place_column : place_column + LANES] = tile
            elif place_column < starts[1][2]:
                base = FACE_ROWS + (place_column - starts[1][1]) // LANES * EDGE_ROWS
                dom_out[base : base + EDGE_ROWS, :] = tile
            else:
                base = FACE_ROWS + (place_column - starts[1][2]) // LANES * EDGE_ROWS
                sub_out[base : base + EDGE_ROWS, :] = tile
        tiles = starts[2][2] // LANES + CORNER_TILES
        total = None
        for corner in range(8):
            at = corner_place(corner)
            values = jnp.concatenate(
                [
                    all_lanes(image_ref, slice(at, at + 1)),
                    all_lanes(diagonal_ref, slice(at, at + 1)),
                    row_high[18 + corner : 19 + corner],
                    row_low[18 + corner : 19 + corner],
                    jnp.zeros((4, size), F32),
                ],
                axis=0,
            )
            more = scatter_two(values, column[18 + corner : 19 + corner], tiles)
            total = more if total is None else total + more
        for number in range(tiles):
            tile = total[number * 16 : number * 16 + 8] + total[number * 16 + 8 : number * 16 + 16]
            place_column = number * LANES
            if place_column < starts[2][1]:
                corner_table[:, place_column : place_column + LANES] = tile
            elif place_column < starts[2][2]:
                base = CORNER_BASE + (place_column - starts[2][1]) // LANES * CORNER_ROWS
                dom_out[base : base + CORNER_ROWS, :] = tile[:CORNER_ROWS]
            else:
                base = CORNER_BASE + (place_column - starts[2][2]) // LANES * CORNER_ROWS
                sub_out[base : base + CORNER_ROWS, :] = tile[:CORNER_ROWS]

    _()


def apply_and_pack(place, ids, field, metric_rows, after, table):
    nodes, size = field.shape
    count = table.shape[0]
    eye = np.eye(count, dtype=np.float32)
    grad = np.concatenate([np.kron(table, eye), np.kron(eye, table)], axis=0)
    square = (table * table).astype(np.float32)
    squares = np.concatenate([np.kron(square, eye), np.kron(eye, square)], axis=0)
    lefts = [split_np(grad), split_np(grad.T), split_np(squares.T)]

    def out(*shape, dtype=F32):
        return jax.ShapeDtypeStruct(shape, dtype)

    outs = [
        out(size // LANES, nodes, LANES),
        out(size // LANES, nodes, LANES),
        out(sum(KINDS), size, dtype=I32),
        out(FACE_ROWS, 3 * size),
        out(EDGE_ROWS, 3 * size),
        out(8, size),
        out(MESSAGE_ROWS, LANES),
        out(MESSAGE_ROWS, LANES),
    ]
    return pl.pallas_call(
        functools.partial(apply_kernel, table=table),
        in_specs=[SMEM, VMEM, VMEM, HBM, VMEM, VMEM, VMEM, ANY],
        out_specs=[VMEM] * len(outs),
        out_shape=outs,
        scratch_shapes=[
            pltpu.VMEM(metric_rows.shape, F32),
            pltpu.VMEM((nodes, size), F32),
            pltpu.SemaphoreType.DMA((14,)),
        ],
        name="apply_and_pack",
        cost_estimate=QUICK,
        compiler_params=LARGE,
    )(place, ids, field, metric_rows, *[jnp.asarray(left) for left in lefts], after)


def message_parts(kind):
    if kind == 0:
        return [0], FACE_ROWS
    if kind == 1:
        return [FACE_ROWS + q * EDGE_ROWS for q in range(EDGE_TILES)], EDGE_ROWS
    return [CORNER_BASE + q * CORNER_ROWS for q in range(CORNER_TILES)], CORNER_ROWS


def message_tiles(ref, kind):
    places, rows = message_parts(kind)
    return [ref[at : at + rows, :] for at in places]


def table_tiles(ref):
    return [ref[:, c : c + LANES] for c in range(0, ref.shape[1], LANES)]


def message_values(ref, kind, limit):
    values = jnp.concatenate(message_tiles(ref, kind), axis=1)
    first = 2 if kind == 2 else 0
    second = 3 if kind == 2 else 7
    row = (values[first : first + 1] * 16.0 + values[second : second + 1]).astype(I32)
    row = jnp.where(iota(row.shape, 1) < limit, row, -1)
    if kind == 2:
        values = jnp.concatenate([values, jnp.zeros_like(values)], axis=0)
    return values, row


def add_message(ref, tables, outs, limits):
    values, row = message_values(ref, 0, limits[0])
    parts = jnp.concatenate(split(values), axis=0)
    for base in range(0, outs[0].shape[1], 2 * LANES):
        lanes = slice(base, base + 2 * LANES)
        more = dot_nt(parts, one_hot_rows(row, base, 2 * LANES))
        outs[0][:, lanes] = tables[0][:, lanes] + more[:FACE_ROWS] + more[FACE_ROWS:]
    for kind in (1, 2):
        values, row = message_values(ref, kind, limits[kind])
        rows = values.shape[0]
        count = outs[kind].shape[1] // LANES
        total = scatter_two(values, row, count)
        for number in range(count):
            lanes = slice(number * LANES, (number + 1) * LANES)
            first = number * 2 * rows
            more = total[first : first + rows] + total[first + rows : first + 2 * rows]
            outs[kind][:, lanes] = tables[kind][:, lanes] + more


def read_message(ref, tables, back):
    for kind in range(3):
        places, rows = message_parts(kind)
        row = jnp.maximum(message_values(ref, kind, 1 << 20)[1], 0)
        tiles = table_tiles(tables[kind])
        depth = tiles[0].shape[0]
        for number, at in enumerate(places):
            spot = jnp.broadcast_to(row[:, number * LANES : (number + 1) * LANES], (depth, LANES))
            got = gather_tiles(tiles, spot & (LANES - 1), spot >> 7)
            back[at : at + rows, :] = got[:rows]


SUB_LIMITS = (FACE_SUB, EDGE_SUB, CORNER_SUB)
DOM_LIMITS = (FACE_DOM, EDGE_SUB + EZ, CORNER_SUB + 2 * EZ)


def passed_on(message, received):
    parts = [message[0:FACE_ROWS, :]]
    for kind, limit in ((1, EDGE_SUB), (2, CORNER_SUB)):
        ours, theirs = message_tiles(message, kind), message_tiles(received, kind)
        for number in range(len(ours)):
            lane = iota(ours[number].shape, 1) + number * LANES
            parts.append(jnp.where(lane < limit, ours[number], theirs[number]))
    return parts


def pass_on_kernel(message, received, *rest):
    out = rest[-1]
    at = 0
    for part in passed_on(message, received):
        out[at : at + part.shape[0], :] = part
        at += part.shape[0]


def pass_on(message, received, after=()):
    return pl.pallas_call(
        pass_on_kernel,
        in_specs=[VMEM] * 2 + [ANY] * len(after),
        out_specs=VMEM,
        out_shape=jax.ShapeDtypeStruct(message.shape, F32),
        name="pass_on",
        cost_estimate=QUICK,
        compiler_params=SMALL,
    )(message, received, *after)


def add_sub_kernel(faces, edges, corners, message, after, *outs):
    del after
    add_message(message, (faces, edges, corners), outs, SUB_LIMITS)


def add_sub(tables, message, after):
    return pl.pallas_call(
        add_sub_kernel,
        in_specs=[VMEM] * 4 + [ANY],
        out_specs=[VMEM] * 3,
        out_shape=[jax.ShapeDtypeStruct(a.shape, F32) for a in tables],
        name="add_sub",
        cost_estimate=QUICK,
        compiler_params=SMALL,
    )(*tables, message, after)


def add_dom_kernel(faces, edges, corners, message, *outs):
    add_message(message, (faces, edges, corners), outs[:3], DOM_LIMITS)
    read_message(message, outs[:3], outs[3])


def add_dom(tables, message):
    return pl.pallas_call(
        add_dom_kernel,
        in_specs=[VMEM] * 4,
        out_specs=[VMEM] * 4,
        out_shape=[jax.ShapeDtypeStruct(a.shape, F32) for a in (*tables, message)],
        name="add_dom",
        cost_estimate=QUICK,
        compiler_params=SMALL,
    )(*tables, message)


def read_sub_kernel(faces, edges, corners, message, back):
    read_message(message, (faces, edges, corners), back)


def read_sub(tables, message):
    return pl.pallas_call(
        read_sub_kernel,
        in_specs=[VMEM] * 4,
        out_specs=VMEM,
        out_shape=jax.ShapeDtypeStruct(message.shape, F32),
        name="read_sub",
        cost_estimate=QUICK,
        compiler_params=SMALL,
    )(*tables, message)


def spots(column_ref, line, rows, c, first):
    spot = jnp.broadcast_to(column_ref[line : line + 1, c * LANES : (c + 1) * LANES], (rows, LANES))
    return spot & (LANES - 1), (spot >> 7) - first


def put(ref, c, rows, values, high, count):
    line = iota(values.shape, 0)
    new = (line > 0) & (line < 7) & (high >= 0) & (high < count)
    ref[c, rows, :] = jnp.where(new, values, ref[c, rows, :])


def merge_faces(column_ref, tiles, first, image, diagonal):
    for c in range(image.shape[0]):
        for face in range(6):
            low, high = spots(column_ref, face, FACE_ROWS, c, first)
            got = gather_tiles(tiles, low, high)
            for number in range(INNER):
                rows = face_rows(face, number + 1)
                put(image, c, rows, got[number * 8 : number * 8 + 8], high[:8], len(tiles))
                put(diagonal, c, rows, got[48 + number * 8 : 56 + number * 8], high[:8], len(tiles))


def merge_edges(column_ref, tiles, first, image, diagonal):
    for c in range(image.shape[0]):
        for edge in range(12):
            low, high = spots(column_ref, 6 + edge, EDGE_ROWS, c, first)
            got = gather_tiles(tiles, low, high)
            put(image, c, edge_rows(edge), got[:8], high[:8], len(tiles))
            put(diagonal, c, edge_rows(edge), got[8:], high[:8], len(tiles))


def merge_corners(column_ref, tiles, first, image, diagonal):
    tiles = [jnp.concatenate([tile[0:2]] * 4, axis=0) for tile in tiles]
    for c in range(image.shape[0]):
        lanes = slice(c * LANES, (c + 1) * LANES)
        for group in range(2):
            spot = jnp.concatenate(
                [
                    jnp.broadcast_to(column_ref[n : n + 1, lanes], (2, LANES))
                    for n in range(18 + group * 4, 22 + group * 4)
                ],
                axis=0,
            )
            high = (spot >> 7) - first
            got = gather_tiles(tiles, spot & (LANES - 1), high)
            new = (high >= 0) & (high < len(tiles))
            for number in range(4):
                at = corner_place(group * 4 + number)
                for ref, line in ((image, 2 * number), (diagonal, 2 * number + 1)):
                    ref[c, at : at + 1, :] = jnp.where(
                        new[line : line + 1], got[line : line + 1], ref[c, at : at + 1, :]
                    )


def merge_message(column_ref, message, first_kind, image, diagonal):
    size = image.shape[0] * LANES
    starts = table_starts((3 * size, 3 * size, size))
    for kind, merge in enumerate((merge_faces, merge_edges, merge_corners)):
        first = starts[kind][first_kind] // LANES
        merge(column_ref, message_tiles(message, kind), first, image, diagonal)


def merge_own(column, tables, image, diagonal, after):
    def kernel(column, faces, edges, corners, image_in, diagonal_in, after, image, diagonal):
        del after
        image[...] = image_in[...]
        diagonal[...] = diagonal_in[...]
        merge_faces(column, table_tiles(faces), 0, image, diagonal)
        merge_edges(column, table_tiles(edges), 0, image, diagonal)
        merge_corners(column, table_tiles(corners), 0, image, diagonal)

    return pl.pallas_call(
        kernel,
        in_specs=[VMEM] * 6 + [ANY],
        out_specs=[VMEM] * 2,
        out_shape=[jax.ShapeDtypeStruct(image.shape, F32)] * 2,
        name="merge_own",
        cost_estimate=QUICK,
        compiler_params=SMALL,
    )(column, *tables, image, diagonal, after)


def merge_dom(column, message, image, diagonal, after):
    def kernel(column, message, image_in, diagonal_in, after, image, diagonal):
        del after
        image[...] = image_in[...]
        diagonal[...] = diagonal_in[...]
        merge_message(column, message, 1, image, diagonal)

    return pl.pallas_call(
        kernel,
        in_specs=[VMEM] * 4 + [ANY],
        out_specs=[VMEM] * 2,
        out_shape=[jax.ShapeDtypeStruct(image.shape, F32)] * 2,
        name="merge_dom",
        cost_estimate=QUICK,
        compiler_params=SMALL,
    )(column, message, image, diagonal, after)


def relax_kernel(column, message, image_in, diagonal_in, field, forcing, source, *rest):
    relaxed, *outs, image, diagonal = rest[-7:]
    nodes, size = relaxed.shape
    image[...] = image_in[...]
    diagonal[...] = diagonal_in[...]
    merge_message(column, message, 2, image, diagonal)
    for row in range(0, nodes, STRIP):
        rows = slice(row, row + STRIP)
        for c in range(size // LANES):
            lanes = slice(c * LANES, (c + 1) * LANES)
            step = (forcing[rows, lanes] - image[c, rows, :]) / diagonal[c, rows, :]
            relaxed[rows, lanes] = field[rows, lanes] + RELAX * step
    for pair in range(2):
        source_row = source[:, pair * LANES : (pair + 1) * LANES]
        pack_block(relaxed, 0, nodes, source_row, outs[2 * pair : 2 * pair + 2], 0)


def relax_and_pack(column, message, image, diagonal, field, forcing, source, after):
    nodes, size = field.shape
    leaving = jax.ShapeDtypeStruct((nodes // 2, LANES), F32)
    return pl.pallas_call(
        relax_kernel,
        in_specs=[VMEM] * 7 + [ANY] * len(after),
        out_specs=[VMEM] * 5,
        out_shape=[jax.ShapeDtypeStruct((nodes, size), F32)] + [leaving] * 4,
        scratch_shapes=[pltpu.VMEM((size // LANES, nodes, LANES), F32)] * 2,
        name="relax_and_pack",
        cost_estimate=QUICK,
        compiler_params=SMALL,
    )(column, message, image, diagonal, field, forcing, source, *after)


def shifted(value, axis, steps):
    count = lax.axis_size(axis)
    return lax.ppermute(value, axis, [(i, (i + steps) % count) for i in range(count)])


def swapped(to_previous, to_next, axis):
    return shifted(to_next, axis, 1), shifted(to_previous, axis, -1)


def on_device(solution, forcing, metric, entity_ids, new_owner):
    size = solution.shape[-1]
    place = devices()
    table = derivative_table(solution.shape[0] - 1)
    field = solution.reshape(-1, size)
    metric_rows = metric.reshape(-1, size)
    components = metric.shape[0]
    block = metric_rows.shape[0] // components
    late = components - EARLY
    source, landing, *messages = plan_and_pack(place, new_owner.reshape(1, size), metric_rows, block)
    sub_early = swapped(*messages, "sub")
    messages = pack(source, metric_rows, 0, EARLY, 0, block, landing, "pack_dom_early")
    dom_early = swapped(*messages, "dom")
    image, diagonal, column, *tables, dom, sub = apply_and_pack(
        place, entity_ids, field, metric_rows, messages[0], table
    )
    got_sub = shifted(sub, "sub", 1)
    messages = pack(source, metric_rows, EARLY, late, 1, block, sub, "pack_sub_late")
    sub_late = swapped(*messages, "sub")
    dom = pass_on(dom, got_sub, dom_early + sub_early)
    got_dom = shifted(dom, "dom", 1)
    tables = add_sub(tables, got_sub, dom)
    *tables, dom_back = add_dom(tables, got_dom)
    back_dom = shifted(dom_back, "dom", -1)
    messages = pack(source, metric_rows, EARLY, late, 0, block, dom_back, "pack_dom_late")
    dom_late = swapped(*messages, "dom")
    sub_back = read_sub(tables, got_sub)
    sub_back = pass_on(sub_back, back_dom)
    back_sub = shifted(sub_back, "sub", -1)
    image, diagonal = merge_own(column, tables, image, diagonal, messages[0])
    image, diagonal = merge_dom(column, back_dom, image, diagonal, sub_back)
    relaxed, *leaving = relax_and_pack(
        column, back_sub, image, diagonal, field, forcing.reshape(-1, size), source,
        dom_late + sub_late,
    )
    got_sub = swapped(*leaving[2:], "sub")
    got_dom = swapped(*leaving[:2], "dom")
    moved = land_metric(
        landing, metric_rows, dom_early + sub_early, 0, EARLY, block, None, leaving[0], "land_early"
    )
    moved = land_metric(
        landing, metric_rows, dom_late + sub_late, EARLY, late, block, moved, leaving[0], "land_late"
    )
    smoothed = land_field(landing, relaxed, got_dom + got_sub)
    return smoothed.reshape(solution.shape), moved.reshape(metric.shape)


def solution(mesh):
    placed = (
        P(None, None, None, ("dom", "sub")),
        P(None, None, None, ("dom", "sub")),
        P(None, None, None, None, ("dom", "sub")),
        P(None, ("dom", "sub")),
        P(("dom", "sub")),
    )
    return jax.shard_map(
        on_device,
        mesh=mesh,
        in_specs=placed,
        out_specs=(P(None, None, None, ("dom", "sub")), P(None, None, None, None, ("dom", "sub"))),
        check_vma=False,
    )
```

time: 112 us -> 89.1 us (0.80)
  the two profiles are of different devices: /device:TPU:28 before, /device:TPU:0 now
where the time goes in v2:
time: 89.1 us; the launch traced here: 88.8 us
  Pallas kernels  48.7 us (55%)
  starting transfers between devices  21 us (24%)
  waiting for transfers between devices  14.2 us (16%)
  local copies, waits for them, and re-layouts  3.91 us (4%)
  between operations  0.93 us (1%)
    ppermute x16, starting transfers between devices, shifted(): lax.ppermute(value, axis, [(i, (i + steps) % count) for i in range(count)])  21 us
    ppermute x16, waiting for transfers between devices, shifted(): lax.ppermute(value, axis, [(i, (i + steps) % count) for i in range(count)])  14.2 us
    pallas_call x1, Pallas kernels, apply_and_pack(): pl.pallas_call(functools.partial(apply_kernel, table=table), in_specs=[SM...  13.3 us
    pallas_call x2, Pallas kernels, land_metric(): pl.pallas_call(functools.partial(land_metric_kernel, first=first, block=b...  11.3 us
    pallas_call x3, Pallas kernels, pack(): pl.pallas_call(functools.partial(pack_kernel, first=first, pair=pair, blo...  7.26 us
    pallas_call x1, Pallas kernels, merge_own(): pl.pallas_call(kernel, in_specs=[VMEM] * 6 + [ANY], out_specs=[VMEM] * 2,...  5.42 us
    pallas_call x1, Pallas kernels, plan_and_pack(): pl.pallas_call(functools.partial(plan_and_pack_kernel, block=block), in_s...  3.84 us
    unnamed x18, local copies, waits for them, and re-layouts  3.82 us
  transfers between devices with their start and end apart: 16, of which 2 were waited for; matrix products, arithmetic and copies ran while one was open for 0% of the time, Pallas kernels for 45%

profile of v2, /device:TPU:0, one launch (start us, length us, event | category | flops | bytes accessed | tf_op | source)
XLA Modules:
  0.0 88.8 jit_solution(9544945888866350613)
XLA Ops:
  0.6 0.1 stack.27.place
  0.7 3.1 %copy-done = f32[7,8,8,8,512]{4,3,2,1,0:T(8,128)S(1)} copy-done((f32[7,8,8,8,512]{4,3,2,1,0:T(8,128)S(1)}, f32[7,8,8,8,512]{4,3,2,1,0:T(8,128)}, u32[]{:S(2)}) %copy-start) | copy-done | bytes 7340056
  3.8 0.7 copy-done.8
  4.6 3.8 %plan_and_pack.1 = (s32[1,256]{1,0:T(1,128)S(1)}, s32[1,512]{1,0:T(1,128)S(1)}, f32[1024,128]{1,0:T(8,128)S(1)}, f32[1024,128]{1,0:T(8,128)S(1)}) custom-call(s32[6]{0:T(128)S(1)} %stack.27.place, s32[1,512]{1,0:T(1,128)S(1)} %bitcast.22, f32[3584,512]{1,0:T(8,128)S(1)} %bitcast.12), custom_call_target="tpu_custom_call" | custom-call | flops 1000 | bytes 1000 | tf_op jit(solution)/shard_map/plan_and_pack/pallas_call | solution.py:265
  8.4 3.1 %collective-permute-start.3 = (f32[1024,128]{1,0:T(8,128)S(1)}, f32[1024,128]{1,0:T(8,128)S(1)}, u32[]{:S(2)}, u32[]{:S(2)}) collective-permute-start(f32[1024,128]{1,0:T(8,128)S(1)} %get-tuple-element.46), channel_id=1, source_target_pairs={{0,1},{1,2},{2,3},{3,0},{4,5},{5,6},{6,7},{7,4},{8,9},{9,10},{10,1... | collective-permute-start | bytes 1572872 | tf_op jit(solution)/shard_map/ppermute | solution.py:985
  11.5 2.1 %collective-permute-start.4 = (f32[1024,128]{1,0:T(8,128)S(1)}, f32[1024,128]{1,0:T(8,128)S(1)}, u32[]{:S(2)}, u32[]{:S(2)}) collective-permute-start(f32[1024,128]{1,0:T(8,128)S(1)} %get-tuple-element.47), channel_id=1, source_target_pairs={{0,3},{1,0},{2,1},{3,2},{4,7},{5,4},{6,5},{7,6},{8,11},{9,8},{10,9... | collective-permute-start | bytes 1572872 | tf_op jit(solution)/shard_map/ppermute | solution.py:985
  13.6 2.9 %pack_dom_early.1 = (f32[1024,128]{1,0:T(8,128)S(1)}, f32[1024,128]{1,0:T(8,128)S(1)}) custom-call(s32[1,256]{1,0:T(1,128)S(1)} %get-tuple-element.37.source, f32[3584,512]{1,0:T(8,128)S(1)} %bitcast.13, s32[1,512]{1,0:T(1,128)S(1)} %get-tuple-element.36.after.landing), custom_call_target="tpu_custom_call" | custom-call | flops 1000 | bytes 1000 | tf_op jit(solution)/shard_map/pack_dom_early/pallas_call | solution.py:279
  16.5 0.1 collective-permute-start.1
  16.6 2.6 %collective-permute-start.2 = (f32[1024,128]{1,0:T(8,128)S(1)}, f32[1024,128]{1,0:T(8,128)S(1)}, u32[]{:S(2)}, u32[]{:S(2)}) collective-permute-start(f32[1024,128]{1,0:T(8,128)S(1)} %get-tuple-element.38.after), channel_id=1, source_target_pairs={{0,28},{4,0},{8,4},{12,8},{16,12},{20,16},{24,20},{28,24},{1,29},{... | collective-permute-start | bytes 1572872 | tf_op jit(solution)/shard_map/ppermute | solution.py:985
  19.2 13.3 %apply_and_pack.1 = (f32[4,512,128]{2,1,0:T(8,128)S(1)}, f32[4,512,128]{2,1,0:T(8,128)S(1)}, s32[26,512]{1,0:T(8,128)S(1)}, f32[96,1536]{1,0:T(8,128)S(1)}, f32[...) custom-call(s32[6]{0:T(128)S(1)} %stack.27.place, ...), custom_call_target="tpu_custom_call" | custom-call | flops 1000 | bytes 1000 | tf_op jit(solution)/shard_map/apply_and_pack/pallas_call | solution.py:692
  32.5 0.2 collective-permute-start
  32.8 6.3 %collective-permute-done.received.message = f32[176,128]{1,0:T(8,128)S(1)} collective-permute-done((f32[176,128]{1,0:T(8,128)S(1)}, f32[176,128]{1,0:T(8,128)S(1)}, u32[]{:S(2)}, u32[]{:S(2)}) %collective-permute-start) | collective-permute-done | bytes 90144 | tf_op jit(solution)/shard_map/ppermute | solution.py:985
  39.2 2.2 %pack_sub_late.1 = (f32[768,128]{1,0:T(8,128)S(1)}, f32[768,128]{1,0:T(8,128)S(1)}) custom-call(s32[1,256]{1,0:T(1,128)S(1)} %get-tuple-element.37.source, f32[3584,512]{1,0:T(8,128)S(1)} %bitcast.15, f32[176,128]{1,0:T(8,128)S(1)} %get-tuple-element.43.after), custom_call_target="tpu_custom_call" | custom-call | flops 1000 | bytes 1000 | tf_op jit(solution)/shard_map/pack_sub_late/pallas_call | solution.py:279
  41.4 0.1 collective-permute-start.10
  41.4 3.8 %collective-permute-start.11 = (f32[768,128]{1,0:T(8,128)S(1)}, f32[768,128]{1,0:T(8,128)S(1)}, u32[]{:S(2)}, u32[]{:S(2)}) collective-permute-start(f32[768,128]{1,0:T(8,128)S(1)} %get-tuple-element.64), channel_id=1, source_target_pairs={{0,3},{1,0},{2,1},{3,2},{4,7},{5,4},{6,5},{7,6},{8,11},{9,8},{10,9... | collective-permute-start | bytes 1179656 | tf_op jit(solution)/shard_map/ppermute | solution.py:985
  45.3 0.5 add_sub.1
  45.7 0.7 add_dom.1
  46.4 2.2 %pack_dom_late.1 = (f32[768,128]{1,0:T(8,128)S(1)}, f32[768,128]{1,0:T(8,128)S(1)}) custom-call(s32[1,256]{1,0:T(1,128)S(1)} %get-tuple-element.37.source, f32[3584,512]{1,0:T(8,128)S(1)} %bitcast.16, f32[176,128]{1,0:T(8,128)S(1)} %get-tuple-element.54.after), custom_call_target="tpu_custom_call" | custom-call | flops 1000 | bytes 1000 | tf_op jit(solution)/shard_map/pack_dom_late/pallas_call | solution.py:279
  48.6 0.6 collective-permute-start.8
  49.3 2.1 %collective-permute-start.9 = (f32[768,128]{1,0:T(8,128)S(1)}, f32[768,128]{1,0:T(8,128)S(1)}, u32[]{:S(2)}, u32[]{:S(2)}) collective-permute-start(f32[768,128]{1,0:T(8,128)S(1)} %get-tuple-element.57.after), channel_id=1, source_target_pairs={{0,28},{4,0},{8,4},{12,8},{16,12},{20,16},{24,20},{28,24},{1,29},{... | collective-permute-start | bytes 1179656 | tf_op jit(solution)/shard_map/ppermute | solution.py:985
  51.4 0.4 read_sub.1.message
  51.7 7.9 %collective-permute-done.6.received.message = f32[176,128]{1,0:T(8,128)S(1)} collective-permute-done((f32[176,128]{1,0:T(8,128)S(1)}, f32[176,128]{1,0:T(8,128)S(1)}, u32[]{:S(2)}, u32[]{:S(2)}) %collective-permute-start.6) | collective-permute-done | bytes 90144 | tf_op jit(solution)/shard_map/ppermute | solution.py:985
  59.6 0.1 collective-permute-start.7
  59.7 5.4 %merge_own.1 = (f32[4,512,128]{2,1,0:T(8,128)S(1)}, f32[4,512,128]{2,1,0:T(8,128)S(1)}) custom-call(s32[26,512]{1,0:T(8,128)S(1)} %get-tuple-element.39.column, f32[96,1536]{1,0:T(8,128)S(1)} %get-tuple-element.51.faces, f32[16,1536]{1,0:T(8,128)S(1)} %get-tuple-element.52.edges, f32[8,512]{1,0:T(8,128)S(1)} %get-tuple-element.53.corners, ...), custom_call_target="tpu_custom_call" | custom-call | flops 1000 | bytes 1000 | tf_op jit(solution)/shard_map/merge_own/pallas_call | solution.py:922
  65.1 1.2 %merge_dom.1 = (f32[4,512,128]{2,1,0:T(8,128)S(1)}, f32[4,512,128]{2,1,0:T(8,128)S(1)}) custom-call(s32[26,512]{1,0:T(8,128)S(1)} %get-tuple-element.39.column, f32[176,128]{1,0:T(8,128)S(1)} %collective-permute-done.6.received.message, f32[4,512,128]{2,1,0:T(8,128)S(1)} %get-tuple-element.58.image_in, f32[4,512,128]{2,1,0:T(8,128)S(1)} %get-tuple-element.59.diagonal_in, ...), custom_call_target="tpu_custom_call" | custom-call | flops 1000 | bytes 1000 | tf_op jit(solution)/shard_map/merge_dom/pallas_call | solution.py:940
  66.4 2.6 %relax_and_pack.1 = (f32[512,512]{1,0:T(8,128)S(1)}, f32[256,128]{1,0:T(8,128)S(1)}, f32[256,128]{1,0:T(8,128)S(1)}, f32[256,128]{1,0:T(8,128)S(1)}, f32[256,128]{1,0:T(8,128)S(1)}) custom-call(s32[26,512]{1,0:T(8,128)S(1)} %get-tuple-element.39.column, f32[176,128]{1,0:T(8,128)S(1)} %collective-permute-done.7.message, ...), custom_call_target="tpu_custom_call" | custom-call | flops 1000 | bytes 1000 | tf_op jit(solution)/shard_map/relax_and_pack/pallas_call | solution.py:971
  69.0 2.4 %collective-permute-start.12 = (f32[256,128]{1,0:T(8,128)S(1)}, f32[256,128]{1,0:T(8,128)S(1)}, u32[]{:S(2)}, u32[]{:S(2)}) collective-permute-start(f32[256,128]{1,0:T(8,128)S(1)} %get-tuple-element.66), channel_id=1, source_target_pairs={{0,4},{4,8},{8,12},{12,16},{16,20},{20,24},{24,28},{28,0},{1,5},{5... | collective-permute-start | bytes 393224 | tf_op jit(solution)/shard_map/ppermute | solution.py:985
  71.4 1.7 %collective-permute-start.14 = (f32[256,128]{1,0:T(8,128)S(1)}, f32[256,128]{1,0:T(8,128)S(1)}, u32[]{:S(2)}, u32[]{:S(2)}) collective-permute-start(f32[256,128]{1,0:T(8,128)S(1)} %get-tuple-element.68), channel_id=1, source_target_pairs={{0,1},{1,2},{2,3},{3,0},{4,5},{5,6},{6,7},{7,4},{8,9},{9,10},{10,1... | collective-permute-start | bytes 393224 | tf_op jit(solution)/shard_map/ppermute | solution.py:985
  73.1 2.1 %collective-permute-start.15 = (f32[256,128]{1,0:T(8,128)S(1)}, f32[256,128]{1,0:T(8,128)S(1)}, u32[]{:S(2)}, u32[]{:S(2)}) collective-permute-start(f32[256,128]{1,0:T(8,128)S(1)} %get-tuple-element.69), channel_id=1, source_target_pairs={{0,3},{1,0},{2,1},{3,2},{4,7},{5,4},{6,5},{7,6},{8,11},{9,8},{10,9... | collective-permute-start | bytes 393224 | tf_op jit(solution)/shard_map/ppermute | solution.py:985
  75.2 6.3 %land_early.1.rest_5_ = f32[3584,512]{1,0:T(8,128)} custom-call(s32[1,512]{1,0:T(1,128)S(1)} %get-tuple-element.36.after.landing, f32[3584,512]{1,0:T(8,128)S(1)} %bitcast.17, f32[1024,128]{1,0:T(8,128)S(1)} %collective-permute-done.1.rest_0_, f32[1024,128]{1,0:T(8,128)S(1)} %collective-permute-done.2.rest_1_, ...), custom_call_target="tpu_custom_call" | custom-call | flops 1000 | bytes 1000 | tf_op jit(solution)/shard_map/land_early/pallas_call | solution.py:315
  81.6 5.0 %land_late.1 = f32[3584,512]{1,0:T(8,128)} custom-call(s32[1,512]{1,0:T(1,128)S(1)} %get-tuple-element.36.after.landing, f32[3584,512]{1,0:T(8,128)S(1)} %bitcast.18, f32[768,128]{1,0:T(8,128)S(1)} %collective-permute-done.8.rest_0_, f32[768,128]{1,0:T(8,128)S(1)} %collective-permute-done.9.rest_1_, ...), custom_call_target="tpu_custom_call", output_to_operand_aliasing={{}: (7, {})} | custom-call | flops 1000 | bytes 1000 | tf_op jit(solution)/shard_map/land_late/pallas_call | solution.py:315
  86.6 2.2 %land_field.1 = f32[512,512]{1,0:T(8,128)} custom-call(s32[1,512]{1,0:T(1,128)S(1)} %get-tuple-element.36.after.landing, f32[512,512]{1,0:T(8,128)S(1)} %get-tuple-element.65.relaxed, f32[256,128]{1,0:T(8,128)S(1)} %collective-permute-done.12.first, f32[256,128]{1,0:T(8,128)S(1)} %collective-permute-done.13.second, ...), custom_call_target="tpu_custom_call" | custom-call | flops 1000 | bytes 1000 | tf_op jit(solution)/shard_map/land_field/pallas_call | solution.py:339
  (35 shorter events, 0.2 us)
Async XLA Ops:
  0.7 3.1 %copy-start = (f32[7,8,8,8,512]{4,3,2,1,0:T(8,128)S(1)}, f32[7,8,8,8,512]{4,3,2,1,0:T(8,128)}, u32[]{:S(2)}) copy-start(f32[7,8,8,8,512]{4,3,2,1,0:T(8,128)} %param.10) | copy-start | bytes 22020100
  3.8 0.7 copy-start.8
  4.5 9.1 %copy-start.1 = (f32[7,8,8,8,512]{4,3,2,1,0:T(8,128)S(1)}, f32[7,8,8,8,512]{4,3,2,1,0:T(8,128)}, u32[]{:S(2)}) copy-start(f32[7,8,8,8,512]{4,3,2,1,0:T(8,128)} %param.10) | copy-start | bytes 22020100
  4.5 14.7 %copy-start.2 = (f32[8,8,8,512]{3,2,1,0:T(8,128)S(1)}, f32[8,8,8,512]{3,2,1,0:T(8,128)}, u32[]{:S(2)}) copy-start(f32[8,8,8,512]{3,2,1,0:T(8,128)} %param.8) | copy-start | bytes 3145732
  4.5 14.7 %copy-start.4 = (s32[26,512]{1,0:T(8,128)S(1)}, s32[26,512]{1,0:T(8,128)}, u32[]{:S(2)}) copy-start(s32[26,512]{1,0:T(8,128)} %ids.1) | copy-start | bytes 159748
  4.5 14.7 %copy-start.5 = (bf16[128,192]{1,0:T(8,128)(2,1)S(1)}, bf16[128,192]{1,0:T(8,128)(2,1)}, u32[]{:S(2)}) copy-start(bf16[128,192]{1,0:T(8,128)(2,1)} %constant.35.clone.grad_left) | copy-start | bytes 147460
  4.5 14.7 %copy-start.6 = (bf16[64,384]{1,0:T(8,128)(2,1)S(1)}, bf16[64,384]{1,0:T(8,128)(2,1)}, u32[]{:S(2)}) copy-start(bf16[64,384]{1,0:T(8,128)(2,1)} %constant.37.clone.square_left) | copy-start | bytes 147460
  4.5 14.7 %copy-start.7 = (bf16[64,384]{1,0:T(8,128)(2,1)S(1)}, bf16[64,384]{1,0:T(8,128)(2,1)}, u32[]{:S(2)}) copy-start(bf16[64,384]{1,0:T(8,128)(2,1)} %constant.36.clone.image_left) | copy-start | bytes 147460
  8.4 30.7 %collective-permute-start.3 = (f32[1024,128]{1,0:T(8,128)S(1)}, f32[1024,128]{1,0:T(8,128)S(1)}, u32[]{:S(2)}, u32[]{:S(2)}) collective-permute-start(f32[1024,128]{1,0:T(8,128)S(1)} %get-tuple-element.46), channel_id=1, source_target_pairs={{0,1},{1,2},{2,3},{3,0},{4,5},{5,6},{6,7},{7,4},{8,9},{9,10},{10,1... | collective-permute-start | bytes 1572872 | tf_op jit(solution)/shard_map/ppermute | solution.py:985
  11.5 27.6 %collective-permute-start.4 = (f32[1024,128]{1,0:T(8,128)S(1)}, f32[1024,128]{1,0:T(8,128)S(1)}, u32[]{:S(2)}, u32[]{:S(2)}) collective-permute-start(f32[1024,128]{1,0:T(8,128)S(1)} %get-tuple-element.47), channel_id=1, source_target_pairs={{0,3},{1,0},{2,1},{3,2},{4,7},{5,4},{6,5},{7,6},{8,11},{9,8},{10,9... | collective-permute-start | bytes 1572872 | tf_op jit(solution)/shard_map/ppermute | solution.py:985
  16.5 22.6 %collective-permute-start.1 = (f32[1024,128]{1,0:T(8,128)S(1)}, f32[1024,128]{1,0:T(8,128)S(1)}, u32[]{:S(2)}, u32[]{:S(2)}) collective-permute-start(f32[1024,128]{1,0:T(8,128)S(1)} %get-tuple-element.45), channel_id=1, source_target_pairs={{0,4},{4,8},{8,12},{12,16},{16,20},{20,24},{24,28},{28,0},{1,5},{5... | collective-permute-start | bytes 1572872 | tf_op jit(solution)/shard_map/ppermute | solution.py:985
  16.6 22.5 %collective-permute-start.2 = (f32[1024,128]{1,0:T(8,128)S(1)}, f32[1024,128]{1,0:T(8,128)S(1)}, u32[]{:S(2)}, u32[]{:S(2)}) collective-permute-start(f32[1024,128]{1,0:T(8,128)S(1)} %get-tuple-element.38.after), channel_id=1, source_target_pairs={{0,28},{4,0},{8,4},{12,8},{16,12},{20,16},{24,20},{28,24},{1,29},{... | collective-permute-start | bytes 1572872 | tf_op jit(solution)/shard_map/ppermute | solution.py:985
  32.5 6.6 %collective-permute-start = (f32[176,128]{1,0:T(8,128)S(1)}, f32[176,128]{1,0:T(8,128)S(1)}, u32[]{:S(2)}, u32[]{:S(2)}) collective-permute-start(f32[176,128]{1,0:T(8,128)S(1)} %get-tuple-element.43.after), channel_id=1, source_target_pairs={{0,1},{1,2},{2,3},{3,0},{4,5},{5,6},{6,7},{7,4},{8,9},{9,10},{10,1... | collective-permute-start | bytes 270344 | tf_op jit(solution)/shard_map/ppermute | solution.py:985
  39.1 6.6 %collective-permute-start.5 = (f32[176,128]{1,0:T(8,128)S(1)}, f32[176,128]{1,0:T(8,128)S(1)}, u32[]{:S(2)}, u32[]{:S(2)}) collective-permute-start(f32[176,128]{1,0:T(8,128)S(1)} %pass_on.2.after), channel_id=1, source_target_pairs={{0,4},{4,8},{8,12},{12,16},{16,20},{20,24},{24,28},{28,0},{1,5},{5... | collective-permute-start | bytes 270344 | tf_op jit(solution)/shard_map/ppermute | solution.py:985
  41.4 24.9 %collective-permute-start.10 = (f32[768,128]{1,0:T(8,128)S(1)}, f32[768,128]{1,0:T(8,128)S(1)}, u32[]{:S(2)}, u32[]{:S(2)}) collective-permute-start(f32[768,128]{1,0:T(8,128)S(1)} %get-tuple-element.63), channel_id=1, source_target_pairs={{0,1},{1,2},{2,3},{3,0},{4,5},{5,6},{6,7},{7,4},{8,9},{9,10},{10,1... | collective-permute-start | bytes 1179656 | tf_op jit(solution)/shard_map/ppermute | solution.py:985
  41.4 24.9 %collective-permute-start.11 = (f32[768,128]{1,0:T(8,128)S(1)}, f32[768,128]{1,0:T(8,128)S(1)}, u32[]{:S(2)}, u32[]{:S(2)}) collective-permute-start(f32[768,128]{1,0:T(8,128)S(1)} %get-tuple-element.64), channel_id=1, source_target_pairs={{0,3},{1,0},{2,1},{3,2},{4,7},{5,4},{6,5},{7,6},{8,11},{9,8},{10,9... | collective-permute-start | bytes 1179656 | tf_op jit(solution)/shard_map/ppermute | solution.py:985
  45.7 20.6 %copy-start.3 = (f32[8,8,8,512]{3,2,1,0:T(8,128)S(1)}, f32[8,8,8,512]{3,2,1,0:T(8,128)}, u32[]{:S(2)}) copy-start(f32[8,8,8,512]{3,2,1,0:T(8,128)} %param.9) | copy-start | bytes 3145732
  48.6 17.7 %collective-permute-start.8 = (f32[768,128]{1,0:T(8,128)S(1)}, f32[768,128]{1,0:T(8,128)S(1)}, u32[]{:S(2)}, u32[]{:S(2)}) collective-permute-start(f32[768,128]{1,0:T(8,128)S(1)} %get-tuple-element.62), channel_id=1, source_target_pairs={{0,4},{4,8},{8,12},{12,16},{16,20},{20,24},{24,28},{28,0},{1,5},{5... | collective-permute-start | bytes 1179656 | tf_op jit(solution)/shard_map/ppermute | solution.py:985
  49.3 17.1 %collective-permute-start.9 = (f32[768,128]{1,0:T(8,128)S(1)}, f32[768,128]{1,0:T(8,128)S(1)}, u32[]{:S(2)}, u32[]{:S(2)}) collective-permute-start(f32[768,128]{1,0:T(8,128)S(1)} %get-tuple-element.57.after), channel_id=1, source_target_pairs={{0,28},{4,0},{8,4},{12,8},{16,12},{20,16},{24,20},{28,24},{1,29},{... | collective-permute-start | bytes 1179656 | tf_op jit(solution)/shard_map/ppermute | solution.py:985
  51.3 8.3 %collective-permute-start.6 = (f32[176,128]{1,0:T(8,128)S(1)}, f32[176,128]{1,0:T(8,128)S(1)}, u32[]{:S(2)}, u32[]{:S(2)}) collective-permute-start(f32[176,128]{1,0:T(8,128)S(1)} %get-tuple-element.54.after), channel_id=1, source_target_pairs={{0,28},{4,0},{8,4},{12,8},{16,12},{20,16},{24,20},{28,24},{1,29},{... | collective-permute-start | bytes 270344 | tf_op jit(solution)/shard_map/ppermute | solution.py:985
  59.6 6.7 %collective-permute-start.7 = (f32[176,128]{1,0:T(8,128)S(1)}, f32[176,128]{1,0:T(8,128)S(1)}, u32[]{:S(2)}, u32[]{:S(2)}) collective-permute-start(f32[176,128]{1,0:T(8,128)S(1)} %pass_on.3.after), channel_id=1, source_target_pairs={{0,3},{1,0},{2,1},{3,2},{4,7},{5,4},{6,5},{7,6},{8,11},{9,8},{10,9... | collective-permute-start | bytes 270344 | tf_op jit(solution)/shard_map/ppermute | solution.py:985
  69.0 17.6 %collective-permute-start.12 = (f32[256,128]{1,0:T(8,128)S(1)}, f32[256,128]{1,0:T(8,128)S(1)}, u32[]{:S(2)}, u32[]{:S(2)}) collective-permute-start(f32[256,128]{1,0:T(8,128)S(1)} %get-tuple-element.66), channel_id=1, source_target_pairs={{0,4},{4,8},{8,12},{12,16},{16,20},{20,24},{24,28},{28,0},{1,5},{5... | collective-permute-start | bytes 393224 | tf_op jit(solution)/shard_map/ppermute | solution.py:985
  71.4 15.2 %collective-permute-start.14 = (f32[256,128]{1,0:T(8,128)S(1)}, f32[256,128]{1,0:T(8,128)S(1)}, u32[]{:S(2)}, u32[]{:S(2)}) collective-permute-start(f32[256,128]{1,0:T(8,128)S(1)} %get-tuple-element.68), channel_id=1, source_target_pairs={{0,1},{1,2},{2,3},{3,0},{4,5},{5,6},{6,7},{7,4},{8,9},{9,10},{10,1... | collective-permute-start | bytes 393224 | tf_op jit(solution)/shard_map/ppermute | solution.py:985
  73.1 13.4 %collective-permute-start.15 = (f32[256,128]{1,0:T(8,128)S(1)}, f32[256,128]{1,0:T(8,128)S(1)}, u32[]{:S(2)}, u32[]{:S(2)}) collective-permute-start(f32[256,128]{1,0:T(8,128)S(1)} %get-tuple-element.69), channel_id=1, source_target_pairs={{0,3},{1,0},{2,1},{3,2},{4,7},{5,4},{6,5},{7,6},{8,11},{9,8},{10,9... | collective-permute-start | bytes 393224 | tf_op jit(solution)/shard_map/ppermute | solution.py:985
  75.2 11.4 %collective-permute-start.13 = (f32[256,128]{1,0:T(8,128)S(1)}, f32[256,128]{1,0:T(8,128)S(1)}, u32[]{:S(2)}, u32[]{:S(2)}) collective-permute-start(f32[256,128]{1,0:T(8,128)S(1)} %get-tuple-element.67.rest_4_), channel_id=1, source_target_pairs={{0,28},{4,0},{8,4},{12,8},{16,12},{20,16},{24,20},{28,24},{1,29},{... | collective-permute-start | bytes 393224 | tf_op jit(solution)/shard_map/ppermute | solution.py:985

commit v3 on v2

--- a/solution.py
+++ b/solution.py
@@ -15,7 +15,8 @@
 RELAX = 0.6
 LANES = 128
 INNER = 6
-EARLY = 4
+SUB_EARLY = 5
+DOM_EARLY = 7
 
 NT = (((1,), (1,)), ((), ()))
 VMEM = pl.BlockSpec(memory_space=pltpu.VMEM)
@@ -25,7 +26,7 @@
 HBM = pl.BlockSpec(memory_space=pltpu.HBM)
 LARGE = pltpu.CompilerParams(vmem_limit_bytes=24 << 20)
 SMALL = pltpu.CompilerParams(vmem_limit_bytes=16 << 20)
-STRIP = 64
+STRIP = 256
 F32 = jnp.float32
 BF16 = jnp.bfloat16
 I32 = jnp.int32
@@ -153,35 +154,41 @@
 
 def pack_block(ref, start, block, source_row, outs, to):
     half = block // 2
-    source = jnp.broadcast_to(source_row, (STRIP, LANES))
+    source = jnp.broadcast_to(source_row, (half, LANES))
     low, high = source & (LANES - 1), source >> 7
-    for row in range(0, half, STRIP):
-        top = pick_columns(ref, slice(start + row, start + row + STRIP), low, high)
-        bottom = pick_columns(ref, slice(start + half + row, start + half + row + STRIP), low, high)
-        for out, message in zip(outs, pack_pair(top, bottom)):
-            out[to + row : to + row + STRIP, :] = message
-
-
-def land_block(ref, start, block, landing_row, messages, at, out, to):
-    half = block // 2
-    size = ref.shape[1]
-    spots = []
-    for c in range(0, size, LANES):
-        spot = jnp.broadcast_to(landing_row[:, c : c + LANES], (STRIP, LANES))
-        spots.append((spot < 0, spot & (LANES - 1), spot >> 7))
-    for row in range(0, half, STRIP):
-        parts = [message[at + row : at + row + STRIP, :] for message in messages]
-        pairs = [pack_pair(parts[0], parts[1]), pack_pair(parts[2], parts[3])]
-        for side in range(2):
-            tiles = [pair[side] for pair in pairs]
-            first = start + side * half + row
-            last = to + side * half + row
-            for number, (stays, low, high) in enumerate(spots):
-                lanes = slice(number * LANES, (number + 1) * LANES)
-                got = gather_tiles(tiles, low, high)
-                out[last : last + STRIP, lanes] = jnp.where(
-                    stays, ref[first : first + STRIP, lanes], got
-                )
+    top = pick_columns(ref, slice(start, start + half), low, high)
+    bottom = pick_columns(ref, slice(start + half, start + block), low, high)
+    for out, message in zip(outs, pack_pair(top, bottom)):
+        out[to : to + half, :] = message
+
+
+def arrival_spots(landing_row):
+    return jnp.concatenate([one_hot_rows(landing_row, 0, 4 * MOVE)] * 3, axis=0)
+
+
+def split_exactly(values):
+    parts = []
+    for _ in range(3):
+        parts.append(values.astype(BF16))
+        values = values - parts[-1].astype(F32)
+    return jnp.concatenate(parts, axis=1)
+
+
+def land_block(ref, start, block, landing_row, spots, messages, ats, out, to):
+    land_strips(ref, start, block // 2, 0, block // 2, landing_row, spots, messages, ats, out, to)
+
+
+def land_strips(ref, start, half, from_row, to_row, landing_row, spots, messages, ats, out, to):
+    rows = to_row - from_row
+    parts = [message[at + from_row : at + to_row, :] for message, at in zip(messages, ats)]
+    pairs = [pack_pair(parts[0], parts[1]), pack_pair(parts[2], parts[3])]
+    stays = jnp.broadcast_to(landing_row < 0, (rows, landing_row.shape[1]))
+    for side in range(2):
+        arrived = jnp.concatenate([pairs[0][side], pairs[1][side]], axis=1)
+        got = dot(split_exactly(arrived), spots)
+        first = side * half + from_row
+        held = ref[start + first : start + first + rows, :]
+        out[to + first : to + first + rows, :] = jnp.where(stays, held, got)
 
 
 def move_plan(owner, place):
@@ -235,18 +242,20 @@
         fetch(metric, held, sems, number, (first + number) * block, block, number * block).start()
 
 
-def plan_and_pack_kernel(place, owner, metric, source_ref, landing_ref, *rest, block):
-    *outs, held, sems = rest
+def plan_and_pack_kernel(place, owner_hbm, metric, source_ref, landing_ref, *rest, block):
+    *outs, held, sems, owner, owner_sem = rest
+    copy = pltpu.make_async_copy(owner_hbm, owner, owner_sem)
+    copy.start()
     fetch_parts(metric, 0, held, sems, block)
+    copy.wait()
     source, landing = move_plan(owner[...], place)
     source_ref[...] = source
     landing_ref[...] = landing
     send_parts(metric, 0, source[:, LANES:], outs, held, sems, block)
 
 
-def pack_kernel(source, metric, after, *rest, first, pair, block):
-    del after
-    *outs, held, sems = rest
+def pack_kernel(source, metric, *rest, first, pair, block):
+    *outs, held, sems = rest[-4:]
     fetch_parts(metric, first, held, sems, block)
     lanes = slice(pair * LANES, (pair + 1) * LANES)
     send_parts(metric, first, source[:, lanes], outs, held, sems, block)
@@ -260,14 +269,14 @@
 
 def plan_and_pack(place, owner, metric_rows, block):
     size = metric_rows.shape[1]
-    outs, scratch = sent_shapes(EARLY, block, size)
+    outs, scratch = sent_shapes(SUB_EARLY, block, size)
     plan = [jax.ShapeDtypeStruct((1, 4 * MOVE), I32), jax.ShapeDtypeStruct((1, size), I32)]
     return pl.pallas_call(
         functools.partial(plan_and_pack_kernel, block=block),
-        in_specs=[SMEM, VMEM, HBM],
+        in_specs=[SMEM, HBM, HBM],
         out_specs=[VMEM] * 4,
         out_shape=plan + outs,
-        scratch_shapes=scratch,
+        scratch_shapes=scratch + [pltpu.VMEM((1, size), I32), pltpu.SemaphoreType.DMA],
         name="plan_and_pack",
         cost_estimate=QUICK,
         compiler_params=LARGE,
@@ -278,45 +287,64 @@
     outs, scratch = sent_shapes(count, block, metric_rows.shape[1])
     return pl.pallas_call(
         functools.partial(pack_kernel, first=first, pair=pair, block=block),
-        in_specs=[VMEM, HBM, ANY],
+        in_specs=[VMEM, HBM] + [ANY] * len(after),
         out_specs=[VMEM] * 2,
         out_shape=outs,
         scratch_shapes=scratch,
         name=name,
         cost_estimate=QUICK,
         compiler_params=LARGE,
-    )(source, metric_rows, after)
-
-
-def land_metric_kernel(landing, metric, *rest, first, block):
-    messages = rest[:4]
-    out, held, ready, sems, out_sems = rest[-5:]
+    )(source, metric_rows, *after)
+
+
+def land_metric_kernel(landing, metric, *rest, first, block, spots):
+    *messages, out, token, held, ready, sems, out_sems = rest
+    token[...] = jnp.zeros_like(token)
+    columns = arrival_spots(landing[...])
     count = held.shape[0] // block
     fetch_parts(metric, first, held, sems, block)
     for number in range(count):
         start = number * block
+        parts, at = spots[number]
         fetch(metric, held, sems, number, (first + number) * block, block, start).wait()
-        land_block(held, start, block, landing[...], messages, start // 2, ready, start)
+        land_block(
+            held, start, block, landing[...], columns, [messages[k] for k in parts], at, ready, start
+        )
         fetch(ready, out, out_sems, number, start, block, (first + number) * block).start()
     for number in range(count):
         start = number * block
         fetch(ready, out, out_sems, number, start, block, (first + number) * block).wait()
 
 
-def land_metric(landing, metric_rows, arrived, first, count, block, before, after, name):
+def land_metric(landing, metric_rows, dom, sub, first, count, block, before, after, name):
     size = metric_rows.shape[1]
-    operands = [landing, metric_rows, *arrived, after]
-    specs = [VMEM, HBM] + [VMEM] * 4 + [ANY]
+    messages, spots = [], []
+    for number in range(first, first + count):
+        parts, ats = [], None
+        for (early, late), limit in ((dom, DOM_EARLY), (sub, SUB_EARLY)):
+            chosen, local = (early, number) if number < limit else (late, number - limit)
+            for message in chosen:
+                known = [k for k, other in enumerate(messages) if other is message]
+                if not known:
+                    messages.append(message)
+                parts.append(known[0] if known else len(messages) - 1)
+            ats = (ats or []) + [local * block // 2] * 2
+        spots.append((parts, ats))
+    operands = [landing, metric_rows, *messages, after]
+    specs = [VMEM, HBM] + [VMEM] * len(messages) + [ANY]
     aliases = {}
     if before is not None:
+        aliases = {len(operands): 0}
         operands.append(before)
         specs.append(HBM)
-        aliases = {7: 0}
-    return pl.pallas_call(
-        functools.partial(land_metric_kernel, first=first, block=block),
+    return pl.pallas_call(
+        functools.partial(land_metric_kernel, first=first, block=block, spots=spots),
         in_specs=specs,
-        out_specs=HBM,
-        out_shape=jax.ShapeDtypeStruct(metric_rows.shape, F32),
+        out_specs=[HBM, VMEM],
+        out_shape=[
+            jax.ShapeDtypeStruct(metric_rows.shape, F32),
+            jax.ShapeDtypeStruct((8, LANES), F32),
+        ],
         scratch_shapes=[
             pltpu.VMEM((count * block, size), F32),
             pltpu.VMEM((count * block, size), F32),
@@ -330,21 +358,37 @@
     )(*operands)
 
 
-def land_field_kernel(landing, relaxed, first, second, third, fourth, out):
+def land_field_kernel(landing, relaxed, first, second, third, fourth, after, out, ready, sems):
+    del after
     rows = relaxed.shape[0]
-    land_block(relaxed, 0, rows, landing[...], (first, second, third, fourth), 0, out, 0)
-
-
-def land_field(landing, relaxed, arrived):
+    piece = rows // 8
+    half = rows // 2
+    messages = (first, second, third, fourth)
+    copies = []
+    columns = arrival_spots(landing[...])
+    for row in range(0, half, piece):
+        land_strips(
+            relaxed, 0, half, row, row + piece, landing[...], columns, messages, [0] * 4, ready, 0
+        )
+        for side in range(2):
+            copies.append(fetch(ready, out, sems, len(copies), side * half + row, piece, side * half + row))
+            copies[-1].start()
+    for copy in copies:
+        copy.wait()
+
+
+def land_field(landing, relaxed, arrived, after):
+    count = 8
     return pl.pallas_call(
         land_field_kernel,
-        in_specs=[VMEM] * 6,
-        out_specs=VMEM,
+        in_specs=[VMEM] * 6 + [ANY],
+        out_specs=HBM,
         out_shape=jax.ShapeDtypeStruct(relaxed.shape, F32),
+        scratch_shapes=[pltpu.VMEM(relaxed.shape, F32), pltpu.SemaphoreType.DMA((count,))],
         name="land_field",
         cost_estimate=QUICK,
         compiler_params=SMALL,
-    )(landing, relaxed, *arrived)
+    )(landing, relaxed, *arrived, after)
 
 
 FACE_DOM = EY * EZ
@@ -911,8 +955,8 @@
 
 
 def merge_own(column, tables, image, diagonal, after):
-    def kernel(column, faces, edges, corners, image_in, diagonal_in, after, image, diagonal):
-        del after
+    def kernel(column, faces, edges, corners, image_in, diagonal_in, *rest):
+        image, diagonal = rest[-2:]
         image[...] = image_in[...]
         diagonal[...] = diagonal_in[...]
         merge_faces(column, table_tiles(faces), 0, image, diagonal)
@@ -921,31 +965,31 @@
 
     return pl.pallas_call(
         kernel,
-        in_specs=[VMEM] * 6 + [ANY],
+        in_specs=[VMEM] * 6 + [ANY] * len(after),
         out_specs=[VMEM] * 2,
         out_shape=[jax.ShapeDtypeStruct(image.shape, F32)] * 2,
         name="merge_own",
         cost_estimate=QUICK,
         compiler_params=SMALL,
-    )(column, *tables, image, diagonal, after)
+    )(column, *tables, image, diagonal, *after)
 
 
 def merge_dom(column, message, image, diagonal, after):
-    def kernel(column, message, image_in, diagonal_in, after, image, diagonal):
-        del after
+    def kernel(column, message, image_in, diagonal_in, *rest):
+        image, diagonal = rest[-2:]
         image[...] = image_in[...]
         diagonal[...] = diagonal_in[...]
         merge_message(column, message, 1, image, diagonal)
 
     return pl.pallas_call(
         kernel,
-        in_specs=[VMEM] * 4 + [ANY],
+        in_specs=[VMEM] * 4 + [ANY] * len(after),
         out_specs=[VMEM] * 2,
         out_shape=[jax.ShapeDtypeStruct(image.shape, F32)] * 2,
         name="merge_dom",
         cost_estimate=QUICK,
         compiler_params=SMALL,
-    )(column, message, image, diagonal, after)
+    )(column, message, image, diagonal, *after)
 
 
 def relax_kernel(column, message, image_in, diagonal_in, field, forcing, source, *rest):
@@ -994,45 +1038,45 @@
     place = devices()
     table = derivative_table(solution.shape[0] - 1)
     field = solution.reshape(-1, size)
-    metric_rows = metric.reshape(-1, size)
+    metric_rows = pltpu.with_memory_space_constraint(metric.reshape(-1, size), pltpu.HBM)
     components = metric.shape[0]
     block = metric_rows.shape[0] // components
-    late = components - EARLY
     source, landing, *messages = plan_and_pack(place, new_owner.reshape(1, size), metric_rows, block)
     sub_early = swapped(*messages, "sub")
-    messages = pack(source, metric_rows, 0, EARLY, 0, block, landing, "pack_dom_early")
+    messages = pack(source, metric_rows, 0, DOM_EARLY, 0, block, (landing,), "pack_dom")
     dom_early = swapped(*messages, "dom")
     image, diagonal, column, *tables, dom, sub = apply_and_pack(
         place, entity_ids, field, metric_rows, messages[0], table
     )
     got_sub = shifted(sub, "sub", 1)
-    messages = pack(source, metric_rows, EARLY, late, 1, block, sub, "pack_sub_late")
+    messages = pack(
+        source, metric_rows, SUB_EARLY, components - SUB_EARLY, 1, block, (sub,), "pack_sub_late"
+    )
     sub_late = swapped(*messages, "sub")
-    dom = pass_on(dom, got_sub, dom_early + sub_early)
+    dom = pass_on(dom, got_sub, (*sub_early, messages[0]))
     got_dom = shifted(dom, "dom", 1)
     tables = add_sub(tables, got_sub, dom)
     *tables, dom_back = add_dom(tables, got_dom)
     back_dom = shifted(dom_back, "dom", -1)
-    messages = pack(source, metric_rows, EARLY, late, 0, block, dom_back, "pack_dom_late")
-    dom_late = swapped(*messages, "dom")
     sub_back = read_sub(tables, got_sub)
+    image, diagonal = merge_own(column, tables, image, diagonal, (dom_back, *dom_early))
     sub_back = pass_on(sub_back, back_dom)
     back_sub = shifted(sub_back, "sub", -1)
-    image, diagonal = merge_own(column, tables, image, diagonal, messages[0])
-    image, diagonal = merge_dom(column, back_dom, image, diagonal, sub_back)
+    image, diagonal = merge_dom(column, back_dom, image, diagonal, sub_late)
+    dom_moves, sub_moves = (dom_early, ()), (sub_early, sub_late)
+    moved, token = land_metric(
+        landing, metric_rows, dom_moves, sub_moves, 0, SUB_EARLY, block, None, image, "land_early"
+    )
     relaxed, *leaving = relax_and_pack(
-        column, back_sub, image, diagonal, field, forcing.reshape(-1, size), source,
-        dom_late + sub_late,
+        column, back_sub, image, diagonal, field, forcing.reshape(-1, size), source, (token,)
     )
     got_sub = swapped(*leaving[2:], "sub")
     got_dom = swapped(*leaving[:2], "dom")
-    moved = land_metric(
-        landing, metric_rows, dom_early + sub_early, 0, EARLY, block, None, leaving[0], "land_early"
-    )
-    moved = land_metric(
-        landing, metric_rows, dom_late + sub_late, EARLY, late, block, moved, leaving[0], "land_late"
-    )
-    smoothed = land_field(landing, relaxed, got_dom + got_sub)
+    moved, token = land_metric(
+        landing, metric_rows, dom_moves, sub_moves, SUB_EARLY, components - SUB_EARLY, block, moved,
+        leaving[0], "land_late",
+    )
+    smoothed = land_field(landing, relaxed, got_dom + got_sub, token)
     return smoothed.reshape(solution.shape), moved.reshape(metric.shape)
 
 

time: 89.1 us -> 78.5 us (0.88)
  waiting for transfers between devices: 14.2 us -> 9.8 us
  local copies, waits for them, and re-layouts: 3.91 us -> 0.8 us
  Pallas kernels: 48.7 us -> 46.6 us
  starting transfers between devices: 21 us -> 20.1 us
    ppermute x16 -> x14, waiting for transfers between devices: 14.2 us -> 9.8 us  [shifted(): lax.ppermute(value, axis, [(i, (i + steps) % count) for i in range(count)])]
    unnamed x18 -> x14, local copies, waits for them, and re-layouts: 3.82 us -> 0.71 us
    pallas_call x2, Pallas kernels: 11.3 us -> 8.89 us  [land_metric(): pl.pallas_call(functools.partial(land_metric_kernel, first=first, block=b...]
    pallas_call x1, Pallas kernels: 13.3 us -> 14.8 us  [apply_and_pack(): pl.pallas_call(functools.partial(apply_kernel, table=table), in_specs=[SM...]
    ppermute x16 -> x14, starting transfers between devices: 21 us -> 20.1 us  [shifted(): lax.ppermute(value, axis, [(i, (i + steps) % count) for i in range(count)])]
    pallas_call x3 -> x2, Pallas kernels: 7.26 us -> 6.51 us  [pack(): pl.pallas_call(functools.partial(pack_kernel, first=first, pair=pair, blo...]
  transfers between devices with their start and end apart: 16 -> 14, of which waited for: 2 -> 4; matrix products, arithmetic and copies ran while one was open for 0% -> 0% of each run, Pallas kernels for 45% -> 49%
where the time goes in v3:
time: 78.5 us; the launch traced here: 78.3 us
  Pallas kernels  46.6 us (59%)
  starting transfers between devices  20.1 us (26%)
  waiting for transfers between devices  9.8 us (12%)
  between operations  1.04 us (1%)
  local copies, waits for them, and re-layouts  0.8 us (1%)
    ppermute x14, starting transfers between devices, shifted(): lax.ppermute(value, axis, [(i, (i + steps) % count) for i in range(count)])  20.1 us
    pallas_call x1, Pallas kernels, apply_and_pack(): pl.pallas_call(functools.partial(apply_kernel, table=table), in_specs=[SM...  14.8 us
    ppermute x14, waiting for transfers between devices, shifted(): lax.ppermute(value, axis, [(i, (i + steps) % count) for i in range(count)])  9.8 us
    pallas_call x2, Pallas kernels, land_metric(): pl.pallas_call(functools.partial(land_metric_kernel, first=first, block=b...  8.89 us
    pallas_call x2, Pallas kernels, pack(): pl.pallas_call(functools.partial(pack_kernel, first=first, pair=pair, blo...  6.51 us
    pallas_call x1, Pallas kernels, merge_own(): pl.pallas_call(kernel, in_specs=[VMEM] * 6 + [ANY] * len(after), out_spec...  5.41 us
    pallas_call x1, Pallas kernels, plan_and_pack(): pl.pallas_call(functools.partial(plan_and_pack_kernel, block=block), in_s...  4.03 us
    pallas_call x1, Pallas kernels, relax_and_pack(): pl.pallas_call(relax_kernel, in_specs=[VMEM] * 7 + [ANY] * len(after), ou...  2.18 us
  transfers between devices with their start and end apart: 14, of which 4 were waited for; matrix products, arithmetic and copies ran while one was open for 0% of the time, Pallas kernels for 49%

profile of v3, /device:TPU:0, one launch (start us, length us, event | category | flops | bytes accessed | tf_op | source)
XLA Modules:
  0.0 78.3 jit_solution(4578245026093771660)
XLA Ops:
  0.6 0.1 stack.27.place
  0.7 0.7 copy-done.6
  1.4 4.0 %plan_and_pack.1 = (s32[1,256]{1,0:T(1,128)S(1)}, s32[1,512]{1,0:T(1,128)S(1)}, f32[1280,128]{1,0:T(8,128)S(1)}, f32[1280,128]{1,0:T(8,128)S(1)}) custom-call(s32[6]{0:T(128)S(1)} %stack.27.place, s32[1,512]{1,0:T(1,128)S(1)} %bitcast.15, f32[3584,512]{1,0:T(8,128)} %bitcast.16), custom_call_target="tpu_custom_call" | custom-call | flops 1000 | bytes 1000 | tf_op jit(solution)/shard_map/plan_and_pack/pallas_call | solution.py:274
  5.5 3.1 %collective-permute-start.1 = (f32[1280,128]{1,0:T(8,128)S(1)}, f32[1280,128]{1,0:T(8,128)S(1)}, u32[]{:S(2)}, u32[]{:S(2)}) collective-permute-start(f32[1280,128]{1,0:T(8,128)S(1)} %get-tuple-element.47), channel_id=1, source_target_pairs={{0,1},{1,2},{2,3},{3,0},{4,5},{5,6},{6,7},{7,4},{8,9},{9,10},{10,1... | collective-permute-start | bytes 1966088 | tf_op jit(solution)/shard_map/ppermute | solution.py:1029
  8.5 2.1 %collective-permute-start.2 = (f32[1280,128]{1,0:T(8,128)S(1)}, f32[1280,128]{1,0:T(8,128)S(1)}, u32[]{:S(2)}, u32[]{:S(2)}) collective-permute-start(f32[1280,128]{1,0:T(8,128)S(1)} %get-tuple-element.48), channel_id=1, source_target_pairs={{0,3},{1,0},{2,1},{3,2},{4,7},{5,4},{6,5},{7,6},{8,11},{9,8},{10,9... | collective-permute-start | bytes 1966088 | tf_op jit(solution)/shard_map/ppermute | solution.py:1029
  10.6 4.4 %pack_dom.1 = (f32[1792,128]{1,0:T(8,128)S(1)}, f32[1792,128]{1,0:T(8,128)S(1)}) custom-call(s32[1,256]{1,0:T(1,128)S(1)} %get-tuple-element.39.source, f32[3584,512]{1,0:T(8,128)} %bitcast.17, s32[1,512]{1,0:T(1,128)S(1)} %get-tuple-element.38.rest_0_.landing), custom_call_target="tpu_custom_call" | custom-call | flops 1000 | bytes 1000 | tf_op jit(solution)/shard_map/pack_dom/pallas_call | solution.py:288
  15.0 0.1 collective-permute-start.6
  15.1 2.6 %collective-permute-start.7 = (f32[1792,128]{1,0:T(8,128)S(1)}, f32[1792,128]{1,0:T(8,128)S(1)}, u32[]{:S(2)}, u32[]{:S(2)}) collective-permute-start(f32[1792,128]{1,0:T(8,128)S(1)} %get-tuple-element.40.after), channel_id=1, source_target_pairs={{0,28},{4,0},{8,4},{12,8},{16,12},{20,16},{24,20},{28,24},{1,29},{... | collective-permute-start | bytes 2752520 | tf_op jit(solution)/shard_map/ppermute | solution.py:1029
  17.7 14.8 %apply_and_pack.1 = (f32[4,512,128]{2,1,0:T(8,128)S(1)}, f32[4,512,128]{2,1,0:T(8,128)S(1)}, s32[26,512]{1,0:T(8,128)S(1)}, f32[96,1536]{1,0:T(8,128)S(1)}, f32[...) custom-call(s32[6]{0:T(128)S(1)} %stack.27.place, ...), custom_call_target="tpu_custom_call" | custom-call | flops 1000 | bytes 1000 | tf_op jit(solution)/shard_map/apply_and_pack/pallas_call | solution.py:736
  32.5 0.1 collective-permute-start
  32.6 2.1 %pack_sub_late.1 = (f32[512,128]{1,0:T(8,128)S(1)}, f32[512,128]{1,0:T(8,128)S(1)}) custom-call(s32[1,256]{1,0:T(1,128)S(1)} %get-tuple-element.39.source, f32[3584,512]{1,0:T(8,128)} %bitcast.19, f32[176,128]{1,0:T(8,128)S(1)} %get-tuple-element.45.rest_0_), custom_call_target="tpu_custom_call" | custom-call | flops 1000 | bytes 1000 | tf_op jit(solution)/shard_map/pack_sub_late/pallas_call | solution.py:288
  34.8 6.6 %collective-permute-done.received.message = f32[176,128]{1,0:T(8,128)S(1)} collective-permute-done((f32[176,128]{1,0:T(8,128)S(1)}, f32[176,128]{1,0:T(8,128)S(1)}, u32[]{:S(2)}, u32[]{:S(2)}) %collective-permute-start) | collective-permute-done | bytes 90144 | tf_op jit(solution)/shard_map/ppermute | solution.py:1029
  41.4 0.1 collective-permute-start.8
  41.5 3.8 %collective-permute-start.9 = (f32[512,128]{1,0:T(8,128)S(1)}, f32[512,128]{1,0:T(8,128)S(1)}, u32[]{:S(2)}, u32[]{:S(2)}) collective-permute-start(f32[512,128]{1,0:T(8,128)S(1)} %get-tuple-element.49.rest_2_), channel_id=1, source_target_pairs={{0,3},{1,0},{2,1},{3,2},{4,7},{5,4},{6,5},{7,6},{8,11},{9,8},{10,9... | collective-permute-start | bytes 786440 | tf_op jit(solution)/shard_map/ppermute | solution.py:1029
  45.3 0.5 add_sub.1
  45.8 0.5 collective-permute-done.3.message
  46.3 0.7 add_dom.1
  46.9 1.6 %collective-permute-start.4 = (f32[176,128]{1,0:T(8,128)S(1)}, f32[176,128]{1,0:T(8,128)S(1)}, u32[]{:S(2)}, u32[]{:S(2)}) collective-permute-start(f32[176,128]{1,0:T(8,128)S(1)} %get-tuple-element.56.rest_0_), channel_id=1, source_target_pairs={{0,28},{4,0},{8,4},{12,8},{16,12},{20,16},{24,20},{28,24},{1,29},{... | collective-permute-start | bytes 270344 | tf_op jit(solution)/shard_map/ppermute | solution.py:1029
  48.5 0.4 read_sub.1.message
  48.9 1.8 %collective-permute-done.4.received.message = f32[176,128]{1,0:T(8,128)S(1)} collective-permute-done((f32[176,128]{1,0:T(8,128)S(1)}, f32[176,128]{1,0:T(8,128)S(1)}, u32[]{:S(2)}, u32[]{:S(2)}) %collective-permute-start.4) | collective-permute-done | bytes 90144 | tf_op jit(solution)/shard_map/ppermute | solution.py:1029
  50.7 0.6 collective-permute-start.5
  51.3 5.4 %merge_own.1 = (f32[4,512,128]{2,1,0:T(8,128)S(1)}, f32[4,512,128]{2,1,0:T(8,128)S(1)}) custom-call(s32[26,512]{1,0:T(8,128)S(1)} %get-tuple-element.41.column, f32[96,1536]{1,0:T(8,128)S(1)} %get-tuple-element.53.faces, f32[16,1536]{1,0:T(8,128)S(1)} %get-tuple-element.54.edges, f32[8,512]{1,0:T(8,128)S(1)} %get-tuple-element.55.corners, ...), custom_call_target="tpu_custom_call" | custom-call | flops 1000 | bytes 1000 | tf_op jit(solution)/shard_map/merge_own/pallas_call | solution.py:966
  56.7 1.2 %merge_dom.1 = (f32[4,512,128]{2,1,0:T(8,128)S(1)}, f32[4,512,128]{2,1,0:T(8,128)S(1)}) custom-call(s32[26,512]{1,0:T(8,128)S(1)} %get-tuple-element.41.column, f32[176,128]{1,0:T(8,128)S(1)} %collective-permute-done.4.received.message, f32[4,512,128]{2,1,0:T(8,128)S(1)} %get-tuple-element.60.image_in, f32[4,512,128]{2,1,0:T(8,128)S(1)} %get-tuple-element.61.diagonal_in, ...), custom_call_target="tpu_custom_call" | custom-call | flops 1000 | bytes 1000 | tf_op jit(solution)/shard_map/merge_dom/pallas_call | solution.py:984
  57.9 5.4 %land_early.1 = (f32[3584,512]{1,0:T(8,128)}, f32[8,128]{1,0:T(8,128)S(1)}) custom-call(s32[1,512]{1,0:T(1,128)S(1)} %get-tuple-element.38.rest_0_.landing, f32[3584,512]{1,0:T(8,128)} %bitcast.20, f32[1792,128]{1,0:T(8,128)S(1)} %collective-permute-done.6.rest_1_.rest_0_, f32[1792,128]{1,0:T(8,128)S(1)} %collective-permute-done.7.rest_2_.rest_1_, ...), custom_call_target="tpu_custom_call" | custom-call | flops 1000 | bytes 1000 | tf_op jit(solution)/shard_map/land_early/pallas_call | solution.py:340
  63.3 2.2 %relax_and_pack.1 = (f32[512,512]{1,0:T(8,128)S(1)}, f32[256,128]{1,0:T(8,128)S(1)}, f32[256,128]{1,0:T(8,128)S(1)}, f32[256,128]{1,0:T(8,128)S(1)}, f32[256,128]{1,0:T(8,128)S(1)}) custom-call(s32[26,512]{1,0:T(8,128)S(1)} %get-tuple-element.41.column, f32[176,128]{1,0:T(8,128)S(1)} %collective-permute-done.5.message, ...), custom_call_target="tpu_custom_call" | custom-call | flops 1000 | bytes 1000 | tf_op jit(solution)/shard_map/relax_and_pack/pallas_call | solution.py:1015
  65.5 0.9 %collective-permute-start.10 = (f32[256,128]{1,0:T(8,128)S(1)}, f32[256,128]{1,0:T(8,128)S(1)}, u32[]{:S(2)}, u32[]{:S(2)}) collective-permute-start(f32[256,128]{1,0:T(8,128)S(1)} %get-tuple-element.67), channel_id=1, source_target_pairs={{0,4},{4,8},{8,12},{12,16},{16,20},{20,24},{24,28},{28,0},{1,5},{5... | collective-permute-start | bytes 393224 | tf_op jit(solution)/shard_map/ppermute | solution.py:1029
  66.4 1.7 %collective-permute-start.12 = (f32[256,128]{1,0:T(8,128)S(1)}, f32[256,128]{1,0:T(8,128)S(1)}, u32[]{:S(2)}, u32[]{:S(2)}) collective-permute-start(f32[256,128]{1,0:T(8,128)S(1)} %get-tuple-element.69), channel_id=1, source_target_pairs={{0,1},{1,2},{2,3},{3,0},{4,5},{5,6},{6,7},{7,4},{8,9},{9,10},{10,1... | collective-permute-start | bytes 393224 | tf_op jit(solution)/shard_map/ppermute | solution.py:1029
  68.1 2.1 %collective-permute-start.13 = (f32[256,128]{1,0:T(8,128)S(1)}, f32[256,128]{1,0:T(8,128)S(1)}, u32[]{:S(2)}, u32[]{:S(2)}) collective-permute-start(f32[256,128]{1,0:T(8,128)S(1)} %get-tuple-element.70), channel_id=1, source_target_pairs={{0,3},{1,0},{2,1},{3,2},{4,7},{5,4},{6,5},{7,6},{8,11},{9,8},{10,9... | collective-permute-start | bytes 393224 | tf_op jit(solution)/shard_map/ppermute | solution.py:1029
  70.2 1.4 %collective-permute-start.11 = (f32[256,128]{1,0:T(8,128)S(1)}, f32[256,128]{1,0:T(8,128)S(1)}, u32[]{:S(2)}, u32[]{:S(2)}) collective-permute-start(f32[256,128]{1,0:T(8,128)S(1)} %get-tuple-element.68.rest_4_), channel_id=1, source_target_pairs={{0,28},{4,0},{8,4},{12,8},{16,12},{20,16},{24,20},{28,24},{1,29},{... | collective-permute-start | bytes 393224 | tf_op jit(solution)/shard_map/ppermute | solution.py:1029
  71.7 3.5 %land_late.1 = (f32[3584,512]{1,0:T(8,128)}, f32[8,128]{1,0:T(8,128)S(1)}) custom-call(s32[1,512]{1,0:T(1,128)S(1)} %get-tuple-element.38.rest_0_.landing, f32[3584,512]{1,0:T(8,128)} %bitcast.21, f32[1792,128]{1,0:T(8,128)S(1)} %collective-permute-done.6.rest_1_.rest_0_, ...), custom_call_target="tpu_custom_call", output_to_operand_aliasing={{0}: (7, {})} | custom-call | flops 1000 | bytes 1000 | tf_op jit(solution)/shard_map/land_late/pallas_call | solution.py:340
  75.2 0.9 %collective-permute-done.13.fourth = f32[256,128]{1,0:T(8,128)S(1)} collective-permute-done((f32[256,128]{1,0:T(8,128)S(1)}, f32[256,128]{1,0:T(8,128)S(1)}, u32[]{:S(2)}, u32[]{:S(2)}) %collective-permute-start.13) | collective-permute-done | bytes 131104 | tf_op jit(solution)/shard_map/ppermute | solution.py:1029
  76.1 2.0 %land_field.1 = f32[512,512]{1,0:T(8,128)} custom-call(s32[1,512]{1,0:T(1,128)S(1)} %get-tuple-element.38.rest_0_.landing, f32[512,512]{1,0:T(8,128)S(1)} %get-tuple-element.66.relaxed, f32[256,128]{1,0:T(8,128)S(1)} %collective-permute-done.10.first, f32[256,128]{1,0:T(8,128)S(1)} %collective-permute-done.11.second, ...), custom_call_target="tpu_custom_call" | custom-call | flops 1000 | bytes 1000 | tf_op jit(solution)/shard_map/land_field/pallas_call | solution.py:382
  (26 shorter events, 0.1 us)
Async XLA Ops:
  0.7 0.7 copy-start.6
  1.4 16.3 %copy-start = (f32[8,8,8,512]{3,2,1,0:T(8,128)S(1)}, f32[8,8,8,512]{3,2,1,0:T(8,128)}, u32[]{:S(2)}) copy-start(f32[8,8,8,512]{3,2,1,0:T(8,128)} %param.8) | copy-start | bytes 3145732
  1.4 16.3 %copy-start.2 = (s32[26,512]{1,0:T(8,128)S(1)}, s32[26,512]{1,0:T(8,128)}, u32[]{:S(2)}) copy-start(s32[26,512]{1,0:T(8,128)} %ids.1) | copy-start | bytes 159748
  1.4 16.3 %copy-start.3 = (bf16[128,192]{1,0:T(8,128)(2,1)S(1)}, bf16[128,192]{1,0:T(8,128)(2,1)}, u32[]{:S(2)}) copy-start(bf16[128,192]{1,0:T(8,128)(2,1)} %constant.35.clone.grad_left) | copy-start | bytes 147460
  1.4 16.3 %copy-start.4 = (bf16[64,384]{1,0:T(8,128)(2,1)S(1)}, bf16[64,384]{1,0:T(8,128)(2,1)}, u32[]{:S(2)}) copy-start(bf16[64,384]{1,0:T(8,128)(2,1)} %constant.37.clone.square_left) | copy-start | bytes 147460
  1.4 16.3 %copy-start.5 = (bf16[64,384]{1,0:T(8,128)(2,1)S(1)}, bf16[64,384]{1,0:T(8,128)(2,1)}, u32[]{:S(2)}) copy-start(bf16[64,384]{1,0:T(8,128)(2,1)} %constant.36.clone.image_left) | copy-start | bytes 147460
  5.5 35.9 %collective-permute-start.1 = (f32[1280,128]{1,0:T(8,128)S(1)}, f32[1280,128]{1,0:T(8,128)S(1)}, u32[]{:S(2)}, u32[]{:S(2)}) collective-permute-start(f32[1280,128]{1,0:T(8,128)S(1)} %get-tuple-element.47), channel_id=1, source_target_pairs={{0,1},{1,2},{2,3},{3,0},{4,5},{5,6},{6,7},{7,4},{8,9},{9,10},{10,1... | collective-permute-start | bytes 1966088 | tf_op jit(solution)/shard_map/ppermute | solution.py:1029
  8.5 32.8 %collective-permute-start.2 = (f32[1280,128]{1,0:T(8,128)S(1)}, f32[1280,128]{1,0:T(8,128)S(1)}, u32[]{:S(2)}, u32[]{:S(2)}) collective-permute-start(f32[1280,128]{1,0:T(8,128)S(1)} %get-tuple-element.48), channel_id=1, source_target_pairs={{0,3},{1,0},{2,1},{3,2},{4,7},{5,4},{6,5},{7,6},{8,11},{9,8},{10,9... | collective-permute-start | bytes 1966088 | tf_op jit(solution)/shard_map/ppermute | solution.py:1029
  15.0 36.2 %collective-permute-start.6 = (f32[1792,128]{1,0:T(8,128)S(1)}, f32[1792,128]{1,0:T(8,128)S(1)}, u32[]{:S(2)}, u32[]{:S(2)}) collective-permute-start(f32[1792,128]{1,0:T(8,128)S(1)} %get-tuple-element.59), channel_id=1, source_target_pairs={{0,4},{4,8},{8,12},{12,16},{16,20},{20,24},{24,28},{28,0},{1,5},{5... | collective-permute-start | bytes 2752520 | tf_op jit(solution)/shard_map/ppermute | solution.py:1029
  15.1 36.2 %collective-permute-start.7 = (f32[1792,128]{1,0:T(8,128)S(1)}, f32[1792,128]{1,0:T(8,128)S(1)}, u32[]{:S(2)}, u32[]{:S(2)}) collective-permute-start(f32[1792,128]{1,0:T(8,128)S(1)} %get-tuple-element.40.after), channel_id=1, source_target_pairs={{0,28},{4,0},{8,4},{12,8},{16,12},{20,16},{24,20},{28,24},{1,29},{... | collective-permute-start | bytes 2752520 | tf_op jit(solution)/shard_map/ppermute | solution.py:1029
  32.5 8.8 %collective-permute-start = (f32[176,128]{1,0:T(8,128)S(1)}, f32[176,128]{1,0:T(8,128)S(1)}, u32[]{:S(2)}, u32[]{:S(2)}) collective-permute-start(f32[176,128]{1,0:T(8,128)S(1)} %get-tuple-element.45.rest_0_), channel_id=1, source_target_pairs={{0,1},{1,2},{2,3},{3,0},{4,5},{5,6},{6,7},{7,4},{8,9},{9,10},{10,1... | collective-permute-start | bytes 270344 | tf_op jit(solution)/shard_map/ppermute | solution.py:1029
  41.3 4.9 %collective-permute-start.3 = (f32[176,128]{1,0:T(8,128)S(1)}, f32[176,128]{1,0:T(8,128)S(1)}, u32[]{:S(2)}, u32[]{:S(2)}) collective-permute-start(f32[176,128]{1,0:T(8,128)S(1)} %pass_on.2.after), channel_id=1, source_target_pairs={{0,4},{4,8},{8,12},{12,16},{16,20},{20,24},{24,28},{28,0},{1,5},{5... | collective-permute-start | bytes 270344 | tf_op jit(solution)/shard_map/ppermute | solution.py:1029
  41.4 15.3 %collective-permute-start.8 = (f32[512,128]{1,0:T(8,128)S(1)}, f32[512,128]{1,0:T(8,128)S(1)}, u32[]{:S(2)}, u32[]{:S(2)}) collective-permute-start(f32[512,128]{1,0:T(8,128)S(1)} %get-tuple-element.62), channel_id=1, source_target_pairs={{0,1},{1,2},{2,3},{3,0},{4,5},{5,6},{6,7},{7,4},{8,9},{9,10},{10,1... | collective-permute-start | bytes 786440 | tf_op jit(solution)/shard_map/ppermute | solution.py:1029
  41.5 15.2 %collective-permute-start.9 = (f32[512,128]{1,0:T(8,128)S(1)}, f32[512,128]{1,0:T(8,128)S(1)}, u32[]{:S(2)}, u32[]{:S(2)}) collective-permute-start(f32[512,128]{1,0:T(8,128)S(1)} %get-tuple-element.49.rest_2_), channel_id=1, source_target_pairs={{0,3},{1,0},{2,1},{3,2},{4,7},{5,4},{6,5},{7,6},{8,11},{9,8},{10,9... | collective-permute-start | bytes 786440 | tf_op jit(solution)/shard_map/ppermute | solution.py:1029
  46.9 3.7 %collective-permute-start.4 = (f32[176,128]{1,0:T(8,128)S(1)}, f32[176,128]{1,0:T(8,128)S(1)}, u32[]{:S(2)}, u32[]{:S(2)}) collective-permute-start(f32[176,128]{1,0:T(8,128)S(1)} %get-tuple-element.56.rest_0_), channel_id=1, source_target_pairs={{0,28},{4,0},{8,4},{12,8},{16,12},{20,16},{24,20},{28,24},{1,29},{... | collective-permute-start | bytes 270344 | tf_op jit(solution)/shard_map/ppermute | solution.py:1029
  50.7 12.6 %collective-permute-start.5 = (f32[176,128]{1,0:T(8,128)S(1)}, f32[176,128]{1,0:T(8,128)S(1)}, u32[]{:S(2)}, u32[]{:S(2)}) collective-permute-start(f32[176,128]{1,0:T(8,128)S(1)} %pass_on.3), channel_id=1, source_target_pairs={{0,3},{1,0},{2,1},{3,2},{4,7},{5,4},{6,5},{7,6},{8,11},{9,8},{10,9... | collective-permute-start | bytes 270344 | tf_op jit(solution)/shard_map/ppermute | solution.py:1029
  56.7 6.7 %copy-start.1 = (f32[8,8,8,512]{3,2,1,0:T(8,128)S(1)}, f32[8,8,8,512]{3,2,1,0:T(8,128)}, u32[]{:S(2)}) copy-start(f32[8,8,8,512]{3,2,1,0:T(8,128)} %param.9) | copy-start | bytes 3145732
  65.5 9.6 %collective-permute-start.10 = (f32[256,128]{1,0:T(8,128)S(1)}, f32[256,128]{1,0:T(8,128)S(1)}, u32[]{:S(2)}, u32[]{:S(2)}) collective-permute-start(f32[256,128]{1,0:T(8,128)S(1)} %get-tuple-element.67), channel_id=1, source_target_pairs={{0,4},{4,8},{8,12},{12,16},{16,20},{20,24},{24,28},{28,0},{1,5},{5... | collective-permute-start | bytes 393224 | tf_op jit(solution)/shard_map/ppermute | solution.py:1029
  66.4 8.8 %collective-permute-start.12 = (f32[256,128]{1,0:T(8,128)S(1)}, f32[256,128]{1,0:T(8,128)S(1)}, u32[]{:S(2)}, u32[]{:S(2)}) collective-permute-start(f32[256,128]{1,0:T(8,128)S(1)} %get-tuple-element.69), channel_id=1, source_target_pairs={{0,1},{1,2},{2,3},{3,0},{4,5},{5,6},{6,7},{7,4},{8,9},{9,10},{10,1... | collective-permute-start | bytes 393224 | tf_op jit(solution)/shard_map/ppermute | solution.py:1029
  68.1 8.0 %collective-permute-start.13 = (f32[256,128]{1,0:T(8,128)S(1)}, f32[256,128]{1,0:T(8,128)S(1)}, u32[]{:S(2)}, u32[]{:S(2)}) collective-permute-start(f32[256,128]{1,0:T(8,128)S(1)} %get-tuple-element.70), channel_id=1, source_target_pairs={{0,3},{1,0},{2,1},{3,2},{4,7},{5,4},{6,5},{7,6},{8,11},{9,8},{10,9... | collective-permute-start | bytes 393224 | tf_op jit(solution)/shard_map/ppermute | solution.py:1029
  70.2 5.9 %collective-permute-start.11 = (f32[256,128]{1,0:T(8,128)S(1)}, f32[256,128]{1,0:T(8,128)S(1)}, u32[]{:S(2)}, u32[]{:S(2)}) collective-permute-start(f32[256,128]{1,0:T(8,128)S(1)} %get-tuple-element.68.rest_4_), channel_id=1, source_target_pairs={{0,28},{4,0},{8,4},{12,8},{16,12},{20,16},{24,20},{28,24},{1,29},{... | collective-permute-start | bytes 393224 | tf_op jit(solution)/shard_map/ppermute | solution.py:1029

commit v4 on v3

--- a/solution.py
+++ b/solution.py
@@ -230,53 +230,55 @@
     )
 
 
-def send_parts(metric, first, source, outs, held, sems, block):
-    half = block // 2
-    for number in range(held.shape[0] // block):
-        fetch(metric, held, sems, number, (first + number) * block, block, number * block).wait()
-        pack_block(held, number * block, block, source, outs, number * half)
-
-
-def fetch_parts(metric, first, held, sems, block):
-    for number in range(held.shape[0] // block):
-        fetch(metric, held, sems, number, (first + number) * block, block, number * block).start()
-
-
-def plan_and_pack_kernel(place, owner_hbm, metric, source_ref, landing_ref, *rest, block):
-    *outs, held, sems, owner, owner_sem = rest
+def send_part(held, first, number, source, outs, block):
+    pack_block(held, (first + number) * block, block, source, outs, number * block // 2)
+
+
+def plan_and_pack_kernel(
+    place, owner_hbm, metric, source_ref, landing_ref, first_out, second_out, held, sems, owner,
+    owner_sem, *, block,
+):
     copy = pltpu.make_async_copy(owner_hbm, owner, owner_sem)
     copy.start()
-    fetch_parts(metric, 0, held, sems, block)
+    count = held.shape[0] // block
+    copies = [fetch(metric, held, sems, c, c * block, block, c * block) for c in range(count)]
+    for part in copies:
+        part.start()
     copy.wait()
     source, landing = move_plan(owner[...], place)
     source_ref[...] = source
     landing_ref[...] = landing
-    send_parts(metric, 0, source[:, LANES:], outs, held, sems, block)
-
-
-def pack_kernel(source, metric, *rest, first, pair, block):
-    *outs, held, sems = rest[-4:]
-    fetch_parts(metric, first, held, sems, block)
+    for number, part in enumerate(copies):
+        part.wait()
+        if number < SUB_EARLY:
+            send_part(held, 0, number, source[:, LANES:], (first_out, second_out), block)
+
+
+def pack_kernel(source, held, *rest, first, pair, block):
+    outs = rest[-2:]
     lanes = slice(pair * LANES, (pair + 1) * LANES)
-    send_parts(metric, first, source[:, lanes], outs, held, sems, block)
-
-
-def sent_shapes(count, block, size):
-    outs = [jax.ShapeDtypeStruct((count * block // 2, LANES), F32)] * 2
-    scratch = [pltpu.VMEM((count * block, size), F32), pltpu.SemaphoreType.DMA((count,))]
-    return outs, scratch
+    for number in range(outs[0].shape[0] * 2 // block):
+        send_part(held, first, number, source[:, lanes], outs, block)
+
+
+def sent_shapes(count, block):
+    return [jax.ShapeDtypeStruct((count * block // 2, LANES), F32)] * 2
 
 
 def plan_and_pack(place, owner, metric_rows, block):
-    size = metric_rows.shape[1]
-    outs, scratch = sent_shapes(SUB_EARLY, block, size)
+    rows, size = metric_rows.shape
+    outs = sent_shapes(SUB_EARLY, block) + [jax.ShapeDtypeStruct((rows, size), F32)]
     plan = [jax.ShapeDtypeStruct((1, 4 * MOVE), I32), jax.ShapeDtypeStruct((1, size), I32)]
     return pl.pallas_call(
         functools.partial(plan_and_pack_kernel, block=block),
         in_specs=[SMEM, HBM, HBM],
-        out_specs=[VMEM] * 4,
+        out_specs=[VMEM] * 5,
         out_shape=plan + outs,
-        scratch_shapes=scratch + [pltpu.VMEM((1, size), I32), pltpu.SemaphoreType.DMA],
+        scratch_shapes=[
+            pltpu.SemaphoreType.DMA((rows // block,)),
+            pltpu.VMEM((1, size), I32),
+            pltpu.SemaphoreType.DMA,
+        ],
         name="plan_and_pack",
         cost_estimate=QUICK,
         compiler_params=LARGE,
@@ -284,36 +286,34 @@
 
 
 def pack(source, metric_rows, first, count, pair, block, after, name):
-    outs, scratch = sent_shapes(count, block, metric_rows.shape[1])
+    outs = sent_shapes(count, block)
     return pl.pallas_call(
         functools.partial(pack_kernel, first=first, pair=pair, block=block),
-        in_specs=[VMEM, HBM] + [ANY] * len(after),
+        in_specs=[VMEM, VMEM] + [ANY] * len(after),
         out_specs=[VMEM] * 2,
         out_shape=outs,
-        scratch_shapes=scratch,
         name=name,
         cost_estimate=QUICK,
         compiler_params=LARGE,
     )(source, metric_rows, *after)
 
 
-def land_metric_kernel(landing, metric, *rest, first, block, spots):
-    *messages, out, token, held, ready, sems, out_sems = rest
+def land_metric_kernel(landing, held, *rest, first, block, spots):
+    *messages, out, token, ready, sems = rest
     token[...] = jnp.zeros_like(token)
     columns = arrival_spots(landing[...])
-    count = held.shape[0] // block
-    fetch_parts(metric, first, held, sems, block)
-    for number in range(count):
+    copies = []
+    for number in range(ready.shape[0] // block):
         start = number * block
+        source = (first + number) * block
         parts, at = spots[number]
-        fetch(metric, held, sems, number, (first + number) * block, block, start).wait()
         land_block(
-            held, start, block, landing[...], columns, [messages[k] for k in parts], at, ready, start
+            held, source, block, landing[...], columns, [messages[k] for k in parts], at, ready, start
         )
-        fetch(ready, out, out_sems, number, start, block, (first + number) * block).start()
-    for number in range(count):
-        start = number * block
-        fetch(ready, out, out_sems, number, start, block, (first + number) * block).wait()
+        copies.append(fetch(ready, out, sems, number, start, block, source))
+        copies[-1].start()
+    for copy in copies:
+        copy.wait()
 
 
 def land_metric(landing, metric_rows, dom, sub, first, count, block, before, after, name):
@@ -331,7 +331,7 @@
             ats = (ats or []) + [local * block // 2] * 2
         spots.append((parts, ats))
     operands = [landing, metric_rows, *messages, after]
-    specs = [VMEM, HBM] + [VMEM] * len(messages) + [ANY]
+    specs = [VMEM, VMEM] + [VMEM] * len(messages) + [ANY]
     aliases = {}
     if before is not None:
         aliases = {len(operands): 0}
@@ -347,8 +347,6 @@
         ],
         scratch_shapes=[
             pltpu.VMEM((count * block, size), F32),
-            pltpu.VMEM((count * block, size), F32),
-            pltpu.SemaphoreType.DMA((count,)),
             pltpu.SemaphoreType.DMA((count,)),
         ],
         input_output_aliases=aliases,
@@ -509,7 +507,7 @@
     place,
     ids,
     solution,
-    metric_hbm,
+    metric,
     grad_left,
     image_left,
     square_left,
@@ -522,9 +520,7 @@
     corner_table,
     dom_out,
     sub_out,
-    metric,
     flux_r,
-    sems,
     *,
     table,
 ):
@@ -533,20 +529,6 @@
     count = table.shape[0]
     plane = count * count
     nodes = count * plane
-    halves = 2
-    part_rows = nodes // halves
-    copies = [
-        [
-            fetch(metric_hbm, metric, sems, h * 7 + c, c * nodes + h * part_rows, part_rows,
-                  c * nodes + h * part_rows)
-            for c in range(7)
-        ]
-        for h in range(halves)
-    ]
-    for group in copies:
-        for copy in group:
-            copy.start()
-
     width = 2 * LANES
     node = iota((count, width), 0)
     ends = (0, count - 1)
@@ -555,9 +537,6 @@
         node == 0, end_value[0], jnp.where(node == count - 1, end_value[count - 1], 0.0)
     )
     for i in range(count):
-        if i % (count // halves) == 0:
-            for copy in copies[i // (count // halves)]:
-                copy.wait()
         rows = slice(i * plane, (i + 1) * plane)
         for base in range(0, size, width):
             lanes = slice(base, base + width)
@@ -735,13 +714,11 @@
     ]
     return pl.pallas_call(
         functools.partial(apply_kernel, table=table),
-        in_specs=[SMEM, VMEM, VMEM, HBM, VMEM, VMEM, VMEM, ANY],
+        in_specs=[SMEM] + [VMEM] * 6 + [ANY],
         out_specs=[VMEM] * len(outs),
         out_shape=outs,
         scratch_shapes=[
-            pltpu.VMEM(metric_rows.shape, F32),
             pltpu.VMEM((nodes, size), F32),
-            pltpu.SemaphoreType.DMA((14,)),
         ],
         name="apply_and_pack",
         cost_estimate=QUICK,
@@ -1041,7 +1018,9 @@
     metric_rows = pltpu.with_memory_space_constraint(metric.reshape(-1, size), pltpu.HBM)
     components = metric.shape[0]
     block = metric_rows.shape[0] // components
-    source, landing, *messages = plan_and_pack(place, new_owner.reshape(1, size), metric_rows, block)
+    source, landing, *messages, metric_rows = plan_and_pack(
+        place, new_owner.reshape(1, size), metric_rows, block
+    )
     sub_early = swapped(*messages, "sub")
     messages = pack(source, metric_rows, 0, DOM_EARLY, 0, block, (landing,), "pack_dom")
     dom_early = swapped(*messages, "dom")
@@ -1064,11 +1043,12 @@
     back_sub = shifted(sub_back, "sub", -1)
     image, diagonal = merge_dom(column, back_dom, image, diagonal, sub_late)
     dom_moves, sub_moves = (dom_early, ()), (sub_early, sub_late)
+    relaxed, *leaving = relax_and_pack(
+        column, back_sub, image, diagonal, field, forcing.reshape(-1, size), source,
+        (image,),
+    )
     moved, token = land_metric(
-        landing, metric_rows, dom_moves, sub_moves, 0, SUB_EARLY, block, None, image, "land_early"
-    )
-    relaxed, *leaving = relax_and_pack(
-        column, back_sub, image, diagonal, field, forcing.reshape(-1, size), source, (token,)
+        landing, metric_rows, dom_moves, sub_moves, 0, SUB_EARLY, block, None, leaving[0], "land_early"
     )
     got_sub = swapped(*leaving[2:], "sub")
     got_dom = swapped(*leaving[:2], "dom")

time: 78.5 us -> 75.3 us (0.959)
  Pallas kernels: 46.6 us -> 38.6 us
  waiting for transfers between devices: 9.8 us -> 14 us
    ppermute x14, waiting for transfers between devices: 9.8 us -> 14 us  [shifted(): lax.ppermute(value, axis, [(i, (i + steps) % count) for i in range(count)])]
    pallas_call x2, Pallas kernels: 6.51 us -> 3.49 us  [pack(): pl.pallas_call(functools.partial(pack_kernel, first=first, pair=pair, blo...]
    pallas_call x2, Pallas kernels: 8.89 us -> 6.02 us  [land_metric(): pl.pallas_call(functools.partial(land_metric_kernel, first=first, block=b...]
    pallas_call x1, Pallas kernels: 14.8 us -> 12.7 us  [apply_and_pack(): pl.pallas_call(functools.partial(apply_kernel, table=table), in_specs=[SM...]
  transfers between devices with their start and end apart: 14 -> 14, of which waited for: 4 -> 3; matrix products, arithmetic and copies ran while one was open for 0% -> 0% of each run, Pallas kernels for 49% -> 40%
where the time goes in v4:
time: 75.3 us; the launch traced here: 75.1 us
  Pallas kernels  38.6 us (51%)
  starting transfers between devices  20.7 us (27%)
  waiting for transfers between devices  14 us (19%)
  between operations  1.04 us (1%)
  local copies, waits for them, and re-layouts  0.8 us (1%)
    ppermute x14, starting transfers between devices, shifted(): lax.ppermute(value, axis, [(i, (i + steps) % count) for i in range(count)])  20.7 us
    ppermute x14, waiting for transfers between devices, shifted(): lax.ppermute(value, axis, [(i, (i + steps) % count) for i in range(count)])  14 us
    pallas_call x1, Pallas kernels, apply_and_pack(): pl.pallas_call(functools.partial(apply_kernel, table=table), in_specs=[SM...  12.7 us
    pallas_call x2, Pallas kernels, land_metric(): pl.pallas_call(functools.partial(land_metric_kernel, first=first, block=b...  6.02 us
    pallas_call x1, Pallas kernels, merge_own(): pl.pallas_call(kernel, in_specs=[VMEM] * 6 + [ANY] * len(after), out_spec...  5.42 us
    pallas_call x1, Pallas kernels, plan_and_pack(): pl.pallas_call(functools.partial(plan_and_pack_kernel, block=block), in_s...  4.05 us
    pallas_call x2, Pallas kernels, pack(): pl.pallas_call(functools.partial(pack_kernel, first=first, pair=pair, blo...  3.49 us
    pallas_call x1, Pallas kernels, relax_and_pack(): pl.pallas_call(relax_kernel, in_specs=[VMEM] * 7 + [ANY] * len(after), ou...  2.2 us
  transfers between devices with their start and end apart: 14, of which 3 were waited for; matrix products, arithmetic and copies ran while one was open for 0% of the time, Pallas kernels for 40%

profile of v4, /device:TPU:0, one launch (start us, length us, event | category | flops | bytes accessed | tf_op | source)
XLA Modules:
  0.0 75.1 jit_solution(13148773403795483433)
XLA Ops:
  0.6 0.1 stack.27.place
  0.7 0.7 copy-done.6
  1.4 4.1 %plan_and_pack.1 = (s32[1,256]{1,0:T(1,128)S(1)}, s32[1,512]{1,0:T(1,128)S(1)}, f32[1280,128]{1,0:T(8,128)S(1)}, f32[1280,128]{1,0:T(8,128)S(1)}, f32[3584,512]{1,0:T(8,128)S(1)}) custom-call(s32[6]{0:T(128)S(1)} %stack.27.place, s32[1,512]{1,0:T(1,128)S(1)} %bitcast.15, f32[3584,512]{1,0:T(8,128)} %bitcast.17), custom_call_target="tpu_custom_call" | custom-call | flops 1000 | bytes 1000 | tf_op jit(solution)/shard_map/plan_and_pack/pallas_call | solution.py:272
  5.5 3.1 %collective-permute-start.1 = (f32[1280,128]{1,0:T(8,128)S(1)}, f32[1280,128]{1,0:T(8,128)S(1)}, u32[]{:S(2)}, u32[]{:S(2)}) collective-permute-start(f32[1280,128]{1,0:T(8,128)S(1)} %get-tuple-element.48), channel_id=1, source_target_pairs={{0,1},{1,2},{2,3},{3,0},{4,5},{5,6},{6,7},{7,4},{8,9},{9,10},{10,1... | collective-permute-start | bytes 1966088 | tf_op jit(solution)/shard_map/ppermute | solution.py:1006
  8.6 2.1 %collective-permute-start.2 = (f32[1280,128]{1,0:T(8,128)S(1)}, f32[1280,128]{1,0:T(8,128)S(1)}, u32[]{:S(2)}, u32[]{:S(2)}) collective-permute-start(f32[1280,128]{1,0:T(8,128)S(1)} %get-tuple-element.49), channel_id=1, source_target_pairs={{0,3},{1,0},{2,1},{3,2},{4,7},{5,4},{6,5},{7,6},{8,11},{9,8},{10,9... | collective-permute-start | bytes 1966088 | tf_op jit(solution)/shard_map/ppermute | solution.py:1006
  10.7 2.7 %pack_dom.1 = (f32[1792,128]{1,0:T(8,128)S(1)}, f32[1792,128]{1,0:T(8,128)S(1)}) custom-call(s32[1,256]{1,0:T(1,128)S(1)} %get-tuple-element.40.source, f32[3584,512]{1,0:T(8,128)S(1)} %get-tuple-element.39.held.metric, s32[1,512]{1,0:T(1,128)S(1)} %get-tuple-element.38.rest_0_.landing), custom_call_target="tpu_custom_call" | custom-call | flops 1000 | bytes 1000 | tf_op jit(solution)/shard_map/pack_dom/pallas_call | solution.py:290
  13.3 0.1 collective-permute-start.6
  13.4 2.6 %collective-permute-start.7 = (f32[1792,128]{1,0:T(8,128)S(1)}, f32[1792,128]{1,0:T(8,128)S(1)}, u32[]{:S(2)}, u32[]{:S(2)}) collective-permute-start(f32[1792,128]{1,0:T(8,128)S(1)} %get-tuple-element.41.after), channel_id=1, source_target_pairs={{0,28},{4,0},{8,4},{12,8},{16,12},{20,16},{24,20},{28,24},{1,29},{... | collective-permute-start | bytes 2752520 | tf_op jit(solution)/shard_map/ppermute | solution.py:1006
  16.1 12.7 %apply_and_pack.1 = (f32[4,512,128]{2,1,0:T(8,128)S(1)}, f32[4,512,128]{2,1,0:T(8,128)S(1)}, s32[26,512]{1,0:T(8,128)S(1)}, f32[96,1536]{1,0:T(8,128)S(1)}, f32[...) custom-call(s32[6]{0:T(128)S(1)} %stack.27.place, ...), custom_call_target="tpu_custom_call" | custom-call | flops 1000 | bytes 1000 | tf_op jit(solution)/shard_map/apply_and_pack/pallas_call | solution.py:715
  28.7 0.1 collective-permute-start
  28.8 0.8 %pack_sub_late.1 = (f32[512,128]{1,0:T(8,128)S(1)}, f32[512,128]{1,0:T(8,128)S(1)}) custom-call(s32[1,256]{1,0:T(1,128)S(1)} %get-tuple-element.40.source, f32[3584,512]{1,0:T(8,128)S(1)} %get-tuple-element.39.held.metric, f32[176,128]{1,0:T(8,128)S(1)} %get-tuple-element.46.rest_0_), custom_call_target="tpu_custom_call" | custom-call | flops 1000 | bytes 1000 | tf_op jit(solution)/shard_map/pack_sub_late/pallas_call | solution.py:290
  29.6 11.7 %collective-permute-done.received.message = f32[176,128]{1,0:T(8,128)S(1)} collective-permute-done((f32[176,128]{1,0:T(8,128)S(1)}, f32[176,128]{1,0:T(8,128)S(1)}, u32[]{:S(2)}, u32[]{:S(2)}) %collective-permute-start) | collective-permute-done | bytes 90144 | tf_op jit(solution)/shard_map/ppermute | solution.py:1006
  41.4 0.1 collective-permute-start.3
  41.4 0.1 collective-permute-start.8
  41.5 3.8 %collective-permute-start.9 = (f32[512,128]{1,0:T(8,128)S(1)}, f32[512,128]{1,0:T(8,128)S(1)}, u32[]{:S(2)}, u32[]{:S(2)}) collective-permute-start(f32[512,128]{1,0:T(8,128)S(1)} %get-tuple-element.50.rest_2_), channel_id=1, source_target_pairs={{0,3},{1,0},{2,1},{3,2},{4,7},{5,4},{6,5},{7,6},{8,11},{9,8},{10,9... | collective-permute-start | bytes 786440 | tf_op jit(solution)/shard_map/ppermute | solution.py:1006
  45.3 0.5 add_sub.1
  45.8 0.5 collective-permute-done.3.message
  46.3 0.7 add_dom.1
  47.0 1.6 %collective-permute-start.4 = (f32[176,128]{1,0:T(8,128)S(1)}, f32[176,128]{1,0:T(8,128)S(1)}, u32[]{:S(2)}, u32[]{:S(2)}) collective-permute-start(f32[176,128]{1,0:T(8,128)S(1)} %get-tuple-element.57.rest_0_), channel_id=1, source_target_pairs={{0,28},{4,0},{8,4},{12,8},{16,12},{20,16},{24,20},{28,24},{1,29},{... | collective-permute-start | bytes 270344 | tf_op jit(solution)/shard_map/ppermute | solution.py:1006
  48.5 0.4 read_sub.1.message
  48.9 1.8 %collective-permute-done.4.received.message = f32[176,128]{1,0:T(8,128)S(1)} collective-permute-done((f32[176,128]{1,0:T(8,128)S(1)}, f32[176,128]{1,0:T(8,128)S(1)}, u32[]{:S(2)}, u32[]{:S(2)}) %collective-permute-start.4) | collective-permute-done | bytes 90144 | tf_op jit(solution)/shard_map/ppermute | solution.py:1006
  50.7 0.6 collective-permute-start.5
  51.3 5.4 %merge_own.1 = (f32[4,512,128]{2,1,0:T(8,128)S(1)}, f32[4,512,128]{2,1,0:T(8,128)S(1)}) custom-call(s32[26,512]{1,0:T(8,128)S(1)} %get-tuple-element.42.column, f32[96,1536]{1,0:T(8,128)S(1)} %get-tuple-element.54.faces, f32[16,1536]{1,0:T(8,128)S(1)} %get-tuple-element.55.edges, f32[8,512]{1,0:T(8,128)S(1)} %get-tuple-element.56.corners, ...), custom_call_target="tpu_custom_call" | custom-call | flops 1000 | bytes 1000 | tf_op jit(solution)/shard_map/merge_own/pallas_call | solution.py:943
  56.7 1.2 %merge_dom.1 = (f32[4,512,128]{2,1,0:T(8,128)S(1)}, f32[4,512,128]{2,1,0:T(8,128)S(1)}) custom-call(s32[26,512]{1,0:T(8,128)S(1)} %get-tuple-element.42.column, f32[176,128]{1,0:T(8,128)S(1)} %collective-permute-done.4.received.message, f32[4,512,128]{2,1,0:T(8,128)S(1)} %get-tuple-element.61.image_in, f32[4,512,128]{2,1,0:T(8,128)S(1)} %get-tuple-element.62.diagonal_in, ...), custom_call_target="tpu_custom_call" | custom-call | flops 1000 | bytes 1000 | tf_op jit(solution)/shard_map/merge_dom/pallas_call | solution.py:961
  57.9 2.2 %relax_and_pack.1 = (f32[512,512]{1,0:T(8,128)S(1)}, f32[256,128]{1,0:T(8,128)S(1)}, f32[256,128]{1,0:T(8,128)S(1)}, f32[256,128]{1,0:T(8,128)S(1)}, f32[256,128]{1,0:T(8,128)S(1)}) custom-call(s32[26,512]{1,0:T(8,128)S(1)} %get-tuple-element.42.column, f32[176,128]{1,0:T(8,128)S(1)} %collective-permute-done.5.message, ...), custom_call_target="tpu_custom_call" | custom-call | flops 1000 | bytes 1000 | tf_op jit(solution)/shard_map/relax_and_pack/pallas_call | solution.py:992
  60.1 0.9 %collective-permute-start.10 = (f32[256,128]{1,0:T(8,128)S(1)}, f32[256,128]{1,0:T(8,128)S(1)}, u32[]{:S(2)}, u32[]{:S(2)}) collective-permute-start(f32[256,128]{1,0:T(8,128)S(1)} %get-tuple-element.67), channel_id=1, source_target_pairs={{0,4},{4,8},{8,12},{12,16},{16,20},{20,24},{24,28},{28,0},{1,5},{5... | collective-permute-start | bytes 393224 | tf_op jit(solution)/shard_map/ppermute | solution.py:1006
  61.0 2.0 %collective-permute-start.11 = (f32[256,128]{1,0:T(8,128)S(1)}, f32[256,128]{1,0:T(8,128)S(1)}, u32[]{:S(2)}, u32[]{:S(2)}) collective-permute-start(f32[256,128]{1,0:T(8,128)S(1)} %get-tuple-element.68.rest_4_), channel_id=1, source_target_pairs={{0,28},{4,0},{8,4},{12,8},{16,12},{20,16},{24,20},{28,24},{1,29},{... | collective-permute-start | bytes 393224 | tf_op jit(solution)/shard_map/ppermute | solution.py:1006
  63.0 1.7 %collective-permute-start.12 = (f32[256,128]{1,0:T(8,128)S(1)}, f32[256,128]{1,0:T(8,128)S(1)}, u32[]{:S(2)}, u32[]{:S(2)}) collective-permute-start(f32[256,128]{1,0:T(8,128)S(1)} %get-tuple-element.69), channel_id=1, source_target_pairs={{0,1},{1,2},{2,3},{3,0},{4,5},{5,6},{6,7},{7,4},{8,9},{9,10},{10,1... | collective-permute-start | bytes 393224 | tf_op jit(solution)/shard_map/ppermute | solution.py:1006
  64.7 2.1 %collective-permute-start.13 = (f32[256,128]{1,0:T(8,128)S(1)}, f32[256,128]{1,0:T(8,128)S(1)}, u32[]{:S(2)}, u32[]{:S(2)}) collective-permute-start(f32[256,128]{1,0:T(8,128)S(1)} %get-tuple-element.70), channel_id=1, source_target_pairs={{0,3},{1,0},{2,1},{3,2},{4,7},{5,4},{6,5},{7,6},{8,11},{9,8},{10,9... | collective-permute-start | bytes 393224 | tf_op jit(solution)/shard_map/ppermute | solution.py:1006
  66.8 3.9 %land_early.1 = (f32[3584,512]{1,0:T(8,128)}, f32[8,128]{1,0:T(8,128)}) custom-call(s32[1,512]{1,0:T(1,128)S(1)} %get-tuple-element.38.rest_0_.landing, f32[3584,512]{1,0:T(8,128)S(1)} %get-tuple-element.39.held.metric, f32[1792,128]{1,0:T(8,128)S(1)} %collective-permute-done.6.rest_1_.rest_0_, f32[1792,128]{1,0:T(8,128)S(1)} %collective-permute-done.7.rest_2_.rest_1_, ...), custom_call_target="tpu_custom_call" | custom-call | flops 1000 | bytes 1000 | tf_op jit(solution)/shard_map/land_early/pallas_call | solution.py:340
  70.8 2.1 %land_late.1 = (f32[3584,512]{1,0:T(8,128)}, f32[8,128]{1,0:T(8,128)S(1)}) custom-call(s32[1,512]{1,0:T(1,128)S(1)} %get-tuple-element.38.rest_0_.landing, f32[3584,512]{1,0:T(8,128)S(1)} %get-tuple-element.39.held.metric, f32[1792,128]{1,0:T(8,128)S(1)} %collective-permute-done.6.rest_1_.rest_0_, ...), custom_call_target="tpu_custom_call", output_to_operand_aliasing={{0}: (7, {})} | custom-call | flops 1000 | bytes 1000 | tf_op jit(solution)/shard_map/land_late/pallas_call | solution.py:340
  72.9 2.0 %land_field.1 = f32[512,512]{1,0:T(8,128)} custom-call(s32[1,512]{1,0:T(1,128)S(1)} %get-tuple-element.38.rest_0_.landing, f32[512,512]{1,0:T(8,128)S(1)} %get-tuple-element.66.relaxed, f32[256,128]{1,0:T(8,128)S(1)} %collective-permute-done.10.first, f32[256,128]{1,0:T(8,128)S(1)} %collective-permute-done.11.second, ...), custom_call_target="tpu_custom_call" | custom-call | flops 1000 | bytes 1000 | tf_op jit(solution)/shard_map/land_field/pallas_call | solution.py:380
  (26 shorter events, 0.1 us)
Async XLA Ops:
  0.7 0.7 copy-start.6
  1.4 14.6 %copy-start = (f32[8,8,8,512]{3,2,1,0:T(8,128)S(1)}, f32[8,8,8,512]{3,2,1,0:T(8,128)}, u32[]{:S(2)}) copy-start(f32[8,8,8,512]{3,2,1,0:T(8,128)} %param.8) | copy-start | bytes 3145732
  1.4 14.6 %copy-start.2 = (s32[26,512]{1,0:T(8,128)S(1)}, s32[26,512]{1,0:T(8,128)}, u32[]{:S(2)}) copy-start(s32[26,512]{1,0:T(8,128)} %ids.1) | copy-start | bytes 159748
  1.4 14.6 %copy-start.3 = (bf16[128,192]{1,0:T(8,128)(2,1)S(1)}, bf16[128,192]{1,0:T(8,128)(2,1)}, u32[]{:S(2)}) copy-start(bf16[128,192]{1,0:T(8,128)(2,1)} %constant.35.clone.grad_left) | copy-start | bytes 147460
  1.4 14.6 %copy-start.4 = (bf16[64,384]{1,0:T(8,128)(2,1)S(1)}, bf16[64,384]{1,0:T(8,128)(2,1)}, u32[]{:S(2)}) copy-start(bf16[64,384]{1,0:T(8,128)(2,1)} %constant.36.clone.image_left) | copy-start | bytes 147460
  1.4 14.6 %copy-start.5 = (bf16[64,384]{1,0:T(8,128)(2,1)S(1)}, bf16[64,384]{1,0:T(8,128)(2,1)}, u32[]{:S(2)}) copy-start(bf16[64,384]{1,0:T(8,128)(2,1)} %constant.37.clone.square_left) | copy-start | bytes 147460
  5.5 35.9 %collective-permute-start.1 = (f32[1280,128]{1,0:T(8,128)S(1)}, f32[1280,128]{1,0:T(8,128)S(1)}, u32[]{:S(2)}, u32[]{:S(2)}) collective-permute-start(f32[1280,128]{1,0:T(8,128)S(1)} %get-tuple-element.48), channel_id=1, source_target_pairs={{0,1},{1,2},{2,3},{3,0},{4,5},{5,6},{6,7},{7,4},{8,9},{9,10},{10,1... | collective-permute-start | bytes 1966088 | tf_op jit(solution)/shard_map/ppermute | solution.py:1006
  8.6 32.8 %collective-permute-start.2 = (f32[1280,128]{1,0:T(8,128)S(1)}, f32[1280,128]{1,0:T(8,128)S(1)}, u32[]{:S(2)}, u32[]{:S(2)}) collective-permute-start(f32[1280,128]{1,0:T(8,128)S(1)} %get-tuple-element.49), channel_id=1, source_target_pairs={{0,3},{1,0},{2,1},{3,2},{4,7},{5,4},{6,5},{7,6},{8,11},{9,8},{10,9... | collective-permute-start | bytes 1966088 | tf_op jit(solution)/shard_map/ppermute | solution.py:1006
  13.3 37.9 %collective-permute-start.6 = (f32[1792,128]{1,0:T(8,128)S(1)}, f32[1792,128]{1,0:T(8,128)S(1)}, u32[]{:S(2)}, u32[]{:S(2)}) collective-permute-start(f32[1792,128]{1,0:T(8,128)S(1)} %get-tuple-element.60), channel_id=1, source_target_pairs={{0,4},{4,8},{8,12},{12,16},{16,20},{20,24},{24,28},{28,0},{1,5},{5... | collective-permute-start | bytes 2752520 | tf_op jit(solution)/shard_map/ppermute | solution.py:1006
  13.4 37.9 %collective-permute-start.7 = (f32[1792,128]{1,0:T(8,128)S(1)}, f32[1792,128]{1,0:T(8,128)S(1)}, u32[]{:S(2)}, u32[]{:S(2)}) collective-permute-start(f32[1792,128]{1,0:T(8,128)S(1)} %get-tuple-element.41.after), channel_id=1, source_target_pairs={{0,28},{4,0},{8,4},{12,8},{16,12},{20,16},{24,20},{28,24},{1,29},{... | collective-permute-start | bytes 2752520 | tf_op jit(solution)/shard_map/ppermute | solution.py:1006
  28.7 12.6 %collective-permute-start = (f32[176,128]{1,0:T(8,128)S(1)}, f32[176,128]{1,0:T(8,128)S(1)}, u32[]{:S(2)}, u32[]{:S(2)}) collective-permute-start(f32[176,128]{1,0:T(8,128)S(1)} %get-tuple-element.46.rest_0_), channel_id=1, source_target_pairs={{0,1},{1,2},{2,3},{3,0},{4,5},{5,6},{6,7},{7,4},{8,9},{9,10},{10,1... | collective-permute-start | bytes 270344 | tf_op jit(solution)/shard_map/ppermute | solution.py:1006
  29.6 28.3 %copy-start.1 = (f32[8,8,8,512]{3,2,1,0:T(8,128)S(1)}, f32[8,8,8,512]{3,2,1,0:T(8,128)}, u32[]{:S(2)}) copy-start(f32[8,8,8,512]{3,2,1,0:T(8,128)} %param.9) | copy-start | bytes 3145732
  41.4 4.9 %collective-permute-start.3 = (f32[176,128]{1,0:T(8,128)S(1)}, f32[176,128]{1,0:T(8,128)S(1)}, u32[]{:S(2)}, u32[]{:S(2)}) collective-permute-start(f32[176,128]{1,0:T(8,128)S(1)} %pass_on.2.after), channel_id=1, source_target_pairs={{0,4},{4,8},{8,12},{12,16},{16,20},{20,24},{24,28},{28,0},{1,5},{5... | collective-permute-start | bytes 270344 | tf_op jit(solution)/shard_map/ppermute | solution.py:1006
  41.4 15.3 %collective-permute-start.8 = (f32[512,128]{1,0:T(8,128)S(1)}, f32[512,128]{1,0:T(8,128)S(1)}, u32[]{:S(2)}, u32[]{:S(2)}) collective-permute-start(f32[512,128]{1,0:T(8,128)S(1)} %get-tuple-element.63), channel_id=1, source_target_pairs={{0,1},{1,2},{2,3},{3,0},{4,5},{5,6},{6,7},{7,4},{8,9},{9,10},{10,1... | collective-permute-start | bytes 786440 | tf_op jit(solution)/shard_map/ppermute | solution.py:1006
  41.5 15.2 %collective-permute-start.9 = (f32[512,128]{1,0:T(8,128)S(1)}, f32[512,128]{1,0:T(8,128)S(1)}, u32[]{:S(2)}, u32[]{:S(2)}) collective-permute-start(f32[512,128]{1,0:T(8,128)S(1)} %get-tuple-element.50.rest_2_), channel_id=1, source_target_pairs={{0,3},{1,0},{2,1},{3,2},{4,7},{5,4},{6,5},{7,6},{8,11},{9,8},{10,9... | collective-permute-start | bytes 786440 | tf_op jit(solution)/shard_map/ppermute | solution.py:1006
  47.0 3.7 %collective-permute-start.4 = (f32[176,128]{1,0:T(8,128)S(1)}, f32[176,128]{1,0:T(8,128)S(1)}, u32[]{:S(2)}, u32[]{:S(2)}) collective-permute-start(f32[176,128]{1,0:T(8,128)S(1)} %get-tuple-element.57.rest_0_), channel_id=1, source_target_pairs={{0,28},{4,0},{8,4},{12,8},{16,12},{20,16},{24,20},{28,24},{1,29},{... | collective-permute-start | bytes 270344 | tf_op jit(solution)/shard_map/ppermute | solution.py:1006
  50.7 7.2 %collective-permute-start.5 = (f32[176,128]{1,0:T(8,128)S(1)}, f32[176,128]{1,0:T(8,128)S(1)}, u32[]{:S(2)}, u32[]{:S(2)}) collective-permute-start(f32[176,128]{1,0:T(8,128)S(1)} %pass_on.3), channel_id=1, source_target_pairs={{0,3},{1,0},{2,1},{3,2},{4,7},{5,4},{6,5},{7,6},{8,11},{9,8},{10,9... | collective-permute-start | bytes 270344 | tf_op jit(solution)/shard_map/ppermute | solution.py:1006
  60.1 12.7 %collective-permute-start.10 = (f32[256,128]{1,0:T(8,128)S(1)}, f32[256,128]{1,0:T(8,128)S(1)}, u32[]{:S(2)}, u32[]{:S(2)}) collective-permute-start(f32[256,128]{1,0:T(8,128)S(1)} %get-tuple-element.67), channel_id=1, source_target_pairs={{0,4},{4,8},{8,12},{12,16},{16,20},{20,24},{24,28},{28,0},{1,5},{5... | collective-permute-start | bytes 393224 | tf_op jit(solution)/shard_map/ppermute | solution.py:1006
  61.0 11.9 %collective-permute-start.11 = (f32[256,128]{1,0:T(8,128)S(1)}, f32[256,128]{1,0:T(8,128)S(1)}, u32[]{:S(2)}, u32[]{:S(2)}) collective-permute-start(f32[256,128]{1,0:T(8,128)S(1)} %get-tuple-element.68.rest_4_), channel_id=1, source_target_pairs={{0,28},{4,0},{8,4},{12,8},{16,12},{20,16},{24,20},{28,24},{1,29},{... | collective-permute-start | bytes 393224 | tf_op jit(solution)/shard_map/ppermute | solution.py:1006
  63.0 9.9 %collective-permute-start.12 = (f32[256,128]{1,0:T(8,128)S(1)}, f32[256,128]{1,0:T(8,128)S(1)}, u32[]{:S(2)}, u32[]{:S(2)}) collective-permute-start(f32[256,128]{1,0:T(8,128)S(1)} %get-tuple-element.69), channel_id=1, source_target_pairs={{0,1},{1,2},{2,3},{3,0},{4,5},{5,6},{6,7},{7,4},{8,9},{9,10},{10,1... | collective-permute-start | bytes 393224 | tf_op jit(solution)/shard_map/ppermute | solution.py:1006
  64.7 8.2 %collective-permute-start.13 = (f32[256,128]{1,0:T(8,128)S(1)}, f32[256,128]{1,0:T(8,128)S(1)}, u32[]{:S(2)}, u32[]{:S(2)}) collective-permute-start(f32[256,128]{1,0:T(8,128)S(1)} %get-tuple-element.70), channel_id=1, source_target_pairs={{0,3},{1,0},{2,1},{3,2},{4,7},{5,4},{6,5},{7,6},{8,11},{9,8},{10,9... | collective-permute-start | bytes 393224 | tf_op jit(solution)/shard_map/ppermute | solution.py:1006

commit v5 on v4

--- a/solution.py
+++ b/solution.py
@@ -15,7 +15,7 @@
 RELAX = 0.6
 LANES = 128
 INNER = 6
-SUB_EARLY = 5
+SUB_EARLY = 4
 DOM_EARLY = 7
 
 NT = (((1,), (1,)), ((), ()))
@@ -183,12 +183,14 @@
     parts = [message[at + from_row : at + to_row, :] for message, at in zip(messages, ats)]
     pairs = [pack_pair(parts[0], parts[1]), pack_pair(parts[2], parts[3])]
     stays = jnp.broadcast_to(landing_row < 0, (rows, landing_row.shape[1]))
+    arrived = [jnp.concatenate([pairs[0][side], pairs[1][side]], axis=1) for side in range(2)]
+    got = dot(split_exactly(jnp.concatenate(arrived, axis=0)), spots)
     for side in range(2):
-        arrived = jnp.concatenate([pairs[0][side], pairs[1][side]], axis=1)
-        got = dot(split_exactly(arrived), spots)
         first = side * half + from_row
         held = ref[start + first : start + first + rows, :]
-        out[to + first : to + first + rows, :] = jnp.where(stays, held, got)
+        out[to + first : to + first + rows, :] = jnp.where(
+            stays, held, got[side * rows : (side + 1) * rows]
+        )
 
 
 def move_plan(owner, place):
@@ -1038,7 +1040,7 @@
     *tables, dom_back = add_dom(tables, got_dom)
     back_dom = shifted(dom_back, "dom", -1)
     sub_back = read_sub(tables, got_sub)
-    image, diagonal = merge_own(column, tables, image, diagonal, (dom_back, *dom_early))
+    image, diagonal = merge_own(column, tables, image, diagonal, (dom_back,))
     sub_back = pass_on(sub_back, back_dom)
     back_sub = shifted(sub_back, "sub", -1)
     image, diagonal = merge_dom(column, back_dom, image, diagonal, sub_late)
@@ -1047,14 +1049,11 @@
         column, back_sub, image, diagonal, field, forcing.reshape(-1, size), source,
         (image,),
     )
-    moved, token = land_metric(
-        landing, metric_rows, dom_moves, sub_moves, 0, SUB_EARLY, block, None, leaving[0], "land_early"
-    )
     got_sub = swapped(*leaving[2:], "sub")
     got_dom = swapped(*leaving[:2], "dom")
     moved, token = land_metric(
-        landing, metric_rows, dom_moves, sub_moves, SUB_EARLY, components - SUB_EARLY, block, moved,
-        leaving[0], "land_late",
+        landing, metric_rows, dom_moves, sub_moves, 0, components, block, None, leaving[0],
+        "land_metric",
     )
     smoothed = land_field(landing, relaxed, got_dom + got_sub, token)
     return smoothed.reshape(solution.shape), moved.reshape(metric.shape)

time: 75.3 us -> 70.7 us (0.939)
  starting transfers between devices: 20.7 us -> 17.8 us
  Pallas kernels: 38.6 us -> 36.2 us
  waiting for transfers between devices: 14 us -> 14.8 us
    ppermute x14, starting transfers between devices: 20.7 us -> 17.8 us  [shifted(): lax.ppermute(value, axis, [(i, (i + steps) % count) for i in range(count)])]
    pallas_call x2 -> x1, Pallas kernels: 6.02 us -> 4.24 us  [land_metric(): pl.pallas_call(functools.partial(land_metric_kernel, first=first, block=b...]
    ppermute x14, waiting for transfers between devices: 14 us -> 14.8 us  [shifted(): lax.ppermute(value, axis, [(i, (i + steps) % count) for i in range(count)])]
  transfers between devices with their start and end apart: 14 -> 14, of which waited for: 3 -> 5; matrix products, arithmetic and copies ran while one was open for 0% -> 0% of each run, Pallas kernels for 40% -> 44%
where the time goes in v5:
time: 70.7 us; the launch traced here: 70.6 us
  Pallas kernels  36.2 us (51%)
  starting transfers between devices  17.8 us (25%)
  waiting for transfers between devices  14.8 us (21%)
  between operations  1.02 us (1%)
  local copies, waits for them, and re-layouts  0.8 us (1%)
    ppermute x14, starting transfers between devices, shifted(): lax.ppermute(value, axis, [(i, (i + steps) % count) for i in range(count)])  17.8 us
    ppermute x14, waiting for transfers between devices, shifted(): lax.ppermute(value, axis, [(i, (i + steps) % count) for i in range(count)])  14.8 us
    pallas_call x1, Pallas kernels, apply_and_pack(): pl.pallas_call(functools.partial(apply_kernel, table=table), in_specs=[SM...  12.7 us
    pallas_call x1, Pallas kernels, merge_own(): pl.pallas_call(kernel, in_specs=[VMEM] * 6 + [ANY] * len(after), out_spec...  5.42 us
    pallas_call x1, Pallas kernels, land_metric(): pl.pallas_call(functools.partial(land_metric_kernel, first=first, block=b...  4.24 us
    pallas_call x2, Pallas kernels, pack(): pl.pallas_call(functools.partial(pack_kernel, first=first, pair=pair, blo...  3.86 us
    pallas_call x1, Pallas kernels, plan_and_pack(): pl.pallas_call(functools.partial(plan_and_pack_kernel, block=block), in_s...  3.72 us
    pallas_call x1, Pallas kernels, relax_and_pack(): pl.pallas_call(relax_kernel, in_specs=[VMEM] * 7 + [ANY] * len(after), ou...  2.15 us
  transfers between devices with their start and end apart: 14, of which 5 were waited for; matrix products, arithmetic and copies ran while one was open for 0% of the time, Pallas kernels for 44%

profile of v5, /device:TPU:0, one launch (start us, length us, event | category | flops | bytes accessed | tf_op | source)
XLA Modules:
  0.0 70.6 jit_solution(13104938910299976256)
XLA Ops:
  0.6 0.1 stack.27.place
  0.7 0.7 copy-done.6
  1.4 3.7 %plan_and_pack.1 = (s32[1,256]{1,0:T(1,128)S(1)}, s32[1,512]{1,0:T(1,128)S(1)}, f32[1024,128]{1,0:T(8,128)S(1)}, f32[1024,128]{1,0:T(8,128)S(1)}, f32[3584,512]{1,0:T(8,128)S(1)}) custom-call(s32[6]{0:T(128)S(1)} %stack.27.place, s32[1,512]{1,0:T(1,128)S(1)} %bitcast.15, f32[3584,512]{1,0:T(8,128)} %bitcast.16), custom_call_target="tpu_custom_call" | custom-call | flops 1000 | bytes 1000 | tf_op jit(solution)/shard_map/plan_and_pack/pallas_call | solution.py:274
  5.2 3.1 %collective-permute-start.1 = (f32[1024,128]{1,0:T(8,128)S(1)}, f32[1024,128]{1,0:T(8,128)S(1)}, u32[]{:S(2)}, u32[]{:S(2)}) collective-permute-start(f32[1024,128]{1,0:T(8,128)S(1)} %get-tuple-element.47), channel_id=1, source_target_pairs={{0,1},{1,2},{2,3},{3,0},{4,5},{5,6},{6,7},{7,4},{8,9},{9,10},{10,1... | collective-permute-start | bytes 1572872 | tf_op jit(solution)/shard_map/ppermute | solution.py:1008
  8.2 2.7 %pack_dom.1 = (f32[1792,128]{1,0:T(8,128)S(1)}, f32[1792,128]{1,0:T(8,128)S(1)}) custom-call(s32[1,256]{1,0:T(1,128)S(1)} %get-tuple-element.39.source, f32[3584,512]{1,0:T(8,128)S(1)} %get-tuple-element.38.held.metric, s32[1,512]{1,0:T(1,128)S(1)} %get-tuple-element.37.rest_0_.landing), custom_call_target="tpu_custom_call" | custom-call | flops 1000 | bytes 1000 | tf_op jit(solution)/shard_map/pack_dom/pallas_call | solution.py:292
  10.9 0.1 collective-permute-start.12
  11.0 2.1 %collective-permute-start.2 = (f32[1024,128]{1,0:T(8,128)S(1)}, f32[1024,128]{1,0:T(8,128)S(1)}, u32[]{:S(2)}, u32[]{:S(2)}) collective-permute-start(f32[1024,128]{1,0:T(8,128)S(1)} %get-tuple-element.48), channel_id=1, source_target_pairs={{0,3},{1,0},{2,1},{3,2},{4,7},{5,4},{6,5},{7,6},{8,11},{9,8},{10,9... | collective-permute-start | bytes 1572872 | tf_op jit(solution)/shard_map/ppermute | solution.py:1008
  13.1 2.3 %collective-permute-start.13 = (f32[1792,128]{1,0:T(8,128)S(1)}, f32[1792,128]{1,0:T(8,128)S(1)}, u32[]{:S(2)}, u32[]{:S(2)}) collective-permute-start(f32[1792,128]{1,0:T(8,128)S(1)} %get-tuple-element.40.after), channel_id=1, source_target_pairs={{0,28},{4,0},{8,4},{12,8},{16,12},{20,16},{24,20},{28,24},{1,29},{... | collective-permute-start | bytes 2752520 | tf_op jit(solution)/shard_map/ppermute | solution.py:1008
  15.4 12.7 %apply_and_pack.1 = (f32[4,512,128]{2,1,0:T(8,128)S(1)}, f32[4,512,128]{2,1,0:T(8,128)S(1)}, s32[26,512]{1,0:T(8,128)S(1)}, f32[96,1536]{1,0:T(8,128)S(1)}, f32[...) custom-call(s32[6]{0:T(128)S(1)} %stack.27.place, ...), custom_call_target="tpu_custom_call" | custom-call | flops 1000 | bytes 1000 | tf_op jit(solution)/shard_map/apply_and_pack/pallas_call | solution.py:717
  28.1 0.1 collective-permute-start
  28.2 1.2 %pack_sub_late.1 = (f32[768,128]{1,0:T(8,128)S(1)}, f32[768,128]{1,0:T(8,128)S(1)}) custom-call(s32[1,256]{1,0:T(1,128)S(1)} %get-tuple-element.39.source, f32[3584,512]{1,0:T(8,128)S(1)} %get-tuple-element.38.held.metric, f32[176,128]{1,0:T(8,128)S(1)} %get-tuple-element.45.rest_0_), custom_call_target="tpu_custom_call" | custom-call | flops 1000 | bytes 1000 | tf_op jit(solution)/shard_map/pack_sub_late/pallas_call | solution.py:292
  29.4 6.0 %collective-permute-done.received.message = f32[176,128]{1,0:T(8,128)S(1)} collective-permute-done((f32[176,128]{1,0:T(8,128)S(1)}, f32[176,128]{1,0:T(8,128)S(1)}, u32[]{:S(2)}, u32[]{:S(2)}) %collective-permute-start) | collective-permute-done | bytes 90144 | tf_op jit(solution)/shard_map/ppermute | solution.py:1008
  35.4 3.8 %collective-permute-start.7 = (f32[768,128]{1,0:T(8,128)S(1)}, f32[768,128]{1,0:T(8,128)S(1)}, u32[]{:S(2)}, u32[]{:S(2)}) collective-permute-start(f32[768,128]{1,0:T(8,128)S(1)} %get-tuple-element.49.rest_2_), channel_id=1, source_target_pairs={{0,3},{1,0},{2,1},{3,2},{4,7},{5,4},{6,5},{7,6},{8,11},{9,8},{10,9... | collective-permute-start | bytes 1179656 | tf_op jit(solution)/shard_map/ppermute | solution.py:1008
  39.2 0.1 collective-permute-start.3
  39.3 0.5 add_sub.1
  39.8 4.4 %collective-permute-done.3.message = f32[176,128]{1,0:T(8,128)S(1)} collective-permute-done((f32[176,128]{1,0:T(8,128)S(1)}, f32[176,128]{1,0:T(8,128)S(1)}, u32[]{:S(2)}, u32[]{:S(2)}) %collective-permute-start.3) | collective-permute-done | bytes 90144 | tf_op jit(solution)/shard_map/ppermute | solution.py:1008
  44.2 0.7 add_dom.1
  44.8 0.1 collective-permute-start.4
  44.9 0.4 read_sub.1.message
  45.3 1.8 %collective-permute-done.4.received.message = f32[176,128]{1,0:T(8,128)S(1)} collective-permute-done((f32[176,128]{1,0:T(8,128)S(1)}, f32[176,128]{1,0:T(8,128)S(1)}, u32[]{:S(2)}, u32[]{:S(2)}) %collective-permute-start.4) | collective-permute-done | bytes 90144 | tf_op jit(solution)/shard_map/ppermute | solution.py:1008
  47.0 0.3 collective-permute-start.5
  47.3 5.4 %merge_own.1 = (f32[4,512,128]{2,1,0:T(8,128)S(1)}, f32[4,512,128]{2,1,0:T(8,128)S(1)}) custom-call(s32[26,512]{1,0:T(8,128)S(1)} %get-tuple-element.41.column, f32[96,1536]{1,0:T(8,128)S(1)} %get-tuple-element.53.faces, f32[16,1536]{1,0:T(8,128)S(1)} %get-tuple-element.54.edges, f32[8,512]{1,0:T(8,128)S(1)} %get-tuple-element.55.corners, ...), custom_call_target="tpu_custom_call" | custom-call | flops 1000 | bytes 1000 | tf_op jit(solution)/shard_map/merge_own/pallas_call | solution.py:945
  52.8 2.3 %collective-permute-done.7.rest_1_.rest_5_ = f32[768,128]{1,0:T(8,128)S(1)} collective-permute-done((f32[768,128]{1,0:T(8,128)S(1)}, f32[768,128]{1,0:T(8,128)S(1)}, u32[]{:S(2)}, u32[]{:S(2)}) %collective-permute-start.7) | collective-permute-done | bytes 393248 | tf_op jit(solution)/shard_map/ppermute | solution.py:1008
  55.1 1.2 %merge_dom.1 = (f32[4,512,128]{2,1,0:T(8,128)S(1)}, f32[4,512,128]{2,1,0:T(8,128)S(1)}) custom-call(s32[26,512]{1,0:T(8,128)S(1)} %get-tuple-element.41.column, f32[176,128]{1,0:T(8,128)S(1)} %collective-permute-done.4.received.message, f32[4,512,128]{2,1,0:T(8,128)S(1)} %get-tuple-element.59.image_in, f32[4,512,128]{2,1,0:T(8,128)S(1)} %get-tuple-element.60.diagonal_in, ...), custom_call_target="tpu_custom_call" | custom-call | flops 1000 | bytes 1000 | tf_op jit(solution)/shard_map/merge_dom/pallas_call | solution.py:963
  56.3 2.2 %relax_and_pack.1 = (f32[512,512]{1,0:T(8,128)S(1)}, f32[256,128]{1,0:T(8,128)S(1)}, f32[256,128]{1,0:T(8,128)S(1)}, f32[256,128]{1,0:T(8,128)S(1)}, f32[256,128]{1,0:T(8,128)S(1)}) custom-call(s32[26,512]{1,0:T(8,128)S(1)} %get-tuple-element.41.column, f32[176,128]{1,0:T(8,128)S(1)} %collective-permute-done.5.message, ...), custom_call_target="tpu_custom_call" | custom-call | flops 1000 | bytes 1000 | tf_op jit(solution)/shard_map/relax_and_pack/pallas_call | solution.py:994
  58.5 0.1 collective-permute-start.8
  58.5 1.6 %collective-permute-start.10 = (f32[256,128]{1,0:T(8,128)S(1)}, f32[256,128]{1,0:T(8,128)S(1)}, u32[]{:S(2)}, u32[]{:S(2)}) collective-permute-start(f32[256,128]{1,0:T(8,128)S(1)} %get-tuple-element.67), channel_id=1, source_target_pairs={{0,1},{1,2},{2,3},{3,0},{4,5},{5,6},{6,7},{7,4},{8,9},{9,10},{10,1... | collective-permute-start | bytes 393224 | tf_op jit(solution)/shard_map/ppermute | solution.py:1008
  60.1 2.3 %collective-permute-start.11 = (f32[256,128]{1,0:T(8,128)S(1)}, f32[256,128]{1,0:T(8,128)S(1)}, u32[]{:S(2)}, u32[]{:S(2)}) collective-permute-start(f32[256,128]{1,0:T(8,128)S(1)} %get-tuple-element.68), channel_id=1, source_target_pairs={{0,3},{1,0},{2,1},{3,2},{4,7},{5,4},{6,5},{7,6},{8,11},{9,8},{10,9... | collective-permute-start | bytes 393224 | tf_op jit(solution)/shard_map/ppermute | solution.py:1008
  62.4 2.0 %collective-permute-start.9 = (f32[256,128]{1,0:T(8,128)S(1)}, f32[256,128]{1,0:T(8,128)S(1)}, u32[]{:S(2)}, u32[]{:S(2)}) collective-permute-start(f32[256,128]{1,0:T(8,128)S(1)} %get-tuple-element.66.rest_6_), channel_id=1, source_target_pairs={{0,28},{4,0},{8,4},{12,8},{16,12},{20,16},{24,20},{28,24},{1,29},{... | collective-permute-start | bytes 393224 | tf_op jit(solution)/shard_map/ppermute | solution.py:1008
  64.4 4.2 %land_metric.1 = (f32[3584,512]{1,0:T(8,128)}, f32[8,128]{1,0:T(8,128)S(1)}) custom-call(s32[1,512]{1,0:T(1,128)S(1)} %get-tuple-element.37.rest_0_.landing, f32[3584,512]{1,0:T(8,128)S(1)} %get-tuple-element.38.held.metric, f32[1792,128]{1,0:T(8,128)S(1)} %collective-permute-done.12.rest_0_, f32[1792,128]{1,0:T(8,128)S(1)} %collective-permute-done.13.rest_1_, ...), custom_call_target="tpu_custom_call" | custom-call | flops 1000 | bytes 1000 | tf_op jit(solution)/shard_map/land_metric/pallas_call | solution.py:342
  68.7 0.3 collective-permute-done.11.fourth
  69.0 1.4 %land_field.1 = f32[512,512]{1,0:T(8,128)} custom-call(s32[1,512]{1,0:T(1,128)S(1)} %get-tuple-element.37.rest_0_.landing, f32[512,512]{1,0:T(8,128)S(1)} %get-tuple-element.64.relaxed, f32[256,128]{1,0:T(8,128)S(1)} %collective-permute-done.8.first, f32[256,128]{1,0:T(8,128)S(1)} %collective-permute-done.9.second, ...), custom_call_target="tpu_custom_call" | custom-call | flops 1000 | bytes 1000 | tf_op jit(solution)/shard_map/land_field/pallas_call | solution.py:382
  (25 shorter events, 0.1 us)
Async XLA Ops:
  0.7 0.7 copy-start.6
  1.4 14.0 %copy-start = (f32[8,8,8,512]{3,2,1,0:T(8,128)S(1)}, f32[8,8,8,512]{3,2,1,0:T(8,128)}, u32[]{:S(2)}) copy-start(f32[8,8,8,512]{3,2,1,0:T(8,128)} %param.8) | copy-start | bytes 3145732
  1.4 14.0 %copy-start.2 = (s32[26,512]{1,0:T(8,128)S(1)}, s32[26,512]{1,0:T(8,128)}, u32[]{:S(2)}) copy-start(s32[26,512]{1,0:T(8,128)} %ids.1) | copy-start | bytes 159748
  1.4 14.0 %copy-start.3 = (bf16[128,192]{1,0:T(8,128)(2,1)S(1)}, bf16[128,192]{1,0:T(8,128)(2,1)}, u32[]{:S(2)}) copy-start(bf16[128,192]{1,0:T(8,128)(2,1)} %constant.35.clone.grad_left) | copy-start | bytes 147460
  1.4 14.0 %copy-start.4 = (bf16[64,384]{1,0:T(8,128)(2,1)S(1)}, bf16[64,384]{1,0:T(8,128)(2,1)}, u32[]{:S(2)}) copy-start(bf16[64,384]{1,0:T(8,128)(2,1)} %constant.37.clone.square_left) | copy-start | bytes 147460
  1.4 14.0 %copy-start.5 = (bf16[64,384]{1,0:T(8,128)(2,1)S(1)}, bf16[64,384]{1,0:T(8,128)(2,1)}, u32[]{:S(2)}) copy-start(bf16[64,384]{1,0:T(8,128)(2,1)} %constant.36.clone.image_left) | copy-start | bytes 147460
  5.2 30.2 %collective-permute-start.1 = (f32[1024,128]{1,0:T(8,128)S(1)}, f32[1024,128]{1,0:T(8,128)S(1)}, u32[]{:S(2)}, u32[]{:S(2)}) collective-permute-start(f32[1024,128]{1,0:T(8,128)S(1)} %get-tuple-element.47), channel_id=1, source_target_pairs={{0,1},{1,2},{2,3},{3,0},{4,5},{5,6},{6,7},{7,4},{8,9},{9,10},{10,1... | collective-permute-start | bytes 1572872 | tf_op jit(solution)/shard_map/ppermute | solution.py:1008
  10.9 51.5 %collective-permute-start.12 = (f32[1792,128]{1,0:T(8,128)S(1)}, f32[1792,128]{1,0:T(8,128)S(1)}, u32[]{:S(2)}, u32[]{:S(2)}) collective-permute-start(f32[1792,128]{1,0:T(8,128)S(1)} %get-tuple-element.69), channel_id=1, source_target_pairs={{0,4},{4,8},{8,12},{12,16},{16,20},{20,24},{24,28},{28,0},{1,5},{5... | collective-permute-start | bytes 2752520 | tf_op jit(solution)/shard_map/ppermute | solution.py:1008
  11.0 28.2 %collective-permute-start.2 = (f32[1024,128]{1,0:T(8,128)S(1)}, f32[1024,128]{1,0:T(8,128)S(1)}, u32[]{:S(2)}, u32[]{:S(2)}) collective-permute-start(f32[1024,128]{1,0:T(8,128)S(1)} %get-tuple-element.48), channel_id=1, source_target_pairs={{0,3},{1,0},{2,1},{3,2},{4,7},{5,4},{6,5},{7,6},{8,11},{9,8},{10,9... | collective-permute-start | bytes 1572872 | tf_op jit(solution)/shard_map/ppermute | solution.py:1008
  13.1 51.3 %collective-permute-start.13 = (f32[1792,128]{1,0:T(8,128)S(1)}, f32[1792,128]{1,0:T(8,128)S(1)}, u32[]{:S(2)}, u32[]{:S(2)}) collective-permute-start(f32[1792,128]{1,0:T(8,128)S(1)} %get-tuple-element.40.after), channel_id=1, source_target_pairs={{0,28},{4,0},{8,4},{12,8},{16,12},{20,16},{24,20},{28,24},{1,29},{... | collective-permute-start | bytes 2752520 | tf_op jit(solution)/shard_map/ppermute | solution.py:1008
  28.1 28.2 %copy-start.1 = (f32[8,8,8,512]{3,2,1,0:T(8,128)S(1)}, f32[8,8,8,512]{3,2,1,0:T(8,128)}, u32[]{:S(2)}) copy-start(f32[8,8,8,512]{3,2,1,0:T(8,128)} %param.9) | copy-start | bytes 3145732
  28.1 7.3 %collective-permute-start = (f32[176,128]{1,0:T(8,128)S(1)}, f32[176,128]{1,0:T(8,128)S(1)}, u32[]{:S(2)}, u32[]{:S(2)}) collective-permute-start(f32[176,128]{1,0:T(8,128)S(1)} %get-tuple-element.45.rest_0_), channel_id=1, source_target_pairs={{0,1},{1,2},{2,3},{3,0},{4,5},{5,6},{6,7},{7,4},{8,9},{9,10},{10,1... | collective-permute-start | bytes 270344 | tf_op jit(solution)/shard_map/ppermute | solution.py:1008
  35.4 17.4 %collective-permute-start.6 = (f32[768,128]{1,0:T(8,128)S(1)}, f32[768,128]{1,0:T(8,128)S(1)}, u32[]{:S(2)}, u32[]{:S(2)}) collective-permute-start(f32[768,128]{1,0:T(8,128)S(1)} %get-tuple-element.61), channel_id=1, source_target_pairs={{0,1},{1,2},{2,3},{3,0},{4,5},{5,6},{6,7},{7,4},{8,9},{9,10},{10,1... | collective-permute-start | bytes 1179656 | tf_op jit(solution)/shard_map/ppermute | solution.py:1008
  35.4 19.7 %collective-permute-start.7 = (f32[768,128]{1,0:T(8,128)S(1)}, f32[768,128]{1,0:T(8,128)S(1)}, u32[]{:S(2)}, u32[]{:S(2)}) collective-permute-start(f32[768,128]{1,0:T(8,128)S(1)} %get-tuple-element.49.rest_2_), channel_id=1, source_target_pairs={{0,3},{1,0},{2,1},{3,2},{4,7},{5,4},{6,5},{7,6},{8,11},{9,8},{10,9... | collective-permute-start | bytes 1179656 | tf_op jit(solution)/shard_map/ppermute | solution.py:1008
  39.2 4.9 %collective-permute-start.3 = (f32[176,128]{1,0:T(8,128)S(1)}, f32[176,128]{1,0:T(8,128)S(1)}, u32[]{:S(2)}, u32[]{:S(2)}) collective-permute-start(f32[176,128]{1,0:T(8,128)S(1)} %pass_on.2.after), channel_id=1, source_target_pairs={{0,4},{4,8},{8,12},{12,16},{16,20},{20,24},{24,28},{28,0},{1,5},{5... | collective-permute-start | bytes 270344 | tf_op jit(solution)/shard_map/ppermute | solution.py:1008
  44.8 2.2 %collective-permute-start.4 = (f32[176,128]{1,0:T(8,128)S(1)}, f32[176,128]{1,0:T(8,128)S(1)}, u32[]{:S(2)}, u32[]{:S(2)}) collective-permute-start(f32[176,128]{1,0:T(8,128)S(1)} %get-tuple-element.56.rest_0_), channel_id=1, source_target_pairs={{0,28},{4,0},{8,4},{12,8},{16,12},{20,16},{24,20},{28,24},{1,29},{... | collective-permute-start | bytes 270344 | tf_op jit(solution)/shard_map/ppermute | solution.py:1008
  47.0 9.2 %collective-permute-start.5 = (f32[176,128]{1,0:T(8,128)S(1)}, f32[176,128]{1,0:T(8,128)S(1)}, u32[]{:S(2)}, u32[]{:S(2)}) collective-permute-start(f32[176,128]{1,0:T(8,128)S(1)} %pass_on.3), channel_id=1, source_target_pairs={{0,3},{1,0},{2,1},{3,2},{4,7},{5,4},{6,5},{7,6},{8,11},{9,8},{10,9... | collective-permute-start | bytes 270344 | tf_op jit(solution)/shard_map/ppermute | solution.py:1008
  58.5 10.2 %collective-permute-start.8 = (f32[256,128]{1,0:T(8,128)S(1)}, f32[256,128]{1,0:T(8,128)S(1)}, u32[]{:S(2)}, u32[]{:S(2)}) collective-permute-start(f32[256,128]{1,0:T(8,128)S(1)} %get-tuple-element.65), channel_id=1, source_target_pairs={{0,4},{4,8},{8,12},{12,16},{16,20},{20,24},{24,28},{28,0},{1,5},{5... | collective-permute-start | bytes 393224 | tf_op jit(solution)/shard_map/ppermute | solution.py:1008
  58.5 10.2 %collective-permute-start.10 = (f32[256,128]{1,0:T(8,128)S(1)}, f32[256,128]{1,0:T(8,128)S(1)}, u32[]{:S(2)}, u32[]{:S(2)}) collective-permute-start(f32[256,128]{1,0:T(8,128)S(1)} %get-tuple-element.67), channel_id=1, source_target_pairs={{0,1},{1,2},{2,3},{3,0},{4,5},{5,6},{6,7},{7,4},{8,9},{9,10},{10,1... | collective-permute-start | bytes 393224 | tf_op jit(solution)/shard_map/ppermute | solution.py:1008
  60.1 8.9 %collective-permute-start.11 = (f32[256,128]{1,0:T(8,128)S(1)}, f32[256,128]{1,0:T(8,128)S(1)}, u32[]{:S(2)}, u32[]{:S(2)}) collective-permute-start(f32[256,128]{1,0:T(8,128)S(1)} %get-tuple-element.68), channel_id=1, source_target_pairs={{0,3},{1,0},{2,1},{3,2},{4,7},{5,4},{6,5},{7,6},{8,11},{9,8},{10,9... | collective-permute-start | bytes 393224 | tf_op jit(solution)/shard_map/ppermute | solution.py:1008
  62.4 6.6 %collective-permute-start.9 = (f32[256,128]{1,0:T(8,128)S(1)}, f32[256,128]{1,0:T(8,128)S(1)}, u32[]{:S(2)}, u32[]{:S(2)}) collective-permute-start(f32[256,128]{1,0:T(8,128)S(1)} %get-tuple-element.66.rest_6_), channel_id=1, source_target_pairs={{0,28},{4,0},{8,4},{12,8},{16,12},{20,16},{24,20},{28,24},{1,29},{... | collective-permute-start | bytes 393224 | tf_op jit(solution)/shard_map/ppermute | solution.py:1008
